TPU v7x, 256 devices: a whole 4x4x8 slice. The times are simulated.
256 devices in a mesh: rep: 16 (over x, y_lo, core), fsdp: 16 (over z, y_hi).
Axes of the slice: x: 4, y: 4 (y_hi: 2, y_lo: 2; y = y_hi * 2 + y_lo), z: 8, core: 2. Of those that a mesh axis runs over, the one named last changes fastest.
Arguments:
- grad_parts: bfloat16 [16, 16, 1024, 4096], P('rep', 'fsdp')
- momentum: float32 [16, 1024, 4096], P('rep', 'fsdp'), may hold values from -24 to 24
- band: int32 [32], replicated, may hold values from 0 to 4095, as said below
Outputs:
- new_momentum: float32 [16, 1024, 4096], P('rep', 'fsdp')
- step_dir: float32 [1024, 4096], P('fsdp')
Inputs may be any that keep to these rules, and one draw needn't show every extreme that they name: `band`: 32 distinct indices; 0 and 4095 are always among them.
All inputs are finite; a program needn't handle non-finite values.
Results may differ from a plain program's by a relative error of at most 0.0003.
Values sent between devices are 32-bit elements; how exact they have to be, the bound alone decides.
No kernel may reach another device: no remote copies, remote signals or barrier semaphores. Data moves between devices by JAX's collectives and lax.ppermute only.
A program may use at most 128 MiB of HBM per device.

v0:
```python
import jax
import jax.numpy as jnp
from jax import lax
from jax.sharding import PartitionSpec as P

SPAN = 64
BAND = 32


def dct_table(index):
    pos = jnp.arange(SPAN).astype(jnp.float32)
    freq = index.astype(jnp.float32)[:, None]
    table = jnp.cos(jnp.pi * (2.0 * pos[None, :] + 1.0) * freq / (2.0 * SPAN)) * jnp.sqrt(
        2.0 / SPAN
    )
    return jnp.where(index[:, None] == 0, jnp.sqrt(1.0 / SPAN) * jnp.ones_like(table), table)


def make_basis(band):
    first = dct_table(band // SPAN)
    second = dct_table(band % SPAN)
    return (first[:, :, None] * second[:, None, :]).reshape(BAND, SPAN * SPAN)


def project(field, basis):
    row_blocks = field.shape[0] // SPAN
    col_blocks = field.shape[1] // SPAN
    blocks = field.reshape(row_blocks, SPAN, col_blocks, SPAN).transpose(0, 2, 1, 3)
    blocks = blocks.reshape(row_blocks * col_blocks, SPAN * SPAN)
    coeffs = jnp.dot(blocks, basis.T, precision=lax.Precision.HIGHEST)
    return coeffs.reshape(row_blocks, col_blocks, BAND)


def decode(coeffs, basis):
    row_blocks, col_blocks = (coeffs.shape[0], coeffs.shape[1])
    flat = jnp.dot(coeffs.reshape(-1, BAND), basis, precision=lax.Precision.HIGHEST)
    flat = flat.reshape(row_blocks, col_blocks, SPAN, SPAN).transpose(0, 2, 1, 3)
    return flat.reshape(row_blocks * SPAN, col_blocks * SPAN)


def per_device(grad_parts, momentum, band):
    basis = make_basis(band)
    previous = momentum[0]
    grad = lax.psum_scatter(
        grad_parts.astype(jnp.float32), "fsdp", scatter_dimension=2, tiled=True
    )[0, 0]
    mom = 0.9 * previous + grad
    coeffs = project(mom, basis)
    fresh = mom - decode(coeffs, basis)
    replicas = lax.all_gather(coeffs[None], "rep", axis=0, tiled=True)
    average = decode(jnp.mean(replicas, axis=0), basis)
    local_squares = jnp.sum(average * average)
    total_squares = lax.psum(local_squares, "fsdp")
    mean_square = total_squares / (average.size * lax.axis_size("fsdp"))
    step_dir = average * lax.rsqrt(mean_square + 1e-06)
    return (fresh[None], step_dir)


def solution(mesh):
    return jax.shard_map(
        per_device,
        mesh=mesh,
        in_specs=(P("rep", "fsdp", None, None), P("rep", "fsdp", None), P()),
        out_specs=(P("rep", "fsdp", None), P("fsdp", None)),
        check_vma=False,
    )
```

profile of v0, /device:TPU:0, one launch (start us, length us, event | category | flops | bytes accessed | tf_op | source)
XLA Modules:
  0.0 401.8 jit_solution(14321706103433949997)
XLA Ops:
  7.2 0.0 reduce-scatter.2.cloned.1.call-start
  7.2 11.4 %convert_element_type.19 = f32[1,1,1024,4096]{3,2,1,0:T(8,128)} convert(bf16[1,1,1024,4096]{3,2,1,0:T(8,128)(2,1)} %param.3) | non-fusion elementwise | flops 4194304 | bytes 25165824 | tf_op jit(solution)/shard_map/convert_element_type | solution.py:45
  18.6 0.0 copy-start.3
  18.6 0.0 reduce-scatter.2.cloned.1.call-update
  18.6 0.6 copy-done.3
  19.2 0.0 copy-start.2
  19.3 0.2 multiply_select_fusion.1
  19.5 0.3 broadcast_multiply_fusion
  19.8 1.2 mul.147
  21.0 0.0 copy-done.2
  21.0 0.1 broadcast_multiply_fusion.1
  21.1 0.8 mul.134
  21.9 1.5 dot_general.17
  23.4 282.8 %reduce-scatter.2.cloned.1.call-done = f32[1,1,64,4096]{3,2,1,0:T(8,128)} async-done(((f32[1,1,1024,4096]{3,2,1,0:T(8,128)}), f32[1,1,64,4096]{3,2,1,0:T(8,128)}) %reduce-scatter.2.cloned.1.call-update) | async-done | bytes 1048592 | tf_op jit(solution)/shard_map/reduce_scatter | solution.py:44
  306.2 3.1 squeeze.7
  309.3 5.2 %fusion = f32[1,64,64,64]{3,2,1,0:T(8,128)} fusion(f32[1,64,64,64]{3,2,1,0:T(8,128)} %squeeze.7, f32[1,64,64,64]{3,2,1,0:T(8,128)S(1)} %mul.134), kind=kLoop, calls=%fused_computation.1 | loop fusion | flops 262144 | bytes 3145728 | tf_op jit(solution)/shard_map/transpose | solution.py:28
  314.5 0.0 copy-start
  314.5 2.2 reshape.170
  316.7 0.0 copy-done
  316.7 0.9 fusion.11
  317.6 19.5 %all-gather.1 = f32[16,64,32]{1,2,0:T(8,128)S(1)} all-gather(f32[1,64,32]{1,2,0:T(8,128)S(1)} %bitcast.37), channel_id=2, replica_groups=mesh['rep'=16,'fsdp'=16] {'rep'}, dimensions={0}, use_global_device_ids=true | all-gather | bytes 139264 | tf_op jit(solution)/shard_map/all_gather | solution.py:50
  337.2 2.3 convolution_bitcast_fusion
  339.5 4.1 %multiply_reduce_fusion = (f32[]{:T(128)}, f32[64,64,64]{2,0,1:T(8,128)}) fusion(f32[64,64,32]{1,0,2:T(8,128)S(1)} %dot_general.17, f32[64,32]{0,1:T(8,128)S(1)} %reduce.4), kind=kOutput, calls=%fused_computation.3 | convolution fusion | flops 101189632 | bytes 1581060 | tf_op jit(solution)/shard_map/dot_general | solution.py:36
  343.7 40.2 %psum.7 = f32[]{:T(128)} all-reduce(f32[]{:T(128)} %get-tuple-element.7), channel_id=1, replica_groups=mesh['rep'=16,'fsdp'=16] {'fsdp'}, use_global_device_ids=true, to_apply=%region_3.4 | all-reduce | flops 1 | bytes 8 | tf_op jit(solution)/shard_map/psum | solution.py:53
  384.5 3.2 multiply_bitcast_fusion
  387.7 2.9 mul.153
  390.6 0.0 copy-start.1
  390.6 1.6 reshape.171
  392.2 0.0 copy-done.1
  392.2 2.7 fusion.1
  (6 shorter events, 0.1 us)
Async XLA Ops:
  7.2 299.0 %reduce-scatter.2.cloned.1.call-start = ((), (), s32[]{:S(2)}) async-start(), calls=%async_computation.1 | async-start | bytes 17825792 | tf_op jit(solution)/shard_map/reduce_scatter | solution.py:44
  18.6 0.7 copy-start.3
  19.2 1.8 copy-start.2
  314.5 2.2 copy-start
  390.6 1.6 copy-start.1
Sparse Core Ops, SparseCore 0:
  18.7 287.4 reduce-scatter.1
where the time goes:
time: 402 us
  waiting for transfers between devices  283 us (70%)
  blocking collectives  59.7 us (15%)
  other arithmetic  23.1 us (6%)
  between operations  14.8 us (4%)
  local copies, waits for them, and re-layouts  13.9 us (3%)
  matrix products  7.42 us (2%)
    reduce_scatter x1, waiting for transfers between devices, per_device(): lax.psum_scatter(grad_parts.astype(jnp.float32), 'fsdp', scatter_dimensio...  283 us
    psum x1, blocking collectives, per_device(): total_squares = lax.psum(local_squares, 'fsdp')  40.2 us
    all_gather x1, blocking collectives, per_device(): replicas = lax.all_gather(coeffs[None], 'rep', axis=0, tiled=True)  19.5 us
    convert_element_type x1, other arithmetic, per_device(): grad_parts.astype(jnp.float32)  11.4 us
  transfers between devices with their start and end apart: 1, of which 1 were waited for; matrix products, arithmetic and copies ran while one was open for 1% of the time, Pallas kernels for 0%

commit v1 on v0

v1 whole, which is shorter than its diff:
```python
import functools

import jax
import jax.numpy as jnp
import numpy as np
from jax import lax
from jax.experimental import pallas as pl
from jax.experimental.pallas import tpu as pltpu
from jax.sharding import Mesh, PartitionSpec as P

SPAN = 64
BAND = 32
COLS = 4096
ROWS = 1024
NZ = 8
REPS = 16
HIGHEST = lax.Precision.HIGHEST
VMEM_LIMIT = 16 * 1024 * 1024
NO_COST = pl.CostEstimate(flops=0, bytes_accessed=0, transcendentals=0)

CHUNK, Y_COLS = 1536, 1024
Y_AT = 2 * CHUNK


def dct_table(index):
    pos = jnp.arange(SPAN).astype(jnp.float32)
    freq = index.astype(jnp.float32)[:, None]
    table = jnp.cos(jnp.pi * (2.0 * pos[None, :] + 1.0) * freq / (2.0 * SPAN)) * jnp.sqrt(
        2.0 / SPAN
    )
    return jnp.where(index[:, None] == 0, jnp.sqrt(1.0 / SPAN) * jnp.ones_like(table), table)


def thirds(x):
    high = x.astype(jnp.bfloat16)
    rest = x - high.astype(jnp.float32)
    middle = rest.astype(jnp.bfloat16)
    low = (rest - middle.astype(jnp.float32)).astype(jnp.bfloat16)
    return high, middle, low


def dot(a, b):
    return jnp.dot(a, b, preferred_element_type=jnp.float32)


def add_thirds(stacked):
    n = stacked.shape[0] // 3
    return (stacked[2 * n :] + stacked[n : 2 * n]) + stacked[:n]


def along_blocks(x, ones):
    return add_thirds(dot(jnp.concatenate(thirds(x), axis=0), ones))


def partial_coeffs_kernel(where_ref, grad_ref, mom_ref, first_ref, second_ref, ones_ref, out_ref):
    first3 = jnp.concatenate(thirds(first_ref[...]), axis=0)
    total = jnp.zeros((BAND, 128), jnp.float32)
    for half in range(2):
        rows = grad_ref[half * SPAN : (half + 1) * SPAN, :]
        along = add_thirds(dot(first3, rows)) * second_ref[...]
        total += along_blocks(along, ones_ref[half])
    out_ref[0] = total

    @pl.when(pl.program_id(0) == where_ref[0])
    def _():
        along = jnp.dot(
            first_ref[...], mom_ref[...], precision=HIGHEST, preferred_element_type=jnp.float32
        )
        along = (0.9 * along) * second_ref[...]
        out_ref[0] += along_blocks(along, ones_ref[where_ref[1]])


def partial_coeffs(where, grad, mom, first, second, ones):
    fixed = lambda shape: pl.BlockSpec(shape, lambda i, w: (0,) * len(shape))
    return pl.pallas_call(
        partial_coeffs_kernel,
        out_shape=jax.ShapeDtypeStruct((NZ, BAND, 128), jnp.float32),
        grid_spec=pltpu.PrefetchScalarGridSpec(
            num_scalar_prefetch=1,
            grid=(NZ,),
            in_specs=[
                pl.BlockSpec((2 * SPAN, COLS), lambda i, w: (i, 0)),
                fixed((SPAN, COLS)),
                fixed((BAND, SPAN)),
                fixed((BAND, COLS)),
                fixed((2, COLS, 128)),
            ],
            out_specs=pl.BlockSpec((1, BAND, 128), lambda i, w: (i, 0, 0)),
        ),
        compiler_params=pltpu.CompilerParams(vmem_limit_bytes=2 * VMEM_LIMIT),
        cost_estimate=NO_COST,
        name="partial_coeffs",
    )(where, grad, mom, first, second, ones)


def new_momentum(mom_ref, parts, first_ref, second_ref, same_ref):
    grad = parts[0][...]
    for part in parts[1:]:
        grad = grad + part[...]
    if grad.shape[0] == 2 * SPAN:
        grad = jnp.concatenate([grad[:SPAN], grad[SPAN:]], axis=1)
    mom = 0.9 * mom_ref[...] + grad
    first, second = first_ref[...], second_ref[...]
    along = jnp.dot(first, mom, precision=HIGHEST, preferred_element_type=jnp.float32)
    spread = [
        along_blocks(along[:, c : c + 128] * second, same_ref[...]) * second
        for c in range(0, mom.shape[1], 128)
    ]
    own = lax.dot_general(
        first, jnp.concatenate(spread, axis=1), (((0,), (0,)), ((), ())), precision=HIGHEST,
        preferred_element_type=jnp.float32,
    )
    return mom - own


def finish_kernel(mom_ref, *refs):
    *parts, first_ref, second_ref, same_ref, out_ref = refs
    out_ref[...] = new_momentum(mom_ref, parts, first_ref, second_ref, same_ref)


def whole(x):
    return pl.BlockSpec(x.shape, lambda i: (0, 0))


def finish(mom, at, width, parts, first, second, same):
    others = (*parts, first, second, same)
    return pl.pallas_call(
        finish_kernel,
        out_shape=jax.ShapeDtypeStruct((SPAN, width), jnp.float32),
        grid=(1,),
        in_specs=[pl.BlockSpec((SPAN, width), lambda i: (0, at // width)), *map(whole, others)],
        out_specs=pl.BlockSpec((SPAN, width), lambda i: (0, 0)),
        compiler_params=pltpu.CompilerParams(vmem_limit_bytes=VMEM_LIMIT),
        cost_estimate=NO_COST,
        name="finish",
    )(mom, *others)


def last_kernel(n_fronts, *refs):
    squares_ref, more_ref, average_ref = refs[n_fronts : n_fronts + 3]
    mom_ref, *parts, first_ref, second_ref, same_ref, out_ref, dir_ref = refs[n_fronts + 3 :]
    mean_square = jnp.sum(squares_ref[...] + more_ref[...]) / (ROWS * COLS) + 1e-06
    scale = lax.rsqrt(mean_square)
    scale = scale * (1.5 - 0.5 * (mean_square * scale) * scale)
    dir_ref[...] = average_ref[...] * scale
    at = 0
    for ref in refs[:n_fronts]:
        out_ref[:, at : at + ref.shape[1]] = ref[...]
        at += ref.shape[1]
    out_ref[:, at:] = new_momentum(mom_ref, parts, first_ref, second_ref, same_ref)


def last(fronts, squares, more, average, mom, at, width, parts, first, second, same):
    before, others = (*fronts, squares, more, average), (*parts, first, second, same)
    out = jax.ShapeDtypeStruct((SPAN, COLS), jnp.float32)
    return pl.pallas_call(
        functools.partial(last_kernel, len(fronts)),
        out_shape=[out, out],
        grid=(1,),
        in_specs=[
            *map(whole, before),
            pl.BlockSpec((SPAN, width), lambda i: (0, at // width)),
            *map(whole, others),
        ],
        out_specs=[whole(out), whole(out)],
        compiler_params=pltpu.CompilerParams(vmem_limit_bytes=VMEM_LIMIT),
        cost_estimate=NO_COST,
        name="last",
    )(*before, mom, *others)


def decode_kernel(where_ref, coeffs_ref, first_ref, second_ref, spread_ref, out_ref):
    along = along_blocks(coeffs_ref[...], spread_ref[where_ref[1]]) * second_ref[...]
    out_ref[...] = lax.dot_general(
        first_ref[...], along, (((0,), (0,)), ((), ())), precision=HIGHEST,
        preferred_element_type=jnp.float32,
    )


def decode(where, coeffs, first, second, spread):
    vmem = pl.BlockSpec(memory_space=pltpu.VMEM)
    return pl.pallas_call(
        decode_kernel,
        out_shape=jax.ShapeDtypeStruct((SPAN, COLS), jnp.float32),
        in_specs=[pl.BlockSpec(memory_space=pltpu.SMEM)] + [vmem] * 4,
        compiler_params=pltpu.CompilerParams(vmem_limit_bytes=VMEM_LIMIT),
        cost_estimate=NO_COST,
        name="decode",
    )(where, coeffs, first, second, spread)


def flip(x, axis, size, bit):
    return lax.ppermute(x, axis, [(i, i ^ bit) for i in range(size)])


def up(x):
    return lax.ppermute(x, "z", [(i, (i + 1) % NZ) for i in range(NZ)])


def down(x):
    return lax.ppermute(x, "z", [(i, (i - 1) % NZ) for i in range(NZ)])


def after(x, *earlier):
    return lax.optimization_barrier((x, *earlier))[0]


def add_four(terms):
    own, one, two, three = terms
    return (own + one) + (two + three)


def swap(x, axes, flips):
    sizes = [lax.axis_size(axis) for axis in axes]
    places = list(np.ndindex(*sizes))
    index = lambda place: int(np.ravel_multi_index(place, sizes))
    return lax.ppermute(x, axes, [(index(p), index([i ^ f for i, f in zip(p, flips)])) for p in places])


def swap_three(x, axes, one, two):
    return [x] + [swap(x, axes, flips) for flips in ((one, 0), (0, two), (one, two))]


def squares_kernel(coeffs_ref, gram_ref, out_ref):
    total = jnp.zeros((BAND, 128), jnp.float32)
    for i in range(coeffs_ref.shape[0]):
        coeffs = coeffs_ref[i]
        total += coeffs * jnp.dot(
            gram_ref[...], coeffs, precision=HIGHEST, preferred_element_type=jnp.float32
        )
    out_ref[...] = (total[:8] + total[8:16]) + (total[16:24] + total[24:])


def squares_of(coeffs, gram):
    return pl.pallas_call(
        squares_kernel,
        out_shape=jax.ShapeDtypeStruct((8, 128), jnp.float32),
        cost_estimate=NO_COST,
        name="squares",
    )(coeffs, gram)


class Ring:
    def __init__(self, block, width):
        self.block, self.width = block, width
        self.step = 4
        self.first = block(4)
        self.going = None

    def next(self):
        half = self.width // 2
        if self.step == 4:
            terms = self.first[:, :half], self.first[:, half:]
        else:
            upward, downward = self.going
            if self.step == 3:
                zeros = jnp.zeros((upward.shape[0], half), jnp.float32)
                upward = jnp.concatenate([upward, zeros], axis=1)
                downward = jnp.concatenate([zeros, downward], axis=1)
            terms = self.block(self.step) + upward, self.block(-self.step) + downward
        self.step -= 1
        return terms

    def parts(self):
        return [self.block(0), *self.going]


class Flight:
    def __init__(self, *rings):
        self.rings = rings
        terms = [ring.next() for ring in rings]
        self.widths = [up_term.shape[1] for up_term, _ in terms]
        self.sent = [jnp.concatenate(list(side), axis=1) if len(terms) > 1 else side[0] for side in zip(*terms)]
        self.got = [up(self.sent[0]), down(self.sent[1])]

    def land(self, got):
        at = 0
        for ring, width in zip(self.rings, self.widths):
            ring.going = [side[:, at : at + width] for side in got]
            at += width


def meet(*arrays):
    return lax.optimization_barrier(arrays)


def per_device(grad_parts, momentum, band):
    z, yh = lax.axis_index("z"), lax.axis_index("yh")
    where = jnp.stack([z, yh]).astype(jnp.int32)
    grad = grad_parts[0, 0]
    mom = momentum[0]

    first = dct_table(band // SPAN)
    second_table = dct_table(band % SPAN)
    second = jnp.tile(second_table, (1, COLS // SPAN))
    block_of = np.arange(COLS) // SPAN
    ones = np.zeros((2, COLS, 128), np.float32)
    for half in range(2):
        ones[half, np.arange(COLS), half * 64 + block_of] = 1.0
    spread = jnp.asarray(ones.transpose(0, 2, 1), jnp.bfloat16)
    ones = jnp.asarray(ones, jnp.bfloat16)
    same = jnp.asarray(np.kron(np.eye(2), np.ones((SPAN, SPAN))), jnp.bfloat16)

    def owner(k):
        return lax.rem(z + k + NZ, NZ)

    def z_block(at):
        def block(k):
            rows = lax.dynamic_slice(grad, (owner(k) * 2 * SPAN, at), (2 * SPAN, CHUNK))
            return rows.astype(jnp.float32)

        return block

    def y_block(got):
        def block(k):
            rows = lax.dynamic_slice(grad, ((owner(k) * 2 + yh) * SPAN, Y_AT), (SPAN, Y_COLS))
            term = lax.dynamic_index_in_dim(got, owner(k), 0, keepdims=False) + rows.astype(jnp.float32)
            return jnp.concatenate([term[:, : Y_COLS // 2], term[:, Y_COLS // 2 :]], axis=0)

        return block

    def cross_y(total):
        give = lax.dynamic_slice(total, ((1 - yh) * SPAN, 0), (SPAN, CHUNK))
        keep = lax.dynamic_slice(total, (yh * SPAN, 0), (SPAN, CHUNK))
        return keep, give, flip(give, "yh", 2, 1)

    ring_a, ring_b = Ring(z_block(0), CHUNK), Ring(z_block(CHUNK), CHUNK)
    a = Flight(ring_a)
    ring_b.first = meet(ring_b.first, *a.sent)[0]
    b = Flight(ring_b)
    rows = after(grad, *b.sent).reshape(NZ, 2 * SPAN, COLS)
    give = lax.dynamic_slice(rows, (0, (1 - yh) * SPAN, Y_AT), (NZ, SPAN, Y_COLS)).astype(jnp.float32)
    got = flip(give, "yh", 2, 1)

    a.land(meet(*a.got, give)[:2])
    a = Flight(ring_a)

    b.land(meet(*b.got, *a.sent)[:2])
    b = Flight(ring_b)
    coeffs = partial_coeffs(where, grad, after(mom, *b.sent), first, second, ones)
    pair = second[:, :128]
    gram = jnp.dot(first, first.T, precision=HIGHEST) * jnp.dot(second_table, second_table.T, precision=HIGHEST)

    coeffs, pair, *rest = meet(coeffs, pair, *a.got)
    a.land(rest)
    a = Flight(ring_a)

    got, coeffs, *rest = meet(got, coeffs, *b.got, *a.sent)
    b.land(rest[:2])
    ring_y = Ring(y_block(got), Y_COLS // 2)
    b = Flight(ring_b, ring_y)
    coeffs = coeffs + flip(coeffs, "c", 2, 1)
    coeffs = coeffs + flip(coeffs, "x", 4, 1)

    coeffs, *rest = meet(coeffs, *a.got, *b.sent)
    a.land(rest[:2])
    a = Flight(ring_a)
    coeffs = coeffs + flip(coeffs, "x", 4, 2)
    coeffs = coeffs + flip(coeffs, "yl", 2, 1)
    coeffs = coeffs + flip(coeffs, "yh", 2, 1)

    coeffs, *rest = meet(coeffs, *b.got, *a.sent)
    b.land(rest[:2])
    b = Flight(ring_b, ring_y)
    pairs = coeffs.reshape(4, 2, BAND, 128)
    side = z % 2
    keep = lax.dynamic_index_in_dim(pairs, side, 1, keepdims=False)
    other = lax.dynamic_index_in_dim(pairs, 1 - side, 1, keepdims=False)
    more = flip(other, "z", NZ, 1)

    a.land(meet(*a.got, *b.sent, other)[:2])
    keep_a, give_a, got_a = cross_y(sum(ring_a.parts()))

    front_a = finish(mom, 0, CHUNK, [keep_a, got_a], first, pair, same)

    front_a, keep, more, *rest = meet(front_a, keep, more, *b.got)
    b.land(rest)
    y = Flight(ring_y)
    keep_b, give_b, got_b = cross_y(after(sum(ring_b.parts()), *y.sent))
    coeffs = after(keep, give_b) + more
    coeffs = coeffs + flip(coeffs, "z", NZ, 2)

    coeffs, *rest = meet(coeffs, *y.got)
    y.land(rest)
    y = Flight(ring_y)
    coeffs = after(coeffs, *y.sent)
    coeffs = (coeffs + flip(coeffs, "z", NZ, 4)) * (1.0 / REPS)

    squares = squares_of(coeffs, gram)
    more = flip(squares, "z", NZ, 1)
    coeffs = lax.dynamic_index_in_dim(coeffs, z // 2, 0, keepdims=False)
    average = decode(where, after(coeffs, squares), first, second, spread)
    front_b = finish(mom, CHUNK, CHUNK, [keep_b, after(got_b, average)], first, pair, same)

    front_b, average, squares, more, *rest = meet(front_b, average, squares, more, *y.got)
    y.land(rest)
    momentum, step_dir = last(
        [front_a, front_b], squares, more, average, mom, Y_AT, Y_COLS, ring_y.parts(), first, pair, same
    )
    return (momentum[None], step_dir)


def solution(mesh):
    fine = Mesh(mesh.devices.reshape(4, 2, 2, NZ, 2), ("x", "yl", "c", "z", "yh"))
    rep, fsdp = ("x", "yl", "c"), ("z", "yh")
    return jax.shard_map(
        per_device,
        mesh=fine,
        in_specs=(P(rep, fsdp, None, None), P(rep, fsdp, None), P()),
        out_specs=(P(rep, fsdp, None), P(fsdp, None)),
        check_vma=False,
    )
```

time: 402 us -> 170 us (0.42)
  waiting for transfers between devices: 283 us -> 58.2 us
  starting transfers between devices: 0.04 us -> 62.4 us
  blocking collectives: 59.7 us -> 0 us
  Pallas kernels: 0 us -> 17.2 us
  between operations: 14.8 us -> 1.39 us
  matrix products: 7.42 us -> 1.23 us
  other arithmetic: 23.1 us -> 18 us
  local copies, waits for them, and re-layouts: 13.9 us -> 9.57 us
    reduce_scatter x1 -> x0, waiting for transfers between devices: 283 us -> none  [per_device(): lax.psum_scatter(grad_parts.astype(jnp.float32), 'fsdp', scatter_dimensio...]
    ppermute x0 -> x32, starting transfers between devices: none -> 62.4 us  [the longest x12 29.2 us: flip(): return lax.ppermute(x, axis, [(i, i ^ bit) for i in range(size)])]
    ppermute x0 -> x32, waiting for transfers between devices: none -> 58.2 us  [the longest x10 30.3 us: up(): return lax.ppermute(x, 'z', [(i, (i + 1) % NZ) for i in range(NZ)])]
    psum x1 -> x0, blocking collectives: 40.2 us -> none  [per_device(): total_squares = lax.psum(local_squares, 'fsdp')]
    all_gather x1 -> x0, blocking collectives: 19.5 us -> none  [per_device(): replicas = lax.all_gather(coeffs[None], 'rep', axis=0, tiled=True)]
    pallas_call x0 -> x6, Pallas kernels: none -> 17.2 us  [the longest x1 9.25 us: partial_coeffs(): pl.pallas_call(partial_coeffs_kernel, out_shape=jax.ShapeDtypeStruct((NZ,...]
    add x0 -> x22, other arithmetic: none -> 12.6 us  [the longest x12 10.4 us: next(): terms = (self.block(self.step) + upward, self.block(-self.step) + downward)]
    convert_element_type x1 -> x2, other arithmetic: 11.4 us -> 4.13 us  [the longest x1 2.83 us: per_device(): lax.dynamic_slice(rows, (0, (1 - yh) * SPAN, Y_AT), (NZ, SPAN, Y_COLS))]
  transfers between devices with their start and end apart: 1 -> 32, of which waited for: 1 -> 16; matrix products, arithmetic and copies ran while one was open for 1% -> 12% of each run, Pallas kernels for 0% -> 8%
where the time goes in v1:
time: 170 us; the launch traced here: 168 us
  starting transfers between devices  62.4 us (37%)
  waiting for transfers between devices  58.2 us (34%)
  other arithmetic  18 us (11%)
  Pallas kernels  17.2 us (10%)
  local copies, waits for them, and re-layouts  9.57 us (6%)
    ppermute x10, waiting for transfers between devices, up(): return lax.ppermute(x, 'z', [(i, (i + 1) % NZ) for i in range(NZ)])  30.3 us
    ppermute x12, starting transfers between devices, flip(): return lax.ppermute(x, axis, [(i, i ^ bit) for i in range(size)])  29.2 us
    ppermute x10, starting transfers between devices, down(): return lax.ppermute(x, 'z', [(i, (i - 1) % NZ) for i in range(NZ)])  28.6 us
    ppermute x12, waiting for transfers between devices, flip(): return lax.ppermute(x, axis, [(i, i ^ bit) for i in range(size)])  27.5 us
    add x12, other arithmetic, next(): terms = (self.block(self.step) + upward, self.block(-self.step) + downward)  10.4 us
    pallas_call x1, Pallas kernels, partial_coeffs(): pl.pallas_call(partial_coeffs_kernel, out_shape=jax.ShapeDtypeStruct((NZ,...  9.25 us
    unnamed x14, local copies, waits for them, and re-layouts  7.26 us
    ppermute x10, starting transfers between devices, up(): return lax.ppermute(x, 'z', [(i, (i + 1) % NZ) for i in range(NZ)])  4.58 us
  transfers between devices with their start and end apart: 32, of which 16 were waited for; matrix products, arithmetic and copies ran while one was open for 12% of the time, Pallas kernels for 8%

profile of v1, /device:TPU:0, one launch (start us, length us, event | category | flops | bytes accessed | tf_op | source)
XLA Modules:
  0.0 168.0 jit_solution(9935605147376491850)
XLA Ops:
  0.7 1.3 bitcast_convert_fusion.1
  2.3 4.0 %collective-permute-start.4 = (f32[128,768]{1,0:T(8,128)S(1)}, f32[128,768]{1,0:T(8,128)}, u32[]{:S(2)}, u32[]{:S(2)}) collective-permute-start(f32[128,768]{1,0:T(8,128)S(1)} %get-tuple-element.122), channel_id=1, source_target_pairs={{0,14},{2,0},{4,2},{6,4},{8,6},{10,8},{12,10},{14,12},{1,15},{3,1}... | collective-permute-start | bytes 1179656 | tf_op jit(solution)/shard_map/ppermute | solution.py:201
  6.5 3.2 %collective-permute-start.2 = (f32[128,768]{1,0:T(8,128)S(1)}, f32[128,768]{1,0:T(8,128)S(1)}, u32[]{:S(2)}, u32[]{:S(2)}) collective-permute-start(f32[128,768]{1,0:T(8,128)S(1)} %get-tuple-element.120), channel_id=1, source_target_pairs={{0,14},{2,0},{4,2},{6,4},{8,6},{10,8},{12,10},{14,12},{1,15},{3,1}... | collective-permute-start | bytes 1179656 | tf_op jit(solution)/shard_map/ppermute | solution.py:201
  9.7 2.8 %dynamic-slice_convert_fusion = f32[8,64,1024]{2,1,0:T(8,128)} fusion(bf16[8,128,4096]{2,1,0:T(8,128)(2,1)} %bitcast.105, s32[]{:T(128)S(6)} %select_n.137), kind=kLoop, calls=%fused_computation.3 | loop fusion | flops 524288 | bytes 3145732 | tf_op jit(solution)/shard_map/convert_element_type | solution.py:332
  12.5 3.2 %collective-permute-start = (f32[8,64,1024]{2,1,0:T(8,128)}, f32[8,64,1024]{2,1,0:T(8,128)}, u32[]{:S(2)}, u32[]{:S(2)}) collective-permute-start(f32[8,64,1024]{2,1,0:T(8,128)} %dynamic-slice_convert_fusion), channel_id=1, source_target_pairs={{0,1},{1,0},{2,3},{3,2},{4,5},{5,4},{6,7},{7,6},{8,9},{9,8},{10,11... | collective-permute-start | bytes 6291464 | tf_op jit(solution)/shard_map/ppermute | solution.py:193
  15.9 0.4 collective-permute-done.3
  16.3 2.7 %convert_add_fusion.9 = (f32[128,1536]{1,0:T(8,128)}, f32[128,1536]{1,0:T(8,128)}) fusion(f32[128,768]{1,0:T(8,128)} %collective-permute-done.4, bf16[1,1,1024,4096]{3,2,1,0:T(8,128)(2,1)} %param.6, s32[]{:T(128)S(6)} %select_n.139, f32[128,768]{1,0:T(8,128)} %collective-permute-done.3, s32[]{:T(128)S(6)} %select_n.138), kind=kLoop, calls=%fused_computation.18 | loop fusion | flops 786432 | bytes 3145736 | tf_op jit(solution)/shard_map/add | solution.py:260
  19.0 3.3 %collective-permute-start.6 = (f32[128,1536]{1,0:T(8,128)}, f32[128,1536]{1,0:T(8,128)}, u32[]{:S(2)}, u32[]{:S(2)}) collective-permute-start(f32[128,1536]{1,0:T(8,128)} %get-tuple-element.112), channel_id=1, source_target_pairs={{0,14},{2,0},{4,2},{6,4},{8,6},{10,8},{12,10},{14,12},{1,15},{3,1}... | collective-permute-start | bytes 2359304 | tf_op jit(solution)/shard_map/ppermute | solution.py:201
  22.3 2.3 %collective-permute-done.1 = f32[128,768]{1,0:T(8,128)S(1)} collective-permute-done((f32[128,768]{1,0:T(8,128)S(1)}, f32[128,768]{1,0:T(8,128)S(1)}, u32[]{:S(2)}, u32[]{:S(2)}) %collective-permute-start.1) | collective-permute-done | bytes 393248 | tf_op jit(solution)/shard_map/ppermute | solution.py:197
  24.6 2.6 %convert_add_fusion.8 = (f32[128,1536]{1,0:T(8,128)}, f32[128,1536]{1,0:T(8,128)}) fusion(f32[128,768]{1,0:T(8,128)S(1)} %collective-permute-done.2, bf16[1,1,1024,4096]{3,2,1,0:T(8,128)(2,1)} %param.6, s32[]{:T(128)S(6)} %select_n.139, f32[128,768]{1,0:T(8,128)S(1)} %collective-permute-done.1, s32[]{:T(128)S(6)} %select_n.138), kind=kLoop, calls=%fused_computation.17 | loop fusion | flops 786432 | bytes 3145736 | tf_op jit(solution)/shard_map/add | solution.py:260
  27.2 3.4 %collective-permute-start.8 = (f32[128,1536]{1,0:T(8,128)}, f32[128,1536]{1,0:T(8,128)}, u32[]{:S(2)}, u32[]{:S(2)}) collective-permute-start(f32[128,1536]{1,0:T(8,128)} %get-tuple-element.110), channel_id=1, source_target_pairs={{0,14},{2,0},{4,2},{6,4},{8,6},{10,8},{12,10},{14,12},{1,15},{3,1}... | collective-permute-start | bytes 2359304 | tf_op jit(solution)/shard_map/ppermute | solution.py:201
  30.8 0.4 tile.10.second_ref
  31.4 3.4 %copy-done = bf16[1,1,1024,4096]{3,2,1,0:T(8,128)(2,1)S(1)} copy-done((bf16[1,1,1024,4096]{3,2,1,0:T(8,128)(2,1)S(1)}, bf16[1,1,1024,4096]{3,2,1,0:T(8,128)(2,1)}, u32[]{:S(2)}) %copy-start) | copy-done | bytes 8388632
  34.8 1.6 copy-done.3
  36.4 9.3 %partial_coeffs.1 = f32[8,32,128]{2,1,0:T(8,128)S(1)} custom-call(s32[2]{0:T(128)S(1)} %pad_add_fusion.where_ref, bf16[1024,4096]{1,0:T(8,128)(2,1)S(1)} %bitcast.106, f32[64,4096]{1,0:T(8,128)S(1)} %bitcast.107, f32[32,64]{1,0:T(8,128)S(1)} %get-tuple-element.143.first_ref.refs_2_.refs_9_, f32[32,4096]{1,0:T(8,128)S(1)} %tile.10.second_ref, ...), custom_call_target="tpu_custom_call" | custom-call | tf_op jit(solution)/shard_map/partial_coeffs/pallas_call | solution.py:75
  45.6 1.6 convert_add_fusion.6
  47.3 3.2 %collective-permute-start.12 = (f32[128,1536]{1,0:T(8,128)S(1)}, f32[128,1536]{1,0:T(8,128)S(1)}, u32[]{:S(2)}, u32[]{:S(2)}) collective-permute-start(f32[128,1536]{1,0:T(8,128)S(1)} %get-tuple-element.108), channel_id=1, source_target_pairs={{0,14},{2,0},{4,2},{6,4},{8,6},{10,8},{12,10},{14,12},{1,15},{3,1}... | collective-permute-start | bytes 2359304 | tf_op jit(solution)/shard_map/ppermute | solution.py:201
  50.5 7.9 %collective-permute-done.7 = f32[128,1536]{1,0:T(8,128)} collective-permute-done((f32[128,1536]{1,0:T(8,128)}, f32[128,1536]{1,0:T(8,128)}, u32[]{:S(2)}, u32[]{:S(2)}) %collective-permute-start.7) | collective-permute-done | bytes 786464 | tf_op jit(solution)/shard_map/ppermute | solution.py:197
  58.4 2.5 %collective-permute-done = f32[8,64,1024]{2,1,0:T(8,128)} collective-permute-done((f32[8,64,1024]{2,1,0:T(8,128)}, f32[8,64,1024]{2,1,0:T(8,128)}, u32[]{:S(2)}, u32[]{:S(2)}) %collective-permute-start) | collective-permute-done | bytes 2097184 | tf_op jit(solution)/shard_map/ppermute | solution.py:193
  60.9 1.6 convert_add_fusion.4
  62.4 1.9 %convert_add_fusion.14 = (f32[64,1024]{1,0:T(8,128)S(1)}, f32[64,1024]{1,0:T(8,128)S(1)}, f32[64,1024]{1,0:T(8,128)S(1)}, f32[64,1024]{1,0:T(8,128)S(1)}, f32[64...) fusion(f32[8,64,1024]{2,1,0:T(8,128)} %collective-permute-done, ...), kind=kLoop, calls=%fused_computation.35 | loop fusion | flops 1048576 | bytes 5242944 | tf_op jit(solution)/shard_map/add | solution.py:317
  64.4 1.0 collective-permute-start.19
  65.5 1.6 collective-permute-start.10
  67.1 1.2 collective-permute-start.18
  68.3 2.9 %collective-permute-done.10 = f32[8,32,128]{2,1,0:T(8,128)S(1)} collective-permute-done((f32[8,32,128]{2,1,0:T(8,128)S(1)}, f32[8,32,128]{2,1,0:T(8,128)S(1)}, u32[]{:S(2)}, u32[]{:S(2)}) %collective-permute-start.10) | collective-permute-done | bytes 131104 | tf_op jit(solution)/shard_map/ppermute | solution.py:193
  71.2 3.9 %collective-permute-done.11 = f32[128,1536]{1,0:T(8,128)S(1)} collective-permute-done((f32[128,1536]{1,0:T(8,128)S(1)}, f32[128,1536]{1,0:T(8,128)S(1)}, u32[]{:S(2)}, u32[]{:S(2)}) %collective-permute-start.11) | collective-permute-done | bytes 786464 | tf_op jit(solution)/shard_map/ppermute | solution.py:197
  75.2 3.0 %collective-permute-start.15 = (f32[8,32,128]{2,1,0:T(8,128)S(1)}, f32[8,32,128]{2,1,0:T(8,128)S(1)}, u32[]{:S(2)}, u32[]{:S(2)}) collective-permute-start(f32[8,32,128]{2,1,0:T(8,128)S(1)} %add.389), channel_id=1, source_target_pairs={{0,128},{64,192},{128,0},{192,64},{1,129},{65,193},{129,1},{193,65... | collective-permute-start | bytes 393224 | tf_op jit(solution)/shard_map/ppermute | solution.py:193
  78.2 0.3 fusion.4
  78.5 3.1 %collective-permute-done.15 = f32[8,32,128]{2,1,0:T(8,128)S(1)} collective-permute-done((f32[8,32,128]{2,1,0:T(8,128)S(1)}, f32[8,32,128]{2,1,0:T(8,128)S(1)}, u32[]{:S(2)}, u32[]{:S(2)}) %collective-permute-start.15) | collective-permute-done | bytes 131104 | tf_op jit(solution)/shard_map/ppermute | solution.py:193
  81.7 1.7 collective-permute-start.16
  83.4 3.4 %collective-permute-done.16 = f32[8,32,128]{2,1,0:T(8,128)S(1)} collective-permute-done((f32[8,32,128]{2,1,0:T(8,128)S(1)}, f32[8,32,128]{2,1,0:T(8,128)S(1)}, u32[]{:S(2)}, u32[]{:S(2)}) %collective-permute-start.16) | collective-permute-done | bytes 131104 | tf_op jit(solution)/shard_map/ppermute | solution.py:193
  86.7 3.6 %collective-permute-start.17 = (f32[8,32,128]{2,1,0:T(8,128)S(1)}, f32[8,32,128]{2,1,0:T(8,128)S(1)}, u32[]{:S(2)}, u32[]{:S(2)}) collective-permute-start(f32[8,32,128]{2,1,0:T(8,128)S(1)} %add.401), channel_id=1, source_target_pairs={{0,1},{1,0},{2,3},{3,2},{4,5},{5,4},{6,7},{7,6},{8,9},{9,8},{10,11... | collective-permute-start | bytes 393224 | tf_op jit(solution)/shard_map/ppermute | solution.py:193
  90.6 2.2 %collective-permute-start.13 = (f32[128,1536]{1,0:T(8,128)S(1)}, f32[128,1536]{1,0:T(8,128)S(1)}, u32[]{:S(2)}, u32[]{:S(2)}) collective-permute-start(f32[128,1536]{1,0:T(8,128)S(1)} %get-tuple-element.105), channel_id=1, source_target_pairs={{0,2},{2,4},{4,6},{6,8},{8,10},{10,12},{12,14},{14,0},{1,3},{3,5},... | collective-permute-start | bytes 2359304 | tf_op jit(solution)/shard_map/ppermute | solution.py:197
  92.8 2.0 %collective-permute-start.14 = (f32[128,1536]{1,0:T(8,128)S(1)}, f32[128,1536]{1,0:T(8,128)S(1)}, u32[]{:S(2)}, u32[]{:S(2)}) collective-permute-start(f32[128,1536]{1,0:T(8,128)S(1)} %get-tuple-element.104), channel_id=1, source_target_pairs={{0,14},{2,0},{4,2},{6,4},{8,6},{10,8},{12,10},{14,12},{1,15},{3,1}... | collective-permute-start | bytes 2359304 | tf_op jit(solution)/shard_map/ppermute | solution.py:201
  95.2 3.4 %collective-permute-start.23 = (f32[128,2048]{1,0:T(8,128)S(1)}, f32[128,2048]{1,0:T(8,128)S(1)}, u32[]{:S(2)}, u32[]{:S(2)}) collective-permute-start(f32[128,2048]{1,0:T(8,128)S(1)} %pad_maximum_fusion.1), channel_id=1, source_target_pairs={{0,14},{2,0},{4,2},{6,4},{8,6},{10,8},{12,10},{14,12},{1,15},{3,1}... | collective-permute-start | bytes 3145736 | tf_op jit(solution)/shard_map/ppermute | solution.py:201
  98.8 14.3 %collective-permute-done.13 = f32[128,1536]{1,0:T(8,128)S(1)} collective-permute-done((f32[128,1536]{1,0:T(8,128)S(1)}, f32[128,1536]{1,0:T(8,128)S(1)}, u32[]{:S(2)}, u32[]{:S(2)}) %collective-permute-start.13) | collective-permute-done | bytes 786464 | tf_op jit(solution)/shard_map/ppermute | solution.py:197
  113.5 1.7 collective-permute-start.20
  115.2 0.9 convolution_multiply_fusion.gram_ref
  116.1 2.5 %collective-permute-start.21 = (f32[4,32,128]{2,1,0:T(8,128)S(1)}, f32[4,32,128]{2,1,0:T(8,128)S(1)}, u32[]{:S(2)}, u32[]{:S(2)}) collective-permute-start(f32[4,32,128]{2,1,0:T(8,128)S(1)} %get-tuple-element.141), channel_id=1, source_target_pairs={{0,2},{2,0},{4,6},{6,4},{8,10},{10,8},{12,14},{14,12},{1,3},{3,1},... | collective-permute-start | bytes 196616 | tf_op jit(solution)/shard_map/ppermute | solution.py:193
  118.6 4.3 %collective-permute-done.20.refs_1_ = f32[64,1536]{1,0:T(8,128)S(1)} collective-permute-done((f32[64,1536]{1,0:T(8,128)S(1)}, f32[64,1536]{1,0:T(8,128)S(1)}, u32[]{:S(2)}, u32[]{:S(2)}) %collective-permute-start.20) | collective-permute-done | bytes 393248 | tf_op jit(solution)/shard_map/ppermute | solution.py:193
  122.9 0.8 finish.2.refs_0_
  123.7 8.7 %collective-permute-done.21 = f32[4,32,128]{2,1,0:T(8,128)S(1)} collective-permute-done((f32[4,32,128]{2,1,0:T(8,128)S(1)}, f32[4,32,128]{2,1,0:T(8,128)S(1)}, u32[]{:S(2)}, u32[]{:S(2)}) %collective-permute-start.21) | collective-permute-done | bytes 65568 | tf_op jit(solution)/shard_map/ppermute | solution.py:193
  132.7 0.7 collective-permute-done.22
  133.5 3.2 %collective-permute-start.27 = (f32[128,512]{1,0:T(8,128)S(1)}, f32[128,512]{1,0:T(8,128)S(1)}, u32[]{:S(2)}, u32[]{:S(2)}) collective-permute-start(f32[128,512]{1,0:T(8,128)S(1)} %maximum_add_fusion.3), channel_id=1, source_target_pairs={{0,14},{2,0},{4,2},{6,4},{8,6},{10,8},{12,10},{14,12},{1,15},{3,1}... | collective-permute-start | bytes 786440 | tf_op jit(solution)/shard_map/ppermute | solution.py:201
  136.8 0.3 collective-permute-start.26
  137.1 0.8 constant_dynamic-slice_fusion
  137.9 2.7 %collective-permute-start.25 = (f32[4,32,128]{2,1,0:T(8,128)S(1)}, f32[4,32,128]{2,1,0:T(8,128)S(1)}, u32[]{:S(2)}, u32[]{:S(2)}) collective-permute-start(f32[4,32,128]{2,1,0:T(8,128)S(1)} %add.433), channel_id=1, source_target_pairs={{0,4},{2,6},{4,0},{6,2},{8,12},{10,14},{12,8},{14,10},{1,5},{3,7},... | collective-permute-start | bytes 196616 | tf_op jit(solution)/shard_map/ppermute | solution.py:193
  140.7 3.1 %collective-permute-start.24 = (f32[64,1536]{1,0:T(8,128)}, f32[64,1536]{1,0:T(8,128)S(1)}, u32[]{:S(2)}, u32[]{:S(2)}) collective-permute-start(f32[64,1536]{1,0:T(8,128)} %get-tuple-element.116), channel_id=1, source_target_pairs={{0,1},{1,0},{2,3},{3,2},{4,5},{5,4},{6,7},{7,6},{8,9},{9,8},{10,11... | collective-permute-start | bytes 1179656 | tf_op jit(solution)/shard_map/ppermute | solution.py:193
  143.8 0.9 collective-permute-done.26
  144.6 0.7 maximum_add_fusion.5
  145.4 0.7 maximum_add_fusion.4
  146.1 4.1 %collective-permute-start.28 = (f32[4,32,128]{2,1,0:T(8,128)S(1)}, f32[4,32,128]{2,1,0:T(8,128)S(1)}, u32[]{:S(2)}, u32[]{:S(2)}) collective-permute-start(f32[4,32,128]{2,1,0:T(8,128)S(1)} %add.434), channel_id=1, source_target_pairs={{0,8},{2,10},{4,12},{6,14},{8,0},{10,2},{12,4},{14,6},{1,9},{3,11}... | collective-permute-start | bytes 196616 | tf_op jit(solution)/shard_map/ppermute | solution.py:193
  150.2 1.8 %collective-permute-start.31 = (f32[128,512]{1,0:T(8,128)}, f32[128,512]{1,0:T(8,128)S(1)}, u32[]{:S(2)}, u32[]{:S(2)}) collective-permute-start(f32[128,512]{1,0:T(8,128)} %maximum_add_fusion.5), channel_id=1, source_target_pairs={{0,14},{2,0},{4,2},{6,4},{8,6},{10,8},{12,10},{14,12},{1,15},{3,1}... | collective-permute-start | bytes 786440 | tf_op jit(solution)/shard_map/ppermute | solution.py:201
  152.1 0.3 collective-permute-start.30
  152.3 2.7 %collective-permute-done.28 = f32[4,32,128]{2,1,0:T(8,128)S(1)} collective-permute-done((f32[4,32,128]{2,1,0:T(8,128)S(1)}, f32[4,32,128]{2,1,0:T(8,128)S(1)}, u32[]{:S(2)}, u32[]{:S(2)}) %collective-permute-start.28) | collective-permute-done | bytes 65568 | tf_op jit(solution)/shard_map/ppermute | solution.py:193
  155.0 0.6 add_multiply_fusion.coeffs_ref
  155.7 1.7 squares.1.refs_2_
  157.3 2.1 %collective-permute-start.29 = (f32[8,128]{1,0:T(8,128)}, f32[8,128]{1,0:T(8,128)S(1)}, u32[]{:S(2)}, u32[]{:S(2)}) collective-permute-start(f32[8,128]{1,0:T(8,128)} %squares.1.refs_2_), channel_id=1, source_target_pairs={{0,2},{2,0},{4,6},{6,4},{8,10},{10,8},{12,14},{14,12},{1,3},{3,1},... | collective-permute-start | bytes 12296 | tf_op jit(solution)/shard_map/ppermute | solution.py:193
  159.4 0.7 dynamic-slice_bitcast_fusion.2.coeffs_ref
  160.1 1.6 copy-done.2
  161.7 1.7 %decode.1.refs_4_ = f32[64,4096]{1,0:T(8,128)S(1)} custom-call(s32[2]{0:T(128)S(1)} %pad_add_fusion.where_ref, f32[32,128]{1,0:T(8,128)S(1)} %dynamic-slice_bitcast_fusion.2.coeffs_ref, f32[32,64]{1,0:T(8,128)S(1)} %get-tuple-element.143.first_ref.refs_2_.refs_9_, f32[32,4096]{1,0:T(8,128)S(1)} %tile.10.second_ref, bf16[2,128,4096]{2,1,0:T(8,128)(2,1)S(1)} %copy-done.2), custom_call_target="tpu_custom_call" | custom-call | tf_op jit(solution)/shard_map/decode/pallas_call | solution.py:182
  163.5 0.8 finish.3.refs_1_
  164.3 0.7 copy-done.5
  165.0 3.0 %last.1 = (f32[64,4096]{1,0:T(8,128)}, f32[64,4096]{1,0:T(8,128)}) custom-call(f32[64,1536]{1,0:T(8,128)S(1)} %finish.2.refs_0_, f32[64,1536]{1,0:T(8,128)S(1)} %finish.3.refs_1_, f32[8,128]{1,0:T(8,128)S(1)} %copy-done.5, f32[8,128]{1,0:T(8,128)S(1)} %collective-permute-done.29.refs_3_, f32[64,4096]{1,0:T(8,128)S(1)} %decode.1.refs_4_, ...), custom_call_target="tpu_custom_call" | custom-call | tf_op jit(solution)/shard_map/last/pallas_call | solution.py:156
  (75 shorter events, 2.9 us)
Async XLA Ops:
  0.6 15.1 %copy-start.6 = (s32[32]{0:T(128)S(1)}, s32[32]{0:T(128)}, u32[]{:S(2)}) copy-start(s32[32]{0:T(128)} %param.8) | copy-start | bytes 388
  2.0 29.4 %copy-start.1 = (f32[1,64,4096]{2,1,0:T(8,128)S(1)}, f32[1,64,4096]{2,1,0:T(8,128)}, u32[]{:S(2)}) copy-start(f32[1,64,4096]{2,1,0:T(8,128)} %param.7) | copy-start | bytes 3145732
  2.0 14.2 %collective-permute-start.3 = (f32[128,768]{1,0:T(8,128)S(1)}, f32[128,768]{1,0:T(8,128)}, u32[]{:S(2)}, u32[]{:S(2)}) collective-permute-start(f32[128,768]{1,0:T(8,128)S(1)} %get-tuple-element.123), channel_id=1, source_target_pairs={{0,2},{2,4},{4,6},{6,8},{8,10},{10,12},{12,14},{14,0},{1,3},{3,5},... | collective-permute-start | bytes 1179656 | tf_op jit(solution)/shard_map/ppermute | solution.py:197
  2.3 14.0 %collective-permute-start.4 = (f32[128,768]{1,0:T(8,128)S(1)}, f32[128,768]{1,0:T(8,128)}, u32[]{:S(2)}, u32[]{:S(2)}) collective-permute-start(f32[128,768]{1,0:T(8,128)S(1)} %get-tuple-element.122), channel_id=1, source_target_pairs={{0,14},{2,0},{4,2},{6,4},{8,6},{10,8},{12,10},{14,12},{1,15},{3,1}... | collective-permute-start | bytes 1179656 | tf_op jit(solution)/shard_map/ppermute | solution.py:201
  6.4 18.2 %collective-permute-start.1 = (f32[128,768]{1,0:T(8,128)S(1)}, f32[128,768]{1,0:T(8,128)S(1)}, u32[]{:S(2)}, u32[]{:S(2)}) collective-permute-start(f32[128,768]{1,0:T(8,128)S(1)} %get-tuple-element.121), channel_id=1, source_target_pairs={{0,2},{2,4},{4,6},{6,8},{8,10},{10,12},{12,14},{14,0},{1,3},{3,5},... | collective-permute-start | bytes 1179656 | tf_op jit(solution)/shard_map/ppermute | solution.py:197
  6.5 18.1 %collective-permute-start.2 = (f32[128,768]{1,0:T(8,128)S(1)}, f32[128,768]{1,0:T(8,128)S(1)}, u32[]{:S(2)}, u32[]{:S(2)}) collective-permute-start(f32[128,768]{1,0:T(8,128)S(1)} %get-tuple-element.120), channel_id=1, source_target_pairs={{0,14},{2,0},{4,2},{6,4},{8,6},{10,8},{12,10},{14,12},{1,15},{3,1}... | collective-permute-start | bytes 1179656 | tf_op jit(solution)/shard_map/ppermute | solution.py:201
  12.5 48.3 %collective-permute-start = (f32[8,64,1024]{2,1,0:T(8,128)}, f32[8,64,1024]{2,1,0:T(8,128)}, u32[]{:S(2)}, u32[]{:S(2)}) collective-permute-start(f32[8,64,1024]{2,1,0:T(8,128)} %dynamic-slice_convert_fusion), channel_id=1, source_target_pairs={{0,1},{1,0},{2,3},{3,2},{4,5},{5,4},{6,7},{7,6},{8,9},{9,8},{10,11... | collective-permute-start | bytes 6291464 | tf_op jit(solution)/shard_map/ppermute | solution.py:193
  19.0 26.7 %collective-permute-start.5 = (f32[128,1536]{1,0:T(8,128)}, f32[128,1536]{1,0:T(8,128)}, u32[]{:S(2)}, u32[]{:S(2)}) collective-permute-start(f32[128,1536]{1,0:T(8,128)} %get-tuple-element.113), channel_id=1, source_target_pairs={{0,2},{2,4},{4,6},{6,8},{8,10},{10,12},{12,14},{14,0},{1,3},{3,5},... | collective-permute-start | bytes 2359304 | tf_op jit(solution)/shard_map/ppermute | solution.py:197
  19.0 26.6 %collective-permute-start.6 = (f32[128,1536]{1,0:T(8,128)}, f32[128,1536]{1,0:T(8,128)}, u32[]{:S(2)}, u32[]{:S(2)}) collective-permute-start(f32[128,1536]{1,0:T(8,128)} %get-tuple-element.112), channel_id=1, source_target_pairs={{0,14},{2,0},{4,2},{6,4},{8,6},{10,8},{12,10},{14,12},{1,15},{3,1}... | collective-permute-start | bytes 2359304 | tf_op jit(solution)/shard_map/ppermute | solution.py:201
  27.2 31.3 %collective-permute-start.7 = (f32[128,1536]{1,0:T(8,128)}, f32[128,1536]{1,0:T(8,128)}, u32[]{:S(2)}, u32[]{:S(2)}) collective-permute-start(f32[128,1536]{1,0:T(8,128)} %get-tuple-element.111), channel_id=1, source_target_pairs={{0,2},{2,4},{4,6},{6,8},{8,10},{10,12},{12,14},{14,0},{1,3},{3,5},... | collective-permute-start | bytes 2359304 | tf_op jit(solution)/shard_map/ppermute | solution.py:197
  27.2 31.3 %collective-permute-start.8 = (f32[128,1536]{1,0:T(8,128)}, f32[128,1536]{1,0:T(8,128)}, u32[]{:S(2)}, u32[]{:S(2)}) collective-permute-start(f32[128,1536]{1,0:T(8,128)} %get-tuple-element.110), channel_id=1, source_target_pairs={{0,14},{2,0},{4,2},{6,4},{8,6},{10,8},{12,10},{14,12},{1,15},{3,1}... | collective-permute-start | bytes 2359304 | tf_op jit(solution)/shard_map/ppermute | solution.py:201
  31.4 3.4 %copy-start = (bf16[1,1,1024,4096]{3,2,1,0:T(8,128)(2,1)S(1)}, bf16[1,1,1024,4096]{3,2,1,0:T(8,128)(2,1)}, u32[]{:S(2)}) copy-start(bf16[1,1,1024,4096]{3,2,1,0:T(8,128)(2,1)} %param.6) | copy-start | bytes 25165828
  34.8 1.6 copy-start.3
  47.2 27.9 %collective-permute-start.11 = (f32[128,1536]{1,0:T(8,128)S(1)}, f32[128,1536]{1,0:T(8,128)S(1)}, u32[]{:S(2)}, u32[]{:S(2)}) collective-permute-start(f32[128,1536]{1,0:T(8,128)S(1)} %get-tuple-element.109), channel_id=1, source_target_pairs={{0,2},{2,4},{4,6},{6,8},{8,10},{10,12},{12,14},{14,0},{1,3},{3,5},... | collective-permute-start | bytes 2359304 | tf_op jit(solution)/shard_map/ppermute | solution.py:197
  47.3 27.8 %collective-permute-start.12 = (f32[128,1536]{1,0:T(8,128)S(1)}, f32[128,1536]{1,0:T(8,128)S(1)}, u32[]{:S(2)}, u32[]{:S(2)}) collective-permute-start(f32[128,1536]{1,0:T(8,128)S(1)} %get-tuple-element.108), channel_id=1, source_target_pairs={{0,14},{2,0},{4,2},{6,4},{8,6},{10,8},{12,10},{14,12},{1,15},{3,1}... | collective-permute-start | bytes 2359304 | tf_op jit(solution)/shard_map/ppermute | solution.py:201
  60.9 4.6 %collective-permute-start.9 = (f32[8,32,128]{2,1,0:T(8,128)S(1)}, f32[8,32,128]{2,1,0:T(8,128)S(1)}, u32[]{:S(2)}, u32[]{:S(2)}) collective-permute-start(f32[8,32,128]{2,1,0:T(8,128)S(1)} %partial_coeffs.1), channel_id=1, source_target_pairs={{0,16},{16,0},{1,17},{17,1},{2,18},{18,2},{3,19},{19,3},{4,20},{20... | collective-permute-start | bytes 393224 | tf_op jit(solution)/shard_map/ppermute | solution.py:193
  64.4 30.4 %collective-permute-start.19 = (f32[128,1792]{1,0:T(8,128)S(1)}, f32[128,1792]{1,0:T(8,128)S(1)}, u32[]{:S(2)}, u32[]{:S(2)}) collective-permute-start(f32[128,1792]{1,0:T(8,128)S(1)} %fusion), channel_id=1, source_target_pairs={{0,14},{2,0},{4,2},{6,4},{8,6},{10,8},{12,10},{14,12},{1,15},{3,1}... | collective-permute-start | bytes 2752520 | tf_op jit(solution)/shard_map/ppermute | solution.py:201
  65.5 5.7 %collective-permute-start.10 = (f32[8,32,128]{2,1,0:T(8,128)S(1)}, f32[8,32,128]{2,1,0:T(8,128)S(1)}, u32[]{:S(2)}, u32[]{:S(2)}) collective-permute-start(f32[8,32,128]{2,1,0:T(8,128)S(1)} %add.388), channel_id=1, source_target_pairs={{0,64},{64,0},{128,192},{192,128},{1,65},{65,1},{129,193},{193,129... | collective-permute-start | bytes 393224 | tf_op jit(solution)/shard_map/ppermute | solution.py:193
  67.1 27.7 %collective-permute-start.18 = (f32[128,1792]{1,0:T(8,128)S(1)}, f32[128,1792]{1,0:T(8,128)S(1)}, u32[]{:S(2)}, u32[]{:S(2)}) collective-permute-start(f32[128,1792]{1,0:T(8,128)S(1)} %pad_maximum_fusion.2), channel_id=1, source_target_pairs={{0,2},{2,4},{4,6},{6,8},{8,10},{10,12},{12,14},{14,0},{1,3},{3,5},... | collective-permute-start | bytes 2752520 | tf_op jit(solution)/shard_map/ppermute | solution.py:197
  75.2 6.5 %collective-permute-start.15 = (f32[8,32,128]{2,1,0:T(8,128)S(1)}, f32[8,32,128]{2,1,0:T(8,128)S(1)}, u32[]{:S(2)}, u32[]{:S(2)}) collective-permute-start(f32[8,32,128]{2,1,0:T(8,128)S(1)} %add.389), channel_id=1, source_target_pairs={{0,128},{64,192},{128,0},{192,64},{1,129},{65,193},{129,1},{193,65... | collective-permute-start | bytes 393224 | tf_op jit(solution)/shard_map/ppermute | solution.py:193
  81.7 5.1 %collective-permute-start.16 = (f32[8,32,128]{2,1,0:T(8,128)S(1)}, f32[8,32,128]{2,1,0:T(8,128)S(1)}, u32[]{:S(2)}, u32[]{:S(2)}) collective-permute-start(f32[8,32,128]{2,1,0:T(8,128)S(1)} %add.400), channel_id=1, source_target_pairs={{0,32},{32,0},{1,33},{33,1},{2,34},{34,2},{3,35},{35,3},{4,36},{36... | collective-permute-start | bytes 393224 | tf_op jit(solution)/shard_map/ppermute | solution.py:193
  86.7 8.1 %collective-permute-start.17 = (f32[8,32,128]{2,1,0:T(8,128)S(1)}, f32[8,32,128]{2,1,0:T(8,128)S(1)}, u32[]{:S(2)}, u32[]{:S(2)}) collective-permute-start(f32[8,32,128]{2,1,0:T(8,128)S(1)} %add.401), channel_id=1, source_target_pairs={{0,1},{1,0},{2,3},{3,2},{4,5},{5,4},{6,7},{7,6},{8,9},{9,8},{10,11... | collective-permute-start | bytes 393224 | tf_op jit(solution)/shard_map/ppermute | solution.py:193
  90.6 32.3 %copy-start.4 = (bf16[128,128]{1,0:T(8,128)(2,1)S(1)}, bf16[128,128]{1,0:T(8,128)(2,1)}, u32[]{:S(2)}) copy-start(bf16[128,128]{1,0:T(8,128)(2,1)} %constant.194.clone.refs_4_.refs_11_) | copy-start | bytes 98308
  90.6 22.6 %collective-permute-start.13 = (f32[128,1536]{1,0:T(8,128)S(1)}, f32[128,1536]{1,0:T(8,128)S(1)}, u32[]{:S(2)}, u32[]{:S(2)}) collective-permute-start(f32[128,1536]{1,0:T(8,128)S(1)} %get-tuple-element.105), channel_id=1, source_target_pairs={{0,2},{2,4},{4,6},{6,8},{8,10},{10,12},{12,14},{14,0},{1,3},{3,5},... | collective-permute-start | bytes 2359304 | tf_op jit(solution)/shard_map/ppermute | solution.py:197
  92.8 20.5 %collective-permute-start.14 = (f32[128,1536]{1,0:T(8,128)S(1)}, f32[128,1536]{1,0:T(8,128)S(1)}, u32[]{:S(2)}, u32[]{:S(2)}) collective-permute-start(f32[128,1536]{1,0:T(8,128)S(1)} %get-tuple-element.104), channel_id=1, source_target_pairs={{0,14},{2,0},{4,2},{6,4},{8,6},{10,8},{12,10},{14,12},{1,15},{3,1}... | collective-permute-start | bytes 2359304 | tf_op jit(solution)/shard_map/ppermute | solution.py:201
  95.2 37.4 %collective-permute-start.23 = (f32[128,2048]{1,0:T(8,128)S(1)}, f32[128,2048]{1,0:T(8,128)S(1)}, u32[]{:S(2)}, u32[]{:S(2)}) collective-permute-start(f32[128,2048]{1,0:T(8,128)S(1)} %pad_maximum_fusion.1), channel_id=1, source_target_pairs={{0,14},{2,0},{4,2},{6,4},{8,6},{10,8},{12,10},{14,12},{1,15},{3,1}... | collective-permute-start | bytes 3145736 | tf_op jit(solution)/shard_map/ppermute | solution.py:201
  98.7 34.6 %collective-permute-start.22 = (f32[128,2048]{1,0:T(8,128)S(1)}, f32[128,2048]{1,0:T(8,128)S(1)}, u32[]{:S(2)}, u32[]{:S(2)}) collective-permute-start(f32[128,2048]{1,0:T(8,128)S(1)} %pad_maximum_fusion), channel_id=1, source_target_pairs={{0,2},{2,4},{4,6},{6,8},{8,10},{10,12},{12,14},{14,0},{1,3},{3,5},... | collective-permute-start | bytes 3145736 | tf_op jit(solution)/shard_map/ppermute | solution.py:197
  113.5 9.4 %collective-permute-start.20 = (f32[64,1536]{1,0:T(8,128)S(1)}, f32[64,1536]{1,0:T(8,128)S(1)}, u32[]{:S(2)}, u32[]{:S(2)}) collective-permute-start(f32[64,1536]{1,0:T(8,128)S(1)} %get-tuple-element.118), channel_id=1, source_target_pairs={{0,1},{1,0},{2,3},{3,2},{4,5},{5,4},{6,7},{7,6},{8,9},{9,8},{10,11... | collective-permute-start | bytes 1179656 | tf_op jit(solution)/shard_map/ppermute | solution.py:193
  116.1 16.3 %collective-permute-start.21 = (f32[4,32,128]{2,1,0:T(8,128)S(1)}, f32[4,32,128]{2,1,0:T(8,128)S(1)}, u32[]{:S(2)}, u32[]{:S(2)}) collective-permute-start(f32[4,32,128]{2,1,0:T(8,128)S(1)} %get-tuple-element.141), channel_id=1, source_target_pairs={{0,2},{2,0},{4,6},{6,4},{8,10},{10,8},{12,14},{14,12},{1,3},{3,1},... | collective-permute-start | bytes 196616 | tf_op jit(solution)/shard_map/ppermute | solution.py:193
  133.5 10.3 %collective-permute-start.27 = (f32[128,512]{1,0:T(8,128)S(1)}, f32[128,512]{1,0:T(8,128)S(1)}, u32[]{:S(2)}, u32[]{:S(2)}) collective-permute-start(f32[128,512]{1,0:T(8,128)S(1)} %maximum_add_fusion.3), channel_id=1, source_target_pairs={{0,14},{2,0},{4,2},{6,4},{8,6},{10,8},{12,10},{14,12},{1,15},{3,1}... | collective-permute-start | bytes 786440 | tf_op jit(solution)/shard_map/ppermute | solution.py:201
  136.8 7.9 %collective-permute-start.26 = (f32[128,512]{1,0:T(8,128)S(1)}, f32[128,512]{1,0:T(8,128)S(1)}, u32[]{:S(2)}, u32[]{:S(2)}) collective-permute-start(f32[128,512]{1,0:T(8,128)S(1)} %maximum_add_fusion.2), channel_id=1, source_target_pairs={{0,2},{2,4},{4,6},{6,8},{8,10},{10,12},{12,14},{14,0},{1,3},{3,5},... | collective-permute-start | bytes 786440 | tf_op jit(solution)/shard_map/ppermute | solution.py:197
  137.9 5.9 %collective-permute-start.25 = (f32[4,32,128]{2,1,0:T(8,128)S(1)}, f32[4,32,128]{2,1,0:T(8,128)S(1)}, u32[]{:S(2)}, u32[]{:S(2)}) collective-permute-start(f32[4,32,128]{2,1,0:T(8,128)S(1)} %add.433), channel_id=1, source_target_pairs={{0,4},{2,6},{4,0},{6,2},{8,12},{10,14},{12,8},{14,10},{1,5},{3,7},... | collective-permute-start | bytes 196616 | tf_op jit(solution)/shard_map/ppermute | solution.py:193
  140.7 22.8 %collective-permute-start.24 = (f32[64,1536]{1,0:T(8,128)}, f32[64,1536]{1,0:T(8,128)S(1)}, u32[]{:S(2)}, u32[]{:S(2)}) collective-permute-start(f32[64,1536]{1,0:T(8,128)} %get-tuple-element.116), channel_id=1, source_target_pairs={{0,1},{1,0},{2,3},{3,2},{4,5},{5,4},{6,7},{7,6},{8,9},{9,8},{10,11... | collective-permute-start | bytes 1179656 | tf_op jit(solution)/shard_map/ppermute | solution.py:193
  146.1 8.9 %collective-permute-start.28 = (f32[4,32,128]{2,1,0:T(8,128)S(1)}, f32[4,32,128]{2,1,0:T(8,128)S(1)}, u32[]{:S(2)}, u32[]{:S(2)}) collective-permute-start(f32[4,32,128]{2,1,0:T(8,128)S(1)} %add.434), channel_id=1, source_target_pairs={{0,8},{2,10},{4,12},{6,14},{8,0},{10,2},{12,4},{14,6},{1,9},{3,11}... | collective-permute-start | bytes 196616 | tf_op jit(solution)/shard_map/ppermute | solution.py:193
  150.2 14.0 %collective-permute-start.31 = (f32[128,512]{1,0:T(8,128)}, f32[128,512]{1,0:T(8,128)S(1)}, u32[]{:S(2)}, u32[]{:S(2)}) collective-permute-start(f32[128,512]{1,0:T(8,128)} %maximum_add_fusion.5), channel_id=1, source_target_pairs={{0,14},{2,0},{4,2},{6,4},{8,6},{10,8},{12,10},{14,12},{1,15},{3,1}... | collective-permute-start | bytes 786440 | tf_op jit(solution)/shard_map/ppermute | solution.py:201
  152.1 12.2 %collective-permute-start.30 = (f32[128,512]{1,0:T(8,128)}, f32[128,512]{1,0:T(8,128)}, u32[]{:S(2)}, u32[]{:S(2)}) collective-permute-start(f32[128,512]{1,0:T(8,128)} %maximum_add_fusion.4), channel_id=1, source_target_pairs={{0,2},{2,4},{4,6},{6,8},{8,10},{10,12},{12,14},{14,0},{1,3},{3,5},... | collective-permute-start | bytes 786440 | tf_op jit(solution)/shard_map/ppermute | solution.py:197
  157.3 6.9 %collective-permute-start.29 = (f32[8,128]{1,0:T(8,128)}, f32[8,128]{1,0:T(8,128)S(1)}, u32[]{:S(2)}, u32[]{:S(2)}) collective-permute-start(f32[8,128]{1,0:T(8,128)} %squares.1.refs_2_), channel_id=1, source_target_pairs={{0,2},{2,0},{4,6},{6,4},{8,10},{10,8},{12,14},{14,12},{1,3},{3,1},... | collective-permute-start | bytes 12296 | tf_op jit(solution)/shard_map/ppermute | solution.py:193
  160.1 1.6 copy-start.2
  164.3 0.7 copy-start.5

commit v2 on v1

--- a/solution.py
+++ b/solution.py
@@ -113,8 +113,8 @@
     return mom - own
 
 
-def finish_kernel(mom_ref, *refs):
-    *parts, first_ref, second_ref, same_ref, out_ref = refs
+def finish_kernel(has_front, mom_ref, *refs):
+    *parts, first_ref, second_ref, same_ref, out_ref = refs[has_front:]
     out_ref[...] = new_momentum(mom_ref, parts, first_ref, second_ref, same_ref)
 
 
@@ -122,71 +122,78 @@
     return pl.BlockSpec(x.shape, lambda i: (0, 0))
 
 
-def finish(mom, at, width, parts, first, second, same):
+def finish(front, mom, at, width, parts, first, second, same):
+    front = [] if front is None else [front]
     others = (*parts, first, second, same)
+    columns = pl.BlockSpec((SPAN, width), lambda i: (0, at // width))
     return pl.pallas_call(
-        finish_kernel,
-        out_shape=jax.ShapeDtypeStruct((SPAN, width), jnp.float32),
+        functools.partial(finish_kernel, len(front)),
+        out_shape=jax.ShapeDtypeStruct((SPAN, COLS), jnp.float32),
         grid=(1,),
-        in_specs=[pl.BlockSpec((SPAN, width), lambda i: (0, at // width)), *map(whole, others)],
-        out_specs=pl.BlockSpec((SPAN, width), lambda i: (0, 0)),
+        in_specs=[columns, *[pl.BlockSpec(memory_space=pl.ANY)] * len(front), *map(whole, others)],
+        out_specs=columns,
+        input_output_aliases={1: 0} if front else {},
         compiler_params=pltpu.CompilerParams(vmem_limit_bytes=VMEM_LIMIT),
         cost_estimate=NO_COST,
         name="finish",
-    )(mom, *others)
-
-
-def last_kernel(n_fronts, *refs):
-    squares_ref, more_ref, average_ref = refs[n_fronts : n_fronts + 3]
-    mom_ref, *parts, first_ref, second_ref, same_ref, out_ref, dir_ref = refs[n_fronts + 3 :]
+    )(mom, *front, *others)
+
+
+def last_kernel(front_ref, squares_ref, more_ref, average_ref, mom_ref, *refs):
+    *parts, first_ref, second_ref, same_ref, out_ref, dir_ref = refs
     mean_square = jnp.sum(squares_ref[...] + more_ref[...]) / (ROWS * COLS) + 1e-06
     scale = lax.rsqrt(mean_square)
     scale = scale * (1.5 - 0.5 * (mean_square * scale) * scale)
     dir_ref[...] = average_ref[...] * scale
-    at = 0
-    for ref in refs[:n_fronts]:
-        out_ref[:, at : at + ref.shape[1]] = ref[...]
-        at += ref.shape[1]
-    out_ref[:, at:] = new_momentum(mom_ref, parts, first_ref, second_ref, same_ref)
-
-
-def last(fronts, squares, more, average, mom, at, width, parts, first, second, same):
-    before, others = (*fronts, squares, more, average), (*parts, first, second, same)
+    out_ref[...] = new_momentum(mom_ref, parts, first_ref, second_ref, same_ref)
+
+
+def last(front, squares, more, average, mom, at, width, parts, first, second, same):
+    before, others = (squares, more, average), (*parts, first, second, same)
     out = jax.ShapeDtypeStruct((SPAN, COLS), jnp.float32)
+    columns = pl.BlockSpec((SPAN, width), lambda i: (0, at // width))
     return pl.pallas_call(
-        functools.partial(last_kernel, len(fronts)),
+        last_kernel,
         out_shape=[out, out],
         grid=(1,),
-        in_specs=[
-            *map(whole, before),
-            pl.BlockSpec((SPAN, width), lambda i: (0, at // width)),
-            *map(whole, others),
-        ],
-        out_specs=[whole(out), whole(out)],
+        in_specs=[pl.BlockSpec(memory_space=pl.ANY), *map(whole, before), columns, *map(whole, others)],
+        out_specs=[columns, whole(out)],
+        input_output_aliases={0: 0},
         compiler_params=pltpu.CompilerParams(vmem_limit_bytes=VMEM_LIMIT),
         cost_estimate=NO_COST,
         name="last",
-    )(*before, mom, *others)
-
-
-def decode_kernel(where_ref, coeffs_ref, first_ref, second_ref, spread_ref, out_ref):
-    along = along_blocks(coeffs_ref[...], spread_ref[where_ref[1]]) * second_ref[...]
+    )(front, *before, mom, *others)
+
+
+def average_kernel(where_ref, coeffs_ref, more_ref, gram_ref, first_ref, second_ref, spread_ref, squares_ref, out_ref):
+    total = jnp.zeros((BAND, 128), jnp.float32)
+    for i in range(coeffs_ref.shape[0]):
+        coeffs = (coeffs_ref[i] + more_ref[i]) * (1.0 / REPS)
+        total += coeffs * jnp.dot(
+            gram_ref[...], coeffs, precision=HIGHEST, preferred_element_type=jnp.float32
+        )
+    squares_ref[...] = (total[:8] + total[8:16]) + (total[16:24] + total[24:])
+    row = where_ref[0] // 2
+    coeffs = (coeffs_ref[row] + more_ref[row]) * (1.0 / REPS)
+    half = COLS // SPAN
+    coeffs = jnp.where(where_ref[1] == 0, coeffs[:, :half], coeffs[:, half:])
+    along = along_blocks(coeffs, spread_ref[...]) * second_ref[...]
     out_ref[...] = lax.dot_general(
         first_ref[...], along, (((0,), (0,)), ((), ())), precision=HIGHEST,
         preferred_element_type=jnp.float32,
     )
 
 
-def decode(where, coeffs, first, second, spread):
+def average_of(where, coeffs, more, gram, first, second, spread):
     vmem = pl.BlockSpec(memory_space=pltpu.VMEM)
     return pl.pallas_call(
-        decode_kernel,
-        out_shape=jax.ShapeDtypeStruct((SPAN, COLS), jnp.float32),
-        in_specs=[pl.BlockSpec(memory_space=pltpu.SMEM)] + [vmem] * 4,
+        average_kernel,
+        out_shape=[jax.ShapeDtypeStruct((8, 128), jnp.float32), jax.ShapeDtypeStruct((SPAN, COLS), jnp.float32)],
+        in_specs=[pl.BlockSpec(memory_space=pltpu.SMEM)] + [vmem] * 6,
         compiler_params=pltpu.CompilerParams(vmem_limit_bytes=VMEM_LIMIT),
         cost_estimate=NO_COST,
-        name="decode",
-    )(where, coeffs, first, second, spread)
+        name="average",
+    )(where, coeffs, more, gram, first, second, spread)
 
 
 def flip(x, axis, size, bit):
@@ -219,25 +226,6 @@
 
 def swap_three(x, axes, one, two):
     return [x] + [swap(x, axes, flips) for flips in ((one, 0), (0, two), (one, two))]
-
-
-def squares_kernel(coeffs_ref, gram_ref, out_ref):
-    total = jnp.zeros((BAND, 128), jnp.float32)
-    for i in range(coeffs_ref.shape[0]):
-        coeffs = coeffs_ref[i]
-        total += coeffs * jnp.dot(
-            gram_ref[...], coeffs, precision=HIGHEST, preferred_element_type=jnp.float32
-        )
-    out_ref[...] = (total[:8] + total[8:16]) + (total[16:24] + total[24:])
-
-
-def squares_of(coeffs, gram):
-    return pl.pallas_call(
-        squares_kernel,
-        out_shape=jax.ShapeDtypeStruct((8, 128), jnp.float32),
-        cost_estimate=NO_COST,
-        name="squares",
-    )(coeffs, gram)
 
 
 class Ring:
@@ -297,7 +285,7 @@
     ones = np.zeros((2, COLS, 128), np.float32)
     for half in range(2):
         ones[half, np.arange(COLS), half * 64 + block_of] = 1.0
-    spread = jnp.asarray(ones.transpose(0, 2, 1), jnp.bfloat16)
+    spread = jnp.asarray(ones[0, :, : COLS // SPAN].T, jnp.bfloat16)
     ones = jnp.asarray(ones, jnp.bfloat16)
     same = jnp.asarray(np.kron(np.eye(2), np.ones((SPAN, SPAN))), jnp.bfloat16)
 
@@ -349,53 +337,54 @@
     b.land(rest[:2])
     ring_y = Ring(y_block(got), Y_COLS // 2)
     b = Flight(ring_b, ring_y)
-    coeffs = coeffs + flip(coeffs, "c", 2, 1)
-    coeffs = coeffs + flip(coeffs, "x", 4, 1)
+    for axis, size, bit in (("c", 2, 1), ("x", 4, 1)):
+        coeffs = coeffs + flip(coeffs, axis, size, bit)
 
     coeffs, *rest = meet(coeffs, *a.got, *b.sent)
     a.land(rest[:2])
     a = Flight(ring_a)
     coeffs = coeffs + flip(coeffs, "x", 4, 2)
-    coeffs = coeffs + flip(coeffs, "yl", 2, 1)
-    coeffs = coeffs + flip(coeffs, "yh", 2, 1)
-
-    coeffs, *rest = meet(coeffs, *b.got, *a.sent)
+    pairs = coeffs.reshape(4, 2, BAND, 128)
+    keep = lax.dynamic_index_in_dim(pairs, z % 2, 1, keepdims=False)
+    other = lax.dynamic_index_in_dim(pairs, 1 - z % 2, 1, keepdims=False)
+    more = flip(other, "z", NZ, 1)
+
+    keep, more, *rest = meet(keep, more, *b.got, *a.sent)
     b.land(rest[:2])
     b = Flight(ring_b, ring_y)
-    pairs = coeffs.reshape(4, 2, BAND, 128)
-    side = z % 2
-    keep = lax.dynamic_index_in_dim(pairs, side, 1, keepdims=False)
-    other = lax.dynamic_index_in_dim(pairs, 1 - side, 1, keepdims=False)
-    more = flip(other, "z", NZ, 1)
-
-    a.land(meet(*a.got, *b.sent, other)[:2])
-    keep_a, give_a, got_a = cross_y(sum(ring_a.parts()))
-
-    front_a = finish(mom, 0, CHUNK, [keep_a, got_a], first, pair, same)
-
-    front_a, keep, more, *rest = meet(front_a, keep, more, *b.got)
+    coeffs = after(keep, *b.sent) + more
+    coeffs = coeffs + flip(coeffs, "yl", 2, 1)
+
+    coeffs, *rest = meet(coeffs, *a.got)
+    a.land(rest)
+    total = sum(ring_a.parts())
+    keep_a = lax.dynamic_slice(total, (yh * SPAN, 0), (SPAN, CHUNK))
+    give_a = lax.dynamic_slice(total, ((1 - yh) * SPAN, 0), (SPAN, CHUNK))
+    flat = coeffs.reshape(2, SPAN, 128)
+    got_a = flip(jnp.concatenate([give_a, flat[0], flat[1]], axis=1), "yh", 2, 1)
+    got_a, more = got_a[:, :CHUNK], got_a[:, CHUNK:]
+    coeffs = coeffs + jnp.stack([more[:, :128], more[:, 128:]]).reshape(4, BAND, 128)
+    more = flip(coeffs, "z", NZ, 2)
+    front = finish(None, mom, 0, CHUNK, [keep_a, after(got_a, coeffs)], first, pair, same)
+
+    coeffs, more, front, *rest = meet(coeffs, more, front, *b.got)
     b.land(rest)
     y = Flight(ring_y)
-    keep_b, give_b, got_b = cross_y(after(sum(ring_b.parts()), *y.sent))
-    coeffs = after(keep, give_b) + more
-    coeffs = coeffs + flip(coeffs, "z", NZ, 2)
-
-    coeffs, *rest = meet(coeffs, *y.got)
-    y.land(rest)
+    coeffs = after(coeffs, *y.sent) + more
+    more = flip(coeffs, "z", NZ, 4)
+    keep_b, give_b, got_b = cross_y(after(sum(ring_b.parts()), coeffs))
+
+    y.land(meet(*y.got, give_b)[:2])
     y = Flight(ring_y)
-    coeffs = after(coeffs, *y.sent)
-    coeffs = (coeffs + flip(coeffs, "z", NZ, 4)) * (1.0 / REPS)
-
-    squares = squares_of(coeffs, gram)
+
+    squares, average = average_of(where, after(coeffs, *y.sent), more, gram, first, second, spread)
     more = flip(squares, "z", NZ, 1)
-    coeffs = lax.dynamic_index_in_dim(coeffs, z // 2, 0, keepdims=False)
-    average = decode(where, after(coeffs, squares), first, second, spread)
-    front_b = finish(mom, CHUNK, CHUNK, [keep_b, after(got_b, average)], first, pair, same)
-
-    front_b, average, squares, more, *rest = meet(front_b, average, squares, more, *y.got)
+    front = finish(front, mom, CHUNK, CHUNK, [keep_b, after(got_b, average)], first, pair, same)
+
+    front, average, squares, more, *rest = meet(front, average, squares, more, *y.got)
     y.land(rest)
     momentum, step_dir = last(
-        [front_a, front_b], squares, more, average, mom, Y_AT, Y_COLS, ring_y.parts(), first, pair, same
+        front, squares, more, average, mom, Y_AT, Y_COLS, ring_y.parts(), first, pair, same
     )
     return (momentum[None], step_dir)
 

time: 170 us -> 162 us (0.953)
  waiting for transfers between devices: 58.2 us -> 42.8 us
  other arithmetic: 18 us -> 28.1 us
  starting transfers between devices: 62.4 us -> 60.4 us
    ppermute x10, waiting for transfers between devices: 30.3 us -> 20.3 us  [up(): return lax.ppermute(x, 'z', [(i, (i + 1) % NZ) for i in range(NZ)])]
    ppermute x12 -> x11, starting transfers between devices: 29.2 us -> 24 us  [flip(): return lax.ppermute(x, axis, [(i, i ^ bit) for i in range(size)])]
    ppermute x12 -> x11, waiting for transfers between devices: 27.5 us -> 22.5 us  [flip(): return lax.ppermute(x, axis, [(i, i ^ bit) for i in range(size)])]
    add x12, other arithmetic: 10.4 us -> 14.2 us  [next(): terms = (self.block(self.step) + upward, self.block(-self.step) + downward)]
    concatenate x4, other arithmetic: 0.26 us -> 3.08 us  [__init__(): jnp.concatenate(list(side), axis=1)]
    ppermute x10, starting transfers between devices: 4.58 us -> 7.35 us  [up(): return lax.ppermute(x, 'z', [(i, (i + 1) % NZ) for i in range(NZ)])]
    add x7, other arithmetic: 0.33 us -> 2.8 us  [the longest x1 1.6 us: per_device(): total = sum(ring_a.parts())]
    unnamed x14 -> x22, local copies, waits for them, and re-layouts: 7.26 us -> 5.02 us
  transfers between devices with their start and end apart: 32 -> 31, of which waited for: 16 -> 14; matrix products, arithmetic and copies ran while one was open for 12% -> 20% of each run, Pallas kernels for 8% -> 9%
where the time goes in v2:
time: 162 us; the launch traced here: 159 us
  starting transfers between devices  60.4 us (37%)
  waiting for transfers between devices  42.8 us (26%)
  other arithmetic  28.1 us (17%)
  Pallas kernels  15.9 us (10%)
  local copies, waits for them, and re-layouts  9.39 us (6%)
    ppermute x10, starting transfers between devices, down(): return lax.ppermute(x, 'z', [(i, (i - 1) % NZ) for i in range(NZ)])  29.1 us
    ppermute x11, starting transfers between devices, flip(): return lax.ppermute(x, axis, [(i, i ^ bit) for i in range(size)])  24 us
    ppermute x11, waiting for transfers between devices, flip(): return lax.ppermute(x, axis, [(i, i ^ bit) for i in range(size)])  22.5 us
    ppermute x10, waiting for transfers between devices, up(): return lax.ppermute(x, 'z', [(i, (i + 1) % NZ) for i in range(NZ)])  20.3 us
    add x12, other arithmetic, next(): terms = (self.block(self.step) + upward, self.block(-self.step) + downward)  14.2 us
    pallas_call x1, Pallas kernels, partial_coeffs(): pl.pallas_call(partial_coeffs_kernel, out_shape=jax.ShapeDtypeStruct((NZ,...  9.25 us
    ppermute x10, starting transfers between devices, up(): return lax.ppermute(x, 'z', [(i, (i + 1) % NZ) for i in range(NZ)])  7.35 us
    unnamed x22, local copies, waits for them, and re-layouts  5.02 us
  transfers between devices with their start and end apart: 31, of which 14 were waited for; matrix products, arithmetic and copies ran while one was open for 20% of the time, Pallas kernels for 9%

profile of v2, /device:TPU:0, one launch (start us, length us, event | category | flops | bytes accessed | tf_op | source)
XLA Modules:
  0.0 159.2 jit_solution(2688488039289162020)
XLA Ops:
  0.7 1.3 bitcast_convert_fusion.1
  2.0 0.3 collective-permute-start.3
  2.3 4.0 %collective-permute-start.4 = (f32[128,768]{1,0:T(8,128)S(1)}, f32[128,768]{1,0:T(8,128)}, u32[]{:S(2)}, u32[]{:S(2)}) collective-permute-start(f32[128,768]{1,0:T(8,128)S(1)} %get-tuple-element.130), channel_id=1, source_target_pairs={{0,14},{2,0},{4,2},{6,4},{8,6},{10,8},{12,10},{14,12},{1,15},{3,1}... | collective-permute-start | bytes 1179656 | tf_op jit(solution)/shard_map/ppermute | solution.py:208
  6.5 3.2 %collective-permute-start.2 = (f32[128,768]{1,0:T(8,128)S(1)}, f32[128,768]{1,0:T(8,128)S(1)}, u32[]{:S(2)}, u32[]{:S(2)}) collective-permute-start(f32[128,768]{1,0:T(8,128)S(1)} %get-tuple-element.128), channel_id=1, source_target_pairs={{0,14},{2,0},{4,2},{6,4},{8,6},{10,8},{12,10},{14,12},{1,15},{3,1}... | collective-permute-start | bytes 1179656 | tf_op jit(solution)/shard_map/ppermute | solution.py:208
  9.7 2.8 %dynamic-slice_convert_fusion = f32[8,64,1024]{2,1,0:T(8,128)} fusion(bf16[8,128,4096]{2,1,0:T(8,128)(2,1)} %bitcast.110, s32[]{:T(128)S(6)} %select_n.129), kind=kLoop, calls=%fused_computation.3 | loop fusion | flops 524288 | bytes 3145732 | tf_op jit(solution)/shard_map/convert_element_type | solution.py:320
  12.5 3.2 %collective-permute-start = (f32[8,64,1024]{2,1,0:T(8,128)}, f32[8,64,1024]{2,1,0:T(8,128)}, u32[]{:S(2)}, u32[]{:S(2)}) collective-permute-start(f32[8,64,1024]{2,1,0:T(8,128)} %dynamic-slice_convert_fusion), channel_id=1, source_target_pairs={{0,1},{1,0},{2,3},{3,2},{4,5},{5,4},{6,7},{7,6},{8,9},{9,8},{10,11... | collective-permute-start | bytes 6291464 | tf_op jit(solution)/shard_map/ppermute | solution.py:200
  15.9 0.4 collective-permute-done.3
  16.3 2.7 %convert_add_fusion.11 = (f32[128,1536]{1,0:T(8,128)}, f32[128,1536]{1,0:T(8,128)}) fusion(f32[128,768]{1,0:T(8,128)} %collective-permute-done.4, bf16[1,1,1024,4096]{3,2,1,0:T(8,128)(2,1)} %param.6, s32[]{:T(128)S(6)} %select_n.131, f32[128,768]{1,0:T(8,128)} %collective-permute-done.3, s32[]{:T(128)S(6)} %select_n.130), kind=kLoop, calls=%fused_computation.21 | loop fusion | flops 786432 | bytes 3145736 | tf_op jit(solution)/shard_map/add | solution.py:248
  19.0 3.3 %collective-permute-start.6 = (f32[128,1536]{1,0:T(8,128)}, f32[128,1536]{1,0:T(8,128)}, u32[]{:S(2)}, u32[]{:S(2)}) collective-permute-start(f32[128,1536]{1,0:T(8,128)} %get-tuple-element.120), channel_id=1, source_target_pairs={{0,14},{2,0},{4,2},{6,4},{8,6},{10,8},{12,10},{14,12},{1,15},{3,1}... | collective-permute-start | bytes 2359304 | tf_op jit(solution)/shard_map/ppermute | solution.py:208
  22.3 2.3 %collective-permute-done.1 = f32[128,768]{1,0:T(8,128)S(1)} collective-permute-done((f32[128,768]{1,0:T(8,128)S(1)}, f32[128,768]{1,0:T(8,128)S(1)}, u32[]{:S(2)}, u32[]{:S(2)}) %collective-permute-start.1) | collective-permute-done | bytes 393248 | tf_op jit(solution)/shard_map/ppermute | solution.py:204
  24.6 2.5 %convert_add_fusion.10 = (f32[128,1536]{1,0:T(8,128)}, f32[128,1536]{1,0:T(8,128)}) fusion(f32[128,768]{1,0:T(8,128)S(1)} %collective-permute-done.2, bf16[1,1,1024,4096]{3,2,1,0:T(8,128)(2,1)} %param.6, s32[]{:T(128)S(6)} %select_n.131, f32[128,768]{1,0:T(8,128)S(1)} %collective-permute-done.1, s32[]{:T(128)S(6)} %select_n.130), kind=kLoop, calls=%fused_computation.20 | loop fusion | flops 786432 | bytes 3145736 | tf_op jit(solution)/shard_map/add | solution.py:248
  27.1 3.4 %collective-permute-start.8 = (f32[128,1536]{1,0:T(8,128)}, f32[128,1536]{1,0:T(8,128)}, u32[]{:S(2)}, u32[]{:S(2)}) collective-permute-start(f32[128,1536]{1,0:T(8,128)} %get-tuple-element.118), channel_id=1, source_target_pairs={{0,14},{2,0},{4,2},{6,4},{8,6},{10,8},{12,10},{14,12},{1,15},{3,1}... | collective-permute-start | bytes 2359304 | tf_op jit(solution)/shard_map/ppermute | solution.py:208
  30.7 0.4 tile.10.second_ref
  31.2 3.4 %copy-done = bf16[1,1,1024,4096]{3,2,1,0:T(8,128)(2,1)S(1)} copy-done((bf16[1,1,1024,4096]{3,2,1,0:T(8,128)(2,1)S(1)}, bf16[1,1,1024,4096]{3,2,1,0:T(8,128)(2,1)}, u32[]{:S(2)}) %copy-start) | copy-done | bytes 8388632
  34.6 1.6 copy-done.2
  36.2 9.3 %partial_coeffs.1 = f32[8,32,128]{2,1,0:T(8,128)S(1)} custom-call(s32[2]{0:T(128)S(1)} %pad_add_fusion.where_ref, bf16[1024,4096]{1,0:T(8,128)(2,1)S(1)} %bitcast.111, f32[64,4096]{1,0:T(8,128)S(1)} %bitcast.112, f32[32,64]{1,0:T(8,128)S(1)} %get-tuple-element.155.first_ref.refs_2_.refs_3_, f32[32,4096]{1,0:T(8,128)S(1)} %tile.10.second_ref, ...), custom_call_target="tpu_custom_call" | custom-call | tf_op jit(solution)/shard_map/partial_coeffs/pallas_call | solution.py:75
  45.5 2.7 %convert_add_fusion.8 = (f32[128,1536]{1,0:T(8,128)}, f32[128,1536]{1,0:T(8,128)}) fusion(f32[128,1536]{1,0:T(8,128)} %collective-permute-done.6, bf16[1,1,1024,4096]{3,2,1,0:T(8,128)(2,1)S(1)} %copy-done, s32[]{:T(128)S(6)} %select_n.137, f32[128,1536]{1,0:T(8,128)} %collective-permute-done.5, s32[]{:T(128)S(6)} %select_n.136), kind=kLoop, calls=%fused_computation.18 | loop fusion | flops 786432 | bytes 3932168 | tf_op jit(solution)/shard_map/add | solution.py:248
  48.2 3.2 %collective-permute-start.12 = (f32[128,1536]{1,0:T(8,128)}, f32[128,1536]{1,0:T(8,128)}, u32[]{:S(2)}, u32[]{:S(2)}) collective-permute-start(f32[128,1536]{1,0:T(8,128)} %get-tuple-element.116), channel_id=1, source_target_pairs={{0,14},{2,0},{4,2},{6,4},{8,6},{10,8},{12,10},{14,12},{1,15},{3,1}... | collective-permute-start | bytes 2359304 | tf_op jit(solution)/shard_map/ppermute | solution.py:208
  51.5 6.8 %collective-permute-done.7 = f32[128,1536]{1,0:T(8,128)S(1)} collective-permute-done((f32[128,1536]{1,0:T(8,128)}, f32[128,1536]{1,0:T(8,128)S(1)}, u32[]{:S(2)}, u32[]{:S(2)}) %collective-permute-start.7) | collective-permute-done | bytes 786464 | tf_op jit(solution)/shard_map/ppermute | solution.py:204
  58.3 2.6 %collective-permute-done = f32[8,64,1024]{2,1,0:T(8,128)} collective-permute-done((f32[8,64,1024]{2,1,0:T(8,128)}, f32[8,64,1024]{2,1,0:T(8,128)}, u32[]{:S(2)}, u32[]{:S(2)}) %collective-permute-start) | collective-permute-done | bytes 2097184 | tf_op jit(solution)/shard_map/ppermute | solution.py:200
  60.9 1.3 convert_add_fusion.6
  62.2 2.6 %convert_add_fusion.14 = (f32[64,1024]{1,0:T(8,128)S(1)}, f32[64,1024]{1,0:T(8,128)S(1)}, f32[64,1024]{1,0:T(8,128)S(1)}, f32[64,1024]{1,0:T(8,128)S(1)}, f32[64...) fusion(f32[8,64,1024]{2,1,0:T(8,128)} %collective-permute-done, ...), kind=kLoop, calls=%fused_computation.36 | loop fusion | flops 1048576 | bytes 5242944 | tf_op jit(solution)/shard_map/add | solution.py:305
  64.8 1.0 fusion
  65.9 1.6 collective-permute-start.10
  67.4 1.0 pad_maximum_fusion.2
  68.5 3.2 %collective-permute-start.16 = (f32[128,1792]{1,0:T(8,128)}, f32[128,1792]{1,0:T(8,128)}, u32[]{:S(2)}, u32[]{:S(2)}) collective-permute-start(f32[128,1792]{1,0:T(8,128)} %fusion), channel_id=1, source_target_pairs={{0,14},{2,0},{4,2},{6,4},{8,6},{10,8},{12,10},{14,12},{1,15},{3,1}... | collective-permute-start | bytes 2752520 | tf_op jit(solution)/shard_map/ppermute | solution.py:208
  71.9 3.4 %collective-permute-done.11 = f32[128,1536]{1,0:T(8,128)} collective-permute-done((f32[128,1536]{1,0:T(8,128)}, f32[128,1536]{1,0:T(8,128)}, u32[]{:S(2)}, u32[]{:S(2)}) %collective-permute-start.11) | collective-permute-done | bytes 786464 | tf_op jit(solution)/shard_map/ppermute | solution.py:204
  75.3 3.0 %collective-permute-start.13 = (f32[8,32,128]{2,1,0:T(8,128)S(1)}, f32[8,32,128]{2,1,0:T(8,128)S(1)}, u32[]{:S(2)}, u32[]{:S(2)}) collective-permute-start(f32[8,32,128]{2,1,0:T(8,128)S(1)} %add.378), channel_id=1, source_target_pairs={{0,128},{64,192},{128,0},{192,64},{1,129},{65,193},{129,1},{193,65... | collective-permute-start | bytes 393224 | tf_op jit(solution)/shard_map/ppermute | solution.py:200
  78.3 0.8 fusion.14
  79.0 2.7 %collective-permute-done.13 = f32[8,32,128]{2,1,0:T(8,128)S(1)} collective-permute-done((f32[8,32,128]{2,1,0:T(8,128)S(1)}, f32[8,32,128]{2,1,0:T(8,128)S(1)}, u32[]{:S(2)}, u32[]{:S(2)}) %collective-permute-start.13) | collective-permute-done | bytes 131104 | tf_op jit(solution)/shard_map/ppermute | solution.py:200
  81.9 3.0 %convert_add_fusion.4 = (f32[128,1536]{1,0:T(8,128)}, f32[128,1536]{1,0:T(8,128)}) fusion(f32[128,1536]{1,0:T(8,128)} %collective-permute-done.12, bf16[1,1,1024,4096]{3,2,1,0:T(8,128)(2,1)} %param.6, s32[]{:T(128)S(6)} %select_n.144, f32[128,1536]{1,0:T(8,128)} %collective-permute-done.11, s32[]{:T(128)S(6)} %select_n.143), kind=kLoop, calls=%fused_computation.14 | loop fusion | flops 786432 | bytes 3932168 | tf_op jit(solution)/shard_map/add | solution.py:248
  84.9 2.0 %collective-permute-start.18 = (f32[128,1536]{1,0:T(8,128)}, f32[128,1536]{1,0:T(8,128)}, u32[]{:S(2)}, u32[]{:S(2)}) collective-permute-start(f32[128,1536]{1,0:T(8,128)} %get-tuple-element.113), channel_id=1, source_target_pairs={{0,2},{2,4},{4,6},{6,8},{8,10},{10,12},{12,14},{14,0},{1,3},{3,5},... | collective-permute-start | bytes 2359304 | tf_op jit(solution)/shard_map/ppermute | solution.py:204
  86.9 2.1 %collective-permute-start.19 = (f32[128,1536]{1,0:T(8,128)}, f32[128,1536]{1,0:T(8,128)}, u32[]{:S(2)}, u32[]{:S(2)}) collective-permute-start(f32[128,1536]{1,0:T(8,128)} %get-tuple-element.112), channel_id=1, source_target_pairs={{0,14},{2,0},{4,2},{6,4},{8,6},{10,8},{12,10},{14,12},{1,15},{3,1}... | collective-permute-start | bytes 2359304 | tf_op jit(solution)/shard_map/ppermute | solution.py:208
  89.0 4.6 %collective-permute-done.14 = f32[4,32,128]{2,1,0:T(8,128)S(1)} collective-permute-done((f32[4,32,128]{2,1,0:T(8,128)S(1)}, f32[4,32,128]{2,1,0:T(8,128)S(1)}, u32[]{:S(2)}, u32[]{:S(2)}) %collective-permute-start.14) | collective-permute-done | bytes 65568 | tf_op jit(solution)/shard_map/ppermute | solution.py:200
  93.5 1.4 collective-permute-done.15
  94.9 0.9 slice.125
  95.8 1.8 %convert_add_fusion.2 = (f32[128,1536]{1,0:T(8,128)S(1)}, f32[128,1536]{1,0:T(8,128)S(1)}) fusion(f32[128,1792]{1,0:T(8,128)} %collective-permute-done.16, bf16[1,1,1024,4096]{3,2,1,0:T(8,128)(2,1)} %param.6, s32[]{:T(128)S(6)} %select_n.144, f32[128,1792]{1,0:T(8,128)} %collective-permute-done.15, s32[]{:T(128)S(6)} %select_n.143), kind=kLoop, calls=%fused_computation.12 | loop fusion | flops 786432 | bytes 3932168 | tf_op jit(solution)/shard_map/add | solution.py:248
  97.7 0.9 slice.129
  98.8 1.0 pad_maximum_fusion.1
  99.8 1.7 %collective-permute-start.17 = (f32[4,32,128]{2,1,0:T(8,128)S(1)}, f32[4,32,128]{2,1,0:T(8,128)}, u32[]{:S(2)}, u32[]{:S(2)}) collective-permute-start(f32[4,32,128]{2,1,0:T(8,128)S(1)} %add.407), channel_id=1, source_target_pairs={{0,32},{32,0},{1,33},{33,1},{2,34},{34,2},{3,35},{35,3},{4,36},{36... | collective-permute-start | bytes 196616 | tf_op jit(solution)/shard_map/ppermute | solution.py:200
  101.5 3.4 %collective-permute-start.23 = (f32[128,2048]{1,0:T(8,128)}, f32[128,2048]{1,0:T(8,128)S(1)}, u32[]{:S(2)}, u32[]{:S(2)}) collective-permute-start(f32[128,2048]{1,0:T(8,128)} %pad_maximum_fusion.1), channel_id=1, source_target_pairs={{0,14},{2,0},{4,2},{6,4},{8,6},{10,8},{12,10},{14,12},{1,15},{3,1}... | collective-permute-start | bytes 3145736 | tf_op jit(solution)/shard_map/ppermute | solution.py:208
  104.8 0.9 add.408
  105.7 6.1 %collective-permute-done.18 = f32[128,1536]{1,0:T(8,128)} collective-permute-done((f32[128,1536]{1,0:T(8,128)}, f32[128,1536]{1,0:T(8,128)}, u32[]{:S(2)}, u32[]{:S(2)}) %collective-permute-start.18) | collective-permute-done | bytes 786464 | tf_op jit(solution)/shard_map/ppermute | solution.py:204
  111.8 1.6 %fusion.2 = f32[128,1536]{1,0:T(8,128)S(1)} fusion(f32[128,1536]{1,0:T(8,128)} %collective-permute-done.19, f32[128,1536]{1,0:T(8,128)} %collective-permute-done.18, bf16[1,1,1024,4096]{3,2,1,0:T(8,128)(2,1)} %param.6, s32[]{:T(128)S(6)} %select_n.149), kind=kLoop, calls=%fused_computation.11 | loop fusion | flops 589824 | bytes 2752516 | tf_op jit(solution)/shard_map/add | solution.py:360
  113.5 3.3 %collective-permute-start.20 = (f32[64,1792]{1,0:T(8,128)S(1)}, f32[64,1792]{1,0:T(8,128)S(1)}, u32[]{:S(2)}, u32[]{:S(2)}) collective-permute-start(f32[64,1792]{1,0:T(8,128)S(1)} %pad_maximum_fusion.3), channel_id=1, source_target_pairs={{0,1},{1,0},{2,3},{3,2},{4,5},{5,4},{6,7},{7,6},{8,9},{9,8},{10,11... | collective-permute-start | bytes 1376264 | tf_op jit(solution)/shard_map/ppermute | solution.py:200
  116.8 1.0 fusion.4
  117.8 1.0 fusion.17
  118.9 7.2 %collective-permute-done.20 = f32[64,1792]{1,0:T(8,128)S(1)} collective-permute-done((f32[64,1792]{1,0:T(8,128)S(1)}, f32[64,1792]{1,0:T(8,128)S(1)}, u32[]{:S(2)}, u32[]{:S(2)}) %collective-permute-start.20) | collective-permute-done | bytes 458784 | tf_op jit(solution)/shard_map/ppermute | solution.py:200
  126.0 2.8 %collective-permute-start.21 = (f32[4,32,128]{2,1,0:T(8,128)S(1)}, f32[4,32,128]{2,1,0:T(8,128)S(1)}, u32[]{:S(2)}, u32[]{:S(2)}) collective-permute-start(f32[4,32,128]{2,1,0:T(8,128)S(1)} %add.413), channel_id=1, source_target_pairs={{0,4},{2,6},{4,0},{6,2},{8,12},{10,14},{12,8},{14,10},{1,5},{3,7},... | collective-permute-start | bytes 196616 | tf_op jit(solution)/shard_map/ppermute | solution.py:200
  128.9 1.6 finish.2.refs_0_
  130.5 3.3 %collective-permute-done.21 = f32[4,32,128]{2,1,0:T(8,128)S(1)} collective-permute-done((f32[4,32,128]{2,1,0:T(8,128)S(1)}, f32[4,32,128]{2,1,0:T(8,128)S(1)}, u32[]{:S(2)}, u32[]{:S(2)}) %collective-permute-start.21) | collective-permute-done | bytes 65568 | tf_op jit(solution)/shard_map/ppermute | solution.py:200
  133.9 4.6 %collective-permute-start.25 = (f32[128,512]{1,0:T(8,128)S(1)}, f32[128,512]{1,0:T(8,128)S(1)}, u32[]{:S(2)}, u32[]{:S(2)}) collective-permute-start(f32[128,512]{1,0:T(8,128)S(1)} %maximum_add_fusion.2), channel_id=1, source_target_pairs={{0,2},{2,4},{4,6},{6,8},{8,10},{10,12},{12,14},{14,0},{1,3},{3,5},... | collective-permute-start | bytes 786440 | tf_op jit(solution)/shard_map/ppermute | solution.py:204
  138.5 0.3 collective-permute-start.26
  138.8 1.1 fusion.1
  139.9 4.9 %collective-permute-start.27 = (f32[4,32,128]{2,1,0:T(8,128)S(1)}, f32[4,32,128]{2,1,0:T(8,128)S(1)}, u32[]{:S(2)}, u32[]{:S(2)}) collective-permute-start(f32[4,32,128]{2,1,0:T(8,128)S(1)} %add.427.coeffs_ref), channel_id=1, source_target_pairs={{0,8},{2,10},{4,12},{6,14},{8,0},{10,2},{12,4},{14,6},{1,9},{3,11}... | collective-permute-start | bytes 196616 | tf_op jit(solution)/shard_map/ppermute | solution.py:200
  144.9 3.3 %collective-permute-start.24 = (f32[64,1536]{1,0:T(8,128)S(1)}, f32[64,1536]{1,0:T(8,128)S(1)}, u32[]{:S(2)}, u32[]{:S(2)}) collective-permute-start(f32[64,1536]{1,0:T(8,128)S(1)} %get-tuple-element.124), channel_id=1, source_target_pairs={{0,1},{1,0},{2,3},{3,2},{4,5},{5,4},{6,7},{7,6},{8,9},{9,8},{10,11... | collective-permute-start | bytes 1179656 | tf_op jit(solution)/shard_map/ppermute | solution.py:200
  148.2 0.3 collective-permute-start.29
  148.6 3.0 %collective-permute-start.30 = (f32[128,512]{1,0:T(8,128)S(1)}, f32[128,512]{1,0:T(8,128)S(1)}, u32[]{:S(2)}, u32[]{:S(2)}) collective-permute-start(f32[128,512]{1,0:T(8,128)S(1)} %maximum_add_fusion.5), channel_id=1, source_target_pairs={{0,14},{2,0},{4,2},{6,4},{8,6},{10,8},{12,10},{14,12},{1,15},{3,1}... | collective-permute-start | bytes 786440 | tf_op jit(solution)/shard_map/ppermute | solution.py:208
  151.7 0.3 convolution_multiply_fusion.gram_ref
  152.0 1.8 %average.1 = (f32[8,128]{1,0:T(8,128)S(1)}, f32[64,4096]{1,0:T(8,128)S(1)}) custom-call(s32[2]{0:T(128)S(1)} %pad_add_fusion.where_ref, f32[4,32,128]{2,1,0:T(8,128)S(1)} %add.427.coeffs_ref, f32[4,32,128]{2,1,0:T(8,128)S(1)} %collective-permute-done.27.more_ref, f32[32,32]{1,0:T(8,128)S(1)} %convolution_multiply_fusion.gram_ref, ...), custom_call_target="tpu_custom_call" | custom-call | tf_op jit(solution)/shard_map/average/pallas_call | solution.py:189
  154.0 0.7 collective-permute-done.24.refs_2_
  154.6 1.6 finish.3.front_ref
  156.2 1.3 collective-permute-done.28.more_ref
  157.5 1.7 %last.1 = (f32[64,4096]{1,0:T(8,128)}, f32[64,4096]{1,0:T(8,128)}) custom-call(f32[64,4096]{1,0:T(8,128)} %finish.3.front_ref, f32[8,128]{1,0:T(8,128)S(1)} %get-tuple-element.91.squares_ref, f32[8,128]{1,0:T(8,128)S(1)} %collective-permute-done.28.more_ref, f32[64,4096]{1,0:T(8,128)S(1)} %get-tuple-element.93.average_ref, ...), custom_call_target="tpu_custom_call", output_to_operand_aliasing={{0}: (0, {})} | custom-call | tf_op jit(solution)/shard_map/last/pallas_call | solution.py:155
  (83 shorter events, 1.8 us)
Async XLA Ops:
  0.6 15.1 %copy-start.10 = (s32[32]{0:T(128)S(1)}, s32[32]{0:T(128)}, u32[]{:S(2)}) copy-start(s32[32]{0:T(128)} %param.8) | copy-start | bytes 388
  2.0 29.3 %copy-start.1 = (f32[1,64,4096]{2,1,0:T(8,128)S(1)}, f32[1,64,4096]{2,1,0:T(8,128)}, u32[]{:S(2)}) copy-start(f32[1,64,4096]{2,1,0:T(8,128)} %param.7) | copy-start | bytes 3145732
  2.0 14.2 %collective-permute-start.3 = (f32[128,768]{1,0:T(8,128)S(1)}, f32[128,768]{1,0:T(8,128)}, u32[]{:S(2)}, u32[]{:S(2)}) collective-permute-start(f32[128,768]{1,0:T(8,128)S(1)} %get-tuple-element.131), channel_id=1, source_target_pairs={{0,2},{2,4},{4,6},{6,8},{8,10},{10,12},{12,14},{14,0},{1,3},{3,5},... | collective-permute-start | bytes 1179656 | tf_op jit(solution)/shard_map/ppermute | solution.py:204
  2.3 14.0 %collective-permute-start.4 = (f32[128,768]{1,0:T(8,128)S(1)}, f32[128,768]{1,0:T(8,128)}, u32[]{:S(2)}, u32[]{:S(2)}) collective-permute-start(f32[128,768]{1,0:T(8,128)S(1)} %get-tuple-element.130), channel_id=1, source_target_pairs={{0,14},{2,0},{4,2},{6,4},{8,6},{10,8},{12,10},{14,12},{1,15},{3,1}... | collective-permute-start | bytes 1179656 | tf_op jit(solution)/shard_map/ppermute | solution.py:208
  6.4 18.2 %collective-permute-start.1 = (f32[128,768]{1,0:T(8,128)S(1)}, f32[128,768]{1,0:T(8,128)S(1)}, u32[]{:S(2)}, u32[]{:S(2)}) collective-permute-start(f32[128,768]{1,0:T(8,128)S(1)} %get-tuple-element.129), channel_id=1, source_target_pairs={{0,2},{2,4},{4,6},{6,8},{8,10},{10,12},{12,14},{14,0},{1,3},{3,5},... | collective-permute-start | bytes 1179656 | tf_op jit(solution)/shard_map/ppermute | solution.py:204
  6.5 18.1 %collective-permute-start.2 = (f32[128,768]{1,0:T(8,128)S(1)}, f32[128,768]{1,0:T(8,128)S(1)}, u32[]{:S(2)}, u32[]{:S(2)}) collective-permute-start(f32[128,768]{1,0:T(8,128)S(1)} %get-tuple-element.128), channel_id=1, source_target_pairs={{0,14},{2,0},{4,2},{6,4},{8,6},{10,8},{12,10},{14,12},{1,15},{3,1}... | collective-permute-start | bytes 1179656 | tf_op jit(solution)/shard_map/ppermute | solution.py:208
  12.5 48.3 %collective-permute-start = (f32[8,64,1024]{2,1,0:T(8,128)}, f32[8,64,1024]{2,1,0:T(8,128)}, u32[]{:S(2)}, u32[]{:S(2)}) collective-permute-start(f32[8,64,1024]{2,1,0:T(8,128)} %dynamic-slice_convert_fusion), channel_id=1, source_target_pairs={{0,1},{1,0},{2,3},{3,2},{4,5},{5,4},{6,7},{7,6},{8,9},{9,8},{10,11... | collective-permute-start | bytes 6291464 | tf_op jit(solution)/shard_map/ppermute | solution.py:200
  15.9 81.8 %copy-start.9 = (f32[32]{0:T(128)}, f32[32]{0:T(128)S(1)}, u32[]{:S(2)}) copy-start(f32[32]{0:T(128)S(1)} %convert_element_type.177) | copy-start | bytes 388
  19.0 26.5 %collective-permute-start.5 = (f32[128,1536]{1,0:T(8,128)}, f32[128,1536]{1,0:T(8,128)}, u32[]{:S(2)}, u32[]{:S(2)}) collective-permute-start(f32[128,1536]{1,0:T(8,128)} %get-tuple-element.121), channel_id=1, source_target_pairs={{0,2},{2,4},{4,6},{6,8},{8,10},{10,12},{12,14},{14,0},{1,3},{3,5},... | collective-permute-start | bytes 2359304 | tf_op jit(solution)/shard_map/ppermute | solution.py:204
  19.0 26.5 %collective-permute-start.6 = (f32[128,1536]{1,0:T(8,128)}, f32[128,1536]{1,0:T(8,128)}, u32[]{:S(2)}, u32[]{:S(2)}) collective-permute-start(f32[128,1536]{1,0:T(8,128)} %get-tuple-element.120), channel_id=1, source_target_pairs={{0,14},{2,0},{4,2},{6,4},{8,6},{10,8},{12,10},{14,12},{1,15},{3,1}... | collective-permute-start | bytes 2359304 | tf_op jit(solution)/shard_map/ppermute | solution.py:208
  22.3 23.2 %copy-start.7 = (f32[32]{0:T(128)}, f32[32]{0:T(128)S(1)}, u32[]{:S(2)}) copy-start(f32[32]{0:T(128)S(1)} %fusion.11) | copy-start | bytes 388
  27.1 31.2 %collective-permute-start.7 = (f32[128,1536]{1,0:T(8,128)}, f32[128,1536]{1,0:T(8,128)S(1)}, u32[]{:S(2)}, u32[]{:S(2)}) collective-permute-start(f32[128,1536]{1,0:T(8,128)} %get-tuple-element.119), channel_id=1, source_target_pairs={{0,2},{2,4},{4,6},{6,8},{8,10},{10,12},{12,14},{14,0},{1,3},{3,5},... | collective-permute-start | bytes 2359304 | tf_op jit(solution)/shard_map/ppermute | solution.py:204
  27.1 31.2 %collective-permute-start.8 = (f32[128,1536]{1,0:T(8,128)}, f32[128,1536]{1,0:T(8,128)}, u32[]{:S(2)}, u32[]{:S(2)}) collective-permute-start(f32[128,1536]{1,0:T(8,128)} %get-tuple-element.118), channel_id=1, source_target_pairs={{0,14},{2,0},{4,2},{6,4},{8,6},{10,8},{12,10},{14,12},{1,15},{3,1}... | collective-permute-start | bytes 2359304 | tf_op jit(solution)/shard_map/ppermute | solution.py:208
  31.2 3.4 %copy-start = (bf16[1,1,1024,4096]{3,2,1,0:T(8,128)(2,1)S(1)}, bf16[1,1,1024,4096]{3,2,1,0:T(8,128)(2,1)}, u32[]{:S(2)}) copy-start(bf16[1,1,1024,4096]{3,2,1,0:T(8,128)(2,1)} %param.6) | copy-start | bytes 25165828
  34.6 1.6 copy-start.2
  48.2 27.0 %collective-permute-start.11 = (f32[128,1536]{1,0:T(8,128)}, f32[128,1536]{1,0:T(8,128)}, u32[]{:S(2)}, u32[]{:S(2)}) collective-permute-start(f32[128,1536]{1,0:T(8,128)} %get-tuple-element.117), channel_id=1, source_target_pairs={{0,2},{2,4},{4,6},{6,8},{8,10},{10,12},{12,14},{14,0},{1,3},{3,5},... | collective-permute-start | bytes 2359304 | tf_op jit(solution)/shard_map/ppermute | solution.py:204
  48.2 27.0 %collective-permute-start.12 = (f32[128,1536]{1,0:T(8,128)}, f32[128,1536]{1,0:T(8,128)}, u32[]{:S(2)}, u32[]{:S(2)}) collective-permute-start(f32[128,1536]{1,0:T(8,128)} %get-tuple-element.116), channel_id=1, source_target_pairs={{0,14},{2,0},{4,2},{6,4},{8,6},{10,8},{12,10},{14,12},{1,15},{3,1}... | collective-permute-start | bytes 2359304 | tf_op jit(solution)/shard_map/ppermute | solution.py:208
  60.9 5.0 %collective-permute-start.9 = (f32[8,32,128]{2,1,0:T(8,128)S(1)}, f32[8,32,128]{2,1,0:T(8,128)S(1)}, u32[]{:S(2)}, u32[]{:S(2)}) collective-permute-start(f32[8,32,128]{2,1,0:T(8,128)S(1)} %partial_coeffs.1), channel_id=1, source_target_pairs={{0,16},{16,0},{1,17},{17,1},{2,18},{18,2},{3,19},{19,3},{4,20},{20... | collective-permute-start | bytes 393224 | tf_op jit(solution)/shard_map/ppermute | solution.py:200
  65.9 6.0 %collective-permute-start.10 = (f32[8,32,128]{2,1,0:T(8,128)S(1)}, f32[8,32,128]{2,1,0:T(8,128)S(1)}, u32[]{:S(2)}, u32[]{:S(2)}) collective-permute-start(f32[8,32,128]{2,1,0:T(8,128)S(1)} %add.377), channel_id=1, source_target_pairs={{0,64},{64,0},{128,192},{192,128},{1,65},{65,1},{129,193},{193,129... | collective-permute-start | bytes 393224 | tf_op jit(solution)/shard_map/ppermute | solution.py:200
  68.4 26.5 %collective-permute-start.15 = (f32[128,1792]{1,0:T(8,128)}, f32[128,1792]{1,0:T(8,128)}, u32[]{:S(2)}, u32[]{:S(2)}) collective-permute-start(f32[128,1792]{1,0:T(8,128)} %pad_maximum_fusion.2), channel_id=1, source_target_pairs={{0,2},{2,4},{4,6},{6,8},{8,10},{10,12},{12,14},{14,0},{1,3},{3,5},... | collective-permute-start | bytes 2752520 | tf_op jit(solution)/shard_map/ppermute | solution.py:204
  68.5 26.5 %collective-permute-start.16 = (f32[128,1792]{1,0:T(8,128)}, f32[128,1792]{1,0:T(8,128)}, u32[]{:S(2)}, u32[]{:S(2)}) collective-permute-start(f32[128,1792]{1,0:T(8,128)} %fusion), channel_id=1, source_target_pairs={{0,14},{2,0},{4,2},{6,4},{8,6},{10,8},{12,10},{14,12},{1,15},{3,1}... | collective-permute-start | bytes 2752520 | tf_op jit(solution)/shard_map/ppermute | solution.py:208
  75.3 6.5 %collective-permute-start.13 = (f32[8,32,128]{2,1,0:T(8,128)S(1)}, f32[8,32,128]{2,1,0:T(8,128)S(1)}, u32[]{:S(2)}, u32[]{:S(2)}) collective-permute-start(f32[8,32,128]{2,1,0:T(8,128)S(1)} %add.378), channel_id=1, source_target_pairs={{0,128},{64,192},{128,0},{192,64},{1,129},{65,193},{129,1},{193,65... | collective-permute-start | bytes 393224 | tf_op jit(solution)/shard_map/ppermute | solution.py:200
  81.8 11.8 %collective-permute-start.14 = (f32[4,32,128]{2,1,0:T(8,128)S(1)}, f32[4,32,128]{2,1,0:T(8,128)S(1)}, u32[]{:S(2)}, u32[]{:S(2)}) collective-permute-start(f32[4,32,128]{2,1,0:T(8,128)S(1)} %get-tuple-element.150), channel_id=1, source_target_pairs={{0,2},{2,0},{4,6},{6,4},{8,10},{10,8},{12,14},{14,12},{1,3},{3,1},... | collective-permute-start | bytes 196616 | tf_op jit(solution)/shard_map/ppermute | solution.py:200
  84.9 26.9 %collective-permute-start.18 = (f32[128,1536]{1,0:T(8,128)}, f32[128,1536]{1,0:T(8,128)}, u32[]{:S(2)}, u32[]{:S(2)}) collective-permute-start(f32[128,1536]{1,0:T(8,128)} %get-tuple-element.113), channel_id=1, source_target_pairs={{0,2},{2,4},{4,6},{6,8},{8,10},{10,12},{12,14},{14,0},{1,3},{3,5},... | collective-permute-start | bytes 2359304 | tf_op jit(solution)/shard_map/ppermute | solution.py:204
  86.9 24.9 %collective-permute-start.19 = (f32[128,1536]{1,0:T(8,128)}, f32[128,1536]{1,0:T(8,128)}, u32[]{:S(2)}, u32[]{:S(2)}) collective-permute-start(f32[128,1536]{1,0:T(8,128)} %get-tuple-element.112), channel_id=1, source_target_pairs={{0,14},{2,0},{4,2},{6,4},{8,6},{10,8},{12,10},{14,12},{1,15},{3,1}... | collective-permute-start | bytes 2359304 | tf_op jit(solution)/shard_map/ppermute | solution.py:208
  97.7 31.3 %copy-start.4 = (bf16[128,128]{1,0:T(8,128)(2,1)S(1)}, bf16[128,128]{1,0:T(8,128)(2,1)}, u32[]{:S(2)}) copy-start(bf16[128,128]{1,0:T(8,128)(2,1)} %constant.179.clone.refs_4_.refs_5_) | copy-start | bytes 98308
  99.8 5.0 %collective-permute-start.17 = (f32[4,32,128]{2,1,0:T(8,128)S(1)}, f32[4,32,128]{2,1,0:T(8,128)}, u32[]{:S(2)}, u32[]{:S(2)}) collective-permute-start(f32[4,32,128]{2,1,0:T(8,128)S(1)} %add.407), channel_id=1, source_target_pairs={{0,32},{32,0},{1,33},{33,1},{2,34},{34,2},{3,35},{35,3},{4,36},{36... | collective-permute-start | bytes 196616 | tf_op jit(solution)/shard_map/ppermute | solution.py:200
  101.5 32.3 %collective-permute-start.22 = (f32[128,2048]{1,0:T(8,128)S(1)}, f32[128,2048]{1,0:T(8,128)S(1)}, u32[]{:S(2)}, u32[]{:S(2)}) collective-permute-start(f32[128,2048]{1,0:T(8,128)S(1)} %pad_maximum_fusion), channel_id=1, source_target_pairs={{0,2},{2,4},{4,6},{6,8},{8,10},{10,12},{12,14},{14,0},{1,3},{3,5},... | collective-permute-start | bytes 3145736 | tf_op jit(solution)/shard_map/ppermute | solution.py:204
  101.5 32.3 %collective-permute-start.23 = (f32[128,2048]{1,0:T(8,128)}, f32[128,2048]{1,0:T(8,128)S(1)}, u32[]{:S(2)}, u32[]{:S(2)}) collective-permute-start(f32[128,2048]{1,0:T(8,128)} %pad_maximum_fusion.1), channel_id=1, source_target_pairs={{0,14},{2,0},{4,2},{6,4},{8,6},{10,8},{12,10},{14,12},{1,15},{3,1}... | collective-permute-start | bytes 3145736 | tf_op jit(solution)/shard_map/ppermute | solution.py:208
  113.4 38.3 %copy-start.8 = (f32[32]{0:T(128)S(1)}, f32[32]{0:T(128)}, u32[]{:S(2)}) copy-start(f32[32]{0:T(128)} %copy-done.7) | copy-start | bytes 388
  113.4 38.6 %copy-start.3 = (bf16[64,4096]{1,0:T(8,128)(2,1)S(1)}, bf16[64,4096]{1,0:T(8,128)(2,1)}, u32[]{:S(2)}) copy-start(bf16[64,4096]{1,0:T(8,128)(2,1)} %constant.177.clone.spread_ref) | copy-start | bytes 1572868
  113.5 40.4 %copy-start.5 = (f32[64,512]{1,0:T(8,128)S(1)}, f32[64,512]{1,0:T(8,128)}, u32[]{:S(2)}) copy-start(f32[64,512]{1,0:T(8,128)} %get-tuple-element.134) | copy-start | bytes 393220
  113.5 40.4 %copy-start.6 = (f32[64,512]{1,0:T(8,128)S(1)}, f32[64,512]{1,0:T(8,128)}, u32[]{:S(2)}) copy-start(f32[64,512]{1,0:T(8,128)} %get-tuple-element.135) | copy-start | bytes 393220
  113.5 12.5 %collective-permute-start.20 = (f32[64,1792]{1,0:T(8,128)S(1)}, f32[64,1792]{1,0:T(8,128)S(1)}, u32[]{:S(2)}, u32[]{:S(2)}) collective-permute-start(f32[64,1792]{1,0:T(8,128)S(1)} %pad_maximum_fusion.3), channel_id=1, source_target_pairs={{0,1},{1,0},{2,3},{3,2},{4,5},{5,4},{6,7},{7,6},{8,9},{9,8},{10,11... | collective-permute-start | bytes 1376264 | tf_op jit(solution)/shard_map/ppermute | solution.py:200
  126.0 7.8 %collective-permute-start.21 = (f32[4,32,128]{2,1,0:T(8,128)S(1)}, f32[4,32,128]{2,1,0:T(8,128)S(1)}, u32[]{:S(2)}, u32[]{:S(2)}) collective-permute-start(f32[4,32,128]{2,1,0:T(8,128)S(1)} %add.413), channel_id=1, source_target_pairs={{0,4},{2,6},{4,0},{6,2},{8,12},{10,14},{12,8},{14,10},{1,5},{3,7},... | collective-permute-start | bytes 196616 | tf_op jit(solution)/shard_map/ppermute | solution.py:200
  133.9 14.3 %collective-permute-start.25 = (f32[128,512]{1,0:T(8,128)S(1)}, f32[128,512]{1,0:T(8,128)S(1)}, u32[]{:S(2)}, u32[]{:S(2)}) collective-permute-start(f32[128,512]{1,0:T(8,128)S(1)} %maximum_add_fusion.2), channel_id=1, source_target_pairs={{0,2},{2,4},{4,6},{6,8},{8,10},{10,12},{12,14},{14,0},{1,3},{3,5},... | collective-permute-start | bytes 786440 | tf_op jit(solution)/shard_map/ppermute | solution.py:204
  138.5 9.7 %collective-permute-start.26 = (f32[128,512]{1,0:T(8,128)S(1)}, f32[128,512]{1,0:T(8,128)S(1)}, u32[]{:S(2)}, u32[]{:S(2)}) collective-permute-start(f32[128,512]{1,0:T(8,128)S(1)} %maximum_add_fusion.3), channel_id=1, source_target_pairs={{0,14},{2,0},{4,2},{6,4},{8,6},{10,8},{12,10},{14,12},{1,15},{3,1}... | collective-permute-start | bytes 786440 | tf_op jit(solution)/shard_map/ppermute | solution.py:208
  139.9 12.1 %collective-permute-start.27 = (f32[4,32,128]{2,1,0:T(8,128)S(1)}, f32[4,32,128]{2,1,0:T(8,128)S(1)}, u32[]{:S(2)}, u32[]{:S(2)}) collective-permute-start(f32[4,32,128]{2,1,0:T(8,128)S(1)} %add.427.coeffs_ref), channel_id=1, source_target_pairs={{0,8},{2,10},{4,12},{6,14},{8,0},{10,2},{12,4},{14,6},{1,9},{3,11}... | collective-permute-start | bytes 196616 | tf_op jit(solution)/shard_map/ppermute | solution.py:200
  144.9 9.7 %collective-permute-start.24 = (f32[64,1536]{1,0:T(8,128)S(1)}, f32[64,1536]{1,0:T(8,128)S(1)}, u32[]{:S(2)}, u32[]{:S(2)}) collective-permute-start(f32[64,1536]{1,0:T(8,128)S(1)} %get-tuple-element.124), channel_id=1, source_target_pairs={{0,1},{1,0},{2,3},{3,2},{4,5},{5,4},{6,7},{7,6},{8,9},{9,8},{10,11... | collective-permute-start | bytes 1179656 | tf_op jit(solution)/shard_map/ppermute | solution.py:200
  148.2 9.3 %collective-permute-start.29 = (f32[128,512]{1,0:T(8,128)S(1)}, f32[128,512]{1,0:T(8,128)S(1)}, u32[]{:S(2)}, u32[]{:S(2)}) collective-permute-start(f32[128,512]{1,0:T(8,128)S(1)} %maximum_add_fusion.4), channel_id=1, source_target_pairs={{0,2},{2,4},{4,6},{6,8},{8,10},{10,12},{12,14},{14,0},{1,3},{3,5},... | collective-permute-start | bytes 786440 | tf_op jit(solution)/shard_map/ppermute | solution.py:204
  148.6 8.9 %collective-permute-start.30 = (f32[128,512]{1,0:T(8,128)S(1)}, f32[128,512]{1,0:T(8,128)S(1)}, u32[]{:S(2)}, u32[]{:S(2)}) collective-permute-start(f32[128,512]{1,0:T(8,128)S(1)} %maximum_add_fusion.5), channel_id=1, source_target_pairs={{0,14},{2,0},{4,2},{6,4},{8,6},{10,8},{12,10},{14,12},{1,15},{3,1}... | collective-permute-start | bytes 786440 | tf_op jit(solution)/shard_map/ppermute | solution.py:208
  153.8 3.7 %collective-permute-start.28 = (f32[8,128]{1,0:T(8,128)S(1)}, f32[8,128]{1,0:T(8,128)S(1)}, u32[]{:S(2)}, u32[]{:S(2)}) collective-permute-start(f32[8,128]{1,0:T(8,128)S(1)} %get-tuple-element.91.squares_ref), channel_id=1, source_target_pairs={{0,2},{2,0},{4,6},{6,4},{8,10},{10,8},{12,14},{14,12},{1,3},{3,1},... | collective-permute-start | bytes 12296 | tf_op jit(solution)/shard_map/ppermute | solution.py:200

commit v3 on v2

--- a/solution.py
+++ b/solution.py
@@ -173,7 +173,7 @@
             gram_ref[...], coeffs, precision=HIGHEST, preferred_element_type=jnp.float32
         )
     squares_ref[...] = (total[:8] + total[8:16]) + (total[16:24] + total[24:])
-    row = where_ref[0] // 2
+    row = lax.div(where_ref[0], 4) * 2 + lax.rem(where_ref[0], 2)
     coeffs = (coeffs_ref[row] + more_ref[row]) * (1.0 / REPS)
     half = COLS // SPAN
     coeffs = jnp.where(where_ref[1] == 0, coeffs[:, :half], coeffs[:, half:])
@@ -344,10 +344,11 @@
     a.land(rest[:2])
     a = Flight(ring_a)
     coeffs = coeffs + flip(coeffs, "x", 4, 2)
-    pairs = coeffs.reshape(4, 2, BAND, 128)
-    keep = lax.dynamic_index_in_dim(pairs, z % 2, 1, keepdims=False)
-    other = lax.dynamic_index_in_dim(pairs, 1 - z % 2, 1, keepdims=False)
-    more = flip(other, "z", NZ, 1)
+    side = (z // 2) % 2
+    pairs = coeffs.reshape(2, 2, 2, BAND, 128)
+    keep = lax.dynamic_index_in_dim(pairs, side, 1, keepdims=False).reshape(4, BAND, 128)
+    other = lax.dynamic_index_in_dim(pairs, 1 - side, 1, keepdims=False).reshape(4, BAND, 128)
+    more = flip(other, "z", NZ, 2)
 
     keep, more, *rest = meet(keep, more, *b.got, *a.sent)
     b.land(rest[:2])
@@ -364,21 +365,22 @@
     got_a = flip(jnp.concatenate([give_a, flat[0], flat[1]], axis=1), "yh", 2, 1)
     got_a, more = got_a[:, :CHUNK], got_a[:, CHUNK:]
     coeffs = coeffs + jnp.stack([more[:, :128], more[:, 128:]]).reshape(4, BAND, 128)
-    more = flip(coeffs, "z", NZ, 2)
+    more = flip(coeffs, "z", NZ, 4)
     front = finish(None, mom, 0, CHUNK, [keep_a, after(got_a, coeffs)], first, pair, same)
 
-    coeffs, more, front, *rest = meet(coeffs, more, front, *b.got)
+    coeffs, front, *rest = meet(coeffs, front, *b.got)
     b.land(rest)
     y = Flight(ring_y)
-    coeffs = after(coeffs, *y.sent) + more
-    more = flip(coeffs, "z", NZ, 4)
-    keep_b, give_b, got_b = cross_y(after(sum(ring_b.parts()), coeffs))
-
-    y.land(meet(*y.got, give_b)[:2])
+    keep_b, give_b, got_b = cross_y(after(sum(ring_b.parts()), *y.sent))
+    coeffs = after(coeffs, give_b) + more
+    more = flip(coeffs, "z", NZ, 1)
+
+    coeffs, *rest = meet(coeffs, *y.got)
+    y.land(rest)
     y = Flight(ring_y)
 
     squares, average = average_of(where, after(coeffs, *y.sent), more, gram, first, second, spread)
-    more = flip(squares, "z", NZ, 1)
+    more = flip(squares, "z", NZ, 2)
     front = finish(front, mom, CHUNK, CHUNK, [keep_b, after(got_b, average)], first, pair, same)
 
     front, average, squares, more, *rest = meet(front, average, squares, more, *y.got)

time: 162 us -> 160 us (0.988)
  waiting for transfers between devices: 42.8 us -> 37.9 us
  starting transfers between devices: 60.4 us -> 63.1 us
    ppermute x10, starting transfers between devices: 7.35 us -> 10.8 us  [up(): return lax.ppermute(x, 'z', [(i, (i + 1) % NZ) for i in range(NZ)])]
    ppermute x10, waiting for transfers between devices: 20.3 us -> 16.8 us  [up(): return lax.ppermute(x, 'z', [(i, (i + 1) % NZ) for i in range(NZ)])]
    ppermute x10, starting transfers between devices: 29.1 us -> 26.5 us  [down(): return lax.ppermute(x, 'z', [(i, (i - 1) % NZ) for i in range(NZ)])]
    ppermute x11, waiting for transfers between devices: 22.5 us -> 20.1 us  [flip(): return lax.ppermute(x, axis, [(i, i ^ bit) for i in range(size)])]
    ppermute x11, starting transfers between devices: 24 us -> 25.8 us  [flip(): return lax.ppermute(x, axis, [(i, i ^ bit) for i in range(size)])]
    unnamed x22 -> x24, local copies, waits for them, and re-layouts: 5.02 us -> 5.02 us
  transfers between devices with their start and end apart: 31 -> 31, of which waited for: 14 -> 16; matrix products, arithmetic and copies ran while one was open for 20% -> 21% of each run, Pallas kernels for 9% -> 9%
where the time goes in v3:
time: 160 us; the launch traced here: 157 us
  starting transfers between devices  63.1 us (39%)
  waiting for transfers between devices  37.9 us (24%)
  other arithmetic  28 us (18%)
  Pallas kernels  15.9 us (10%)
  local copies, waits for them, and re-layouts  9.4 us (6%)
  matrix products  1.93 us (1%)
    ppermute x10, starting transfers between devices, down(): return lax.ppermute(x, 'z', [(i, (i - 1) % NZ) for i in range(NZ)])  26.5 us
    ppermute x11, starting transfers between devices, flip(): return lax.ppermute(x, axis, [(i, i ^ bit) for i in range(size)])  25.8 us
    ppermute x11, waiting for transfers between devices, flip(): return lax.ppermute(x, axis, [(i, i ^ bit) for i in range(size)])  20.1 us
    ppermute x10, waiting for transfers between devices, up(): return lax.ppermute(x, 'z', [(i, (i + 1) % NZ) for i in range(NZ)])  16.8 us
    add x12, other arithmetic, next(): terms = (self.block(self.step) + upward, self.block(-self.step) + downward)  14.2 us
    ppermute x10, starting transfers between devices, up(): return lax.ppermute(x, 'z', [(i, (i + 1) % NZ) for i in range(NZ)])  10.8 us
    pallas_call x1, Pallas kernels, partial_coeffs(): pl.pallas_call(partial_coeffs_kernel, out_shape=jax.ShapeDtypeStruct((NZ,...  9.25 us
    unnamed x24, local copies, waits for them, and re-layouts  5.02 us
  transfers between devices with their start and end apart: 31, of which 16 were waited for; matrix products, arithmetic and copies ran while one was open for 21% of the time, Pallas kernels for 9%

profile of v3, /device:TPU:0, one launch (start us, length us, event | category | flops | bytes accessed | tf_op | source)
XLA Modules:
  0.0 157.5 jit_solution(9601654746644785852)
XLA Ops:
  0.7 1.3 bitcast_convert_fusion.1
  2.3 4.0 %collective-permute-start.4 = (f32[128,768]{1,0:T(8,128)S(1)}, f32[128,768]{1,0:T(8,128)}, u32[]{:S(2)}, u32[]{:S(2)}) collective-permute-start(f32[128,768]{1,0:T(8,128)S(1)} %get-tuple-element.130), channel_id=1, source_target_pairs={{0,14},{2,0},{4,2},{6,4},{8,6},{10,8},{12,10},{14,12},{1,15},{3,1}... | collective-permute-start | bytes 1179656 | tf_op jit(solution)/shard_map/ppermute | solution.py:208
  6.5 3.2 %collective-permute-start.2 = (f32[128,768]{1,0:T(8,128)S(1)}, f32[128,768]{1,0:T(8,128)S(1)}, u32[]{:S(2)}, u32[]{:S(2)}) collective-permute-start(f32[128,768]{1,0:T(8,128)S(1)} %get-tuple-element.128), channel_id=1, source_target_pairs={{0,14},{2,0},{4,2},{6,4},{8,6},{10,8},{12,10},{14,12},{1,15},{3,1}... | collective-permute-start | bytes 1179656 | tf_op jit(solution)/shard_map/ppermute | solution.py:208
  9.7 2.8 %dynamic-slice_convert_fusion = f32[8,64,1024]{2,1,0:T(8,128)} fusion(bf16[8,128,4096]{2,1,0:T(8,128)(2,1)} %bitcast.108, s32[]{:T(128)S(6)} %select_n.131), kind=kLoop, calls=%fused_computation.3 | loop fusion | flops 524288 | bytes 3145732 | tf_op jit(solution)/shard_map/convert_element_type | solution.py:320
  12.5 3.2 %collective-permute-start = (f32[8,64,1024]{2,1,0:T(8,128)}, f32[8,64,1024]{2,1,0:T(8,128)}, u32[]{:S(2)}, u32[]{:S(2)}) collective-permute-start(f32[8,64,1024]{2,1,0:T(8,128)} %dynamic-slice_convert_fusion), channel_id=1, source_target_pairs={{0,1},{1,0},{2,3},{3,2},{4,5},{5,4},{6,7},{7,6},{8,9},{9,8},{10,11... | collective-permute-start | bytes 6291464 | tf_op jit(solution)/shard_map/ppermute | solution.py:200
  15.9 0.4 collective-permute-done.3
  16.3 2.7 %convert_add_fusion.11 = (f32[128,1536]{1,0:T(8,128)}, f32[128,1536]{1,0:T(8,128)}) fusion(f32[128,768]{1,0:T(8,128)} %collective-permute-done.4, bf16[1,1,1024,4096]{3,2,1,0:T(8,128)(2,1)} %param.6, s32[]{:T(128)S(6)} %select_n.133, f32[128,768]{1,0:T(8,128)} %collective-permute-done.3, s32[]{:T(128)S(6)} %select_n.132), kind=kLoop, calls=%fused_computation.21 | loop fusion | flops 786432 | bytes 3145736 | tf_op jit(solution)/shard_map/add | solution.py:248
  19.0 3.3 %collective-permute-start.6 = (f32[128,1536]{1,0:T(8,128)}, f32[128,1536]{1,0:T(8,128)}, u32[]{:S(2)}, u32[]{:S(2)}) collective-permute-start(f32[128,1536]{1,0:T(8,128)} %get-tuple-element.120), channel_id=1, source_target_pairs={{0,14},{2,0},{4,2},{6,4},{8,6},{10,8},{12,10},{14,12},{1,15},{3,1}... | collective-permute-start | bytes 2359304 | tf_op jit(solution)/shard_map/ppermute | solution.py:208
  22.3 2.3 %collective-permute-done.1 = f32[128,768]{1,0:T(8,128)S(1)} collective-permute-done((f32[128,768]{1,0:T(8,128)S(1)}, f32[128,768]{1,0:T(8,128)S(1)}, u32[]{:S(2)}, u32[]{:S(2)}) %collective-permute-start.1) | collective-permute-done | bytes 393248 | tf_op jit(solution)/shard_map/ppermute | solution.py:204
  24.6 2.5 %convert_add_fusion.10 = (f32[128,1536]{1,0:T(8,128)}, f32[128,1536]{1,0:T(8,128)}) fusion(f32[128,768]{1,0:T(8,128)S(1)} %collective-permute-done.2, bf16[1,1,1024,4096]{3,2,1,0:T(8,128)(2,1)} %param.6, s32[]{:T(128)S(6)} %select_n.133, f32[128,768]{1,0:T(8,128)S(1)} %collective-permute-done.1, s32[]{:T(128)S(6)} %select_n.132), kind=kLoop, calls=%fused_computation.20 | loop fusion | flops 786432 | bytes 3145736 | tf_op jit(solution)/shard_map/add | solution.py:248
  27.1 3.4 %collective-permute-start.8 = (f32[128,1536]{1,0:T(8,128)}, f32[128,1536]{1,0:T(8,128)}, u32[]{:S(2)}, u32[]{:S(2)}) collective-permute-start(f32[128,1536]{1,0:T(8,128)} %get-tuple-element.118), channel_id=1, source_target_pairs={{0,14},{2,0},{4,2},{6,4},{8,6},{10,8},{12,10},{14,12},{1,15},{3,1}... | collective-permute-start | bytes 2359304 | tf_op jit(solution)/shard_map/ppermute | solution.py:208
  30.7 0.4 tile.10.second_ref
  31.3 3.4 %copy-done = bf16[1,1,1024,4096]{3,2,1,0:T(8,128)(2,1)S(1)} copy-done((bf16[1,1,1024,4096]{3,2,1,0:T(8,128)(2,1)S(1)}, bf16[1,1,1024,4096]{3,2,1,0:T(8,128)(2,1)}, u32[]{:S(2)}) %copy-start) | copy-done | bytes 8388632
  34.6 1.6 %copy-done.2 = bf16[2,4096,128]{2,1,0:T(8,128)(2,1)S(1)} copy-done((bf16[2,4096,128]{2,1,0:T(8,128)(2,1)S(1)}, bf16[2,4096,128]{2,1,0:T(8,128)(2,1)}, u32[]{:S(2)}) %copy-start.2) | copy-done | bytes 2097176
  36.2 9.2 %partial_coeffs.1 = f32[8,32,128]{2,1,0:T(8,128)S(1)} custom-call(s32[2]{0:T(128)S(1)} %pad_add_fusion.where_ref, bf16[1024,4096]{1,0:T(8,128)(2,1)S(1)} %bitcast.109, f32[64,4096]{1,0:T(8,128)S(1)} %bitcast.110, f32[32,64]{1,0:T(8,128)S(1)} %get-tuple-element.155.first_ref.refs_2_.refs_3_, f32[32,4096]{1,0:T(8,128)S(1)} %tile.10.second_ref, ...), custom_call_target="tpu_custom_call" | custom-call | tf_op jit(solution)/shard_map/partial_coeffs/pallas_call | solution.py:75
  45.5 2.7 %convert_add_fusion.8 = (f32[128,1536]{1,0:T(8,128)}, f32[128,1536]{1,0:T(8,128)}) fusion(f32[128,1536]{1,0:T(8,128)} %collective-permute-done.6, bf16[1,1,1024,4096]{3,2,1,0:T(8,128)(2,1)S(1)} %copy-done, s32[]{:T(128)S(6)} %select_n.139, f32[128,1536]{1,0:T(8,128)} %collective-permute-done.5, s32[]{:T(128)S(6)} %select_n.138), kind=kLoop, calls=%fused_computation.18 | loop fusion | flops 786432 | bytes 3932168 | tf_op jit(solution)/shard_map/add | solution.py:248
  48.3 3.2 %collective-permute-start.12 = (f32[128,1536]{1,0:T(8,128)}, f32[128,1536]{1,0:T(8,128)}, u32[]{:S(2)}, u32[]{:S(2)}) collective-permute-start(f32[128,1536]{1,0:T(8,128)} %get-tuple-element.116), channel_id=1, source_target_pairs={{0,14},{2,0},{4,2},{6,4},{8,6},{10,8},{12,10},{14,12},{1,15},{3,1}... | collective-permute-start | bytes 2359304 | tf_op jit(solution)/shard_map/ppermute | solution.py:208
  51.5 6.8 %collective-permute-done.7 = f32[128,1536]{1,0:T(8,128)S(1)} collective-permute-done((f32[128,1536]{1,0:T(8,128)}, f32[128,1536]{1,0:T(8,128)S(1)}, u32[]{:S(2)}, u32[]{:S(2)}) %collective-permute-start.7) | collective-permute-done | bytes 786464 | tf_op jit(solution)/shard_map/ppermute | solution.py:204
  58.3 2.6 %collective-permute-done = f32[8,64,1024]{2,1,0:T(8,128)} collective-permute-done((f32[8,64,1024]{2,1,0:T(8,128)}, f32[8,64,1024]{2,1,0:T(8,128)}, u32[]{:S(2)}, u32[]{:S(2)}) %collective-permute-start) | collective-permute-done | bytes 2097184 | tf_op jit(solution)/shard_map/ppermute | solution.py:200
  60.9 1.3 convert_add_fusion.6
  62.2 2.5 %convert_add_fusion.14 = (f32[64,1024]{1,0:T(8,128)S(1)}, f32[64,1024]{1,0:T(8,128)S(1)}, f32[64,1024]{1,0:T(8,128)S(1)}, f32[64,1024]{1,0:T(8,128)S(1)}, f32[64...) fusion(f32[8,64,1024]{2,1,0:T(8,128)} %collective-permute-done, ...), kind=kLoop, calls=%fused_computation.36 | loop fusion | flops 1048576 | bytes 5242944 | tf_op jit(solution)/shard_map/add | solution.py:305
  64.8 1.0 fusion
  65.8 1.6 %collective-permute-start.10 = (f32[8,32,128]{2,1,0:T(8,128)S(1)}, f32[8,32,128]{2,1,0:T(8,128)S(1)}, u32[]{:S(2)}, u32[]{:S(2)}) collective-permute-start(f32[8,32,128]{2,1,0:T(8,128)S(1)} %add.377), channel_id=1, source_target_pairs={{0,64},{64,0},{128,192},{192,128},{1,65},{65,1},{129,193},{193,129... | collective-permute-start | bytes 393224 | tf_op jit(solution)/shard_map/ppermute | solution.py:200
  67.4 1.0 pad_maximum_fusion.2
  68.4 3.2 %collective-permute-start.16 = (f32[128,1792]{1,0:T(8,128)}, f32[128,1792]{1,0:T(8,128)}, u32[]{:S(2)}, u32[]{:S(2)}) collective-permute-start(f32[128,1792]{1,0:T(8,128)} %fusion), channel_id=1, source_target_pairs={{0,14},{2,0},{4,2},{6,4},{8,6},{10,8},{12,10},{14,12},{1,15},{3,1}... | collective-permute-start | bytes 2752520 | tf_op jit(solution)/shard_map/ppermute | solution.py:208
  71.8 3.4 %collective-permute-done.11 = f32[128,1536]{1,0:T(8,128)} collective-permute-done((f32[128,1536]{1,0:T(8,128)}, f32[128,1536]{1,0:T(8,128)}, u32[]{:S(2)}, u32[]{:S(2)}) %collective-permute-start.11) | collective-permute-done | bytes 786464 | tf_op jit(solution)/shard_map/ppermute | solution.py:204
  75.3 3.0 %collective-permute-start.13 = (f32[8,32,128]{2,1,0:T(8,128)S(1)}, f32[8,32,128]{2,1,0:T(8,128)S(1)}, u32[]{:S(2)}, u32[]{:S(2)}) collective-permute-start(f32[8,32,128]{2,1,0:T(8,128)S(1)} %add.378), channel_id=1, source_target_pairs={{0,128},{64,192},{128,0},{192,64},{1,129},{65,193},{129,1},{193,65... | collective-permute-start | bytes 393224 | tf_op jit(solution)/shard_map/ppermute | solution.py:200
  78.3 0.8 fusion.14
  79.0 2.7 %collective-permute-done.13 = f32[8,32,128]{2,1,0:T(8,128)S(1)} collective-permute-done((f32[8,32,128]{2,1,0:T(8,128)S(1)}, f32[8,32,128]{2,1,0:T(8,128)S(1)}, u32[]{:S(2)}, u32[]{:S(2)}) %collective-permute-start.13) | collective-permute-done | bytes 131104 | tf_op jit(solution)/shard_map/ppermute | solution.py:200
  81.8 3.1 %collective-permute-start.14 = (f32[4,32,128]{2,1,0:T(8,128)S(1)}, f32[4,32,128]{2,1,0:T(8,128)S(1)}, u32[]{:S(2)}, u32[]{:S(2)}) collective-permute-start(f32[4,32,128]{2,1,0:T(8,128)S(1)} %bitcast.120), channel_id=1, source_target_pairs={{0,4},{2,6},{4,0},{6,2},{8,12},{10,14},{12,8},{14,10},{1,5},{3,7},... | collective-permute-start | bytes 196616 | tf_op jit(solution)/shard_map/ppermute | solution.py:200
  84.9 3.0 %convert_add_fusion.4 = (f32[128,1536]{1,0:T(8,128)}, f32[128,1536]{1,0:T(8,128)}) fusion(f32[128,1536]{1,0:T(8,128)} %collective-permute-done.12, bf16[1,1,1024,4096]{3,2,1,0:T(8,128)(2,1)} %param.6, s32[]{:T(128)S(6)} %select_n.147, f32[128,1536]{1,0:T(8,128)} %collective-permute-done.11, s32[]{:T(128)S(6)} %select_n.146), kind=kLoop, calls=%fused_computation.14 | loop fusion | flops 786432 | bytes 3932168 | tf_op jit(solution)/shard_map/add | solution.py:248
  87.9 2.7 %collective-permute-start.18 = (f32[128,1536]{1,0:T(8,128)}, f32[128,1536]{1,0:T(8,128)}, u32[]{:S(2)}, u32[]{:S(2)}) collective-permute-start(f32[128,1536]{1,0:T(8,128)} %get-tuple-element.113), channel_id=1, source_target_pairs={{0,2},{2,4},{4,6},{6,8},{8,10},{10,12},{12,14},{14,0},{1,3},{3,5},... | collective-permute-start | bytes 2359304 | tf_op jit(solution)/shard_map/ppermute | solution.py:204
  90.6 0.5 collective-permute-start.19
  91.2 4.6 %collective-permute-done.14 = f32[4,32,128]{2,1,0:T(8,128)S(1)} collective-permute-done((f32[4,32,128]{2,1,0:T(8,128)S(1)}, f32[4,32,128]{2,1,0:T(8,128)S(1)}, u32[]{:S(2)}, u32[]{:S(2)}) %collective-permute-start.14) | collective-permute-done | bytes 65568 | tf_op jit(solution)/shard_map/ppermute | solution.py:200
  95.8 0.9 slice.125
  96.7 1.8 %convert_add_fusion.2 = (f32[128,1536]{1,0:T(8,128)S(1)}, f32[128,1536]{1,0:T(8,128)S(1)}) fusion(f32[128,1792]{1,0:T(8,128)} %collective-permute-done.16, bf16[1,1,1024,4096]{3,2,1,0:T(8,128)(2,1)} %param.6, s32[]{:T(128)S(6)} %select_n.147, f32[128,1792]{1,0:T(8,128)} %collective-permute-done.15, s32[]{:T(128)S(6)} %select_n.146), kind=kLoop, calls=%fused_computation.12 | loop fusion | flops 786432 | bytes 3932168 | tf_op jit(solution)/shard_map/add | solution.py:248
  98.5 0.9 slice.129
  99.6 1.0 pad_maximum_fusion.1
  100.6 1.7 %collective-permute-start.17 = (f32[4,32,128]{2,1,0:T(8,128)S(1)}, f32[4,32,128]{2,1,0:T(8,128)}, u32[]{:S(2)}, u32[]{:S(2)}) collective-permute-start(f32[4,32,128]{2,1,0:T(8,128)S(1)} %add.407), channel_id=1, source_target_pairs={{0,32},{32,0},{1,33},{33,1},{2,34},{34,2},{3,35},{35,3},{4,36},{36... | collective-permute-start | bytes 196616 | tf_op jit(solution)/shard_map/ppermute | solution.py:200
  102.3 1.6 %fusion.4 = f32[32,32]{1,0:T(8,128)} fusion(f32[32]{0:T(128)} %copy-done.9, f32[64]{0:T(128)S(1)} %add_multiply_fusion, pred[32]{0:T(512)(128)(4,1)S(1)} %get-tuple-element.100), kind=kOutput, calls=%fused_computation.56 | convolution fusion | flops 794624 | bytes 4512 | tf_op jit(solution)/shard_map/dot_general | solution.py:330
  103.9 3.5 %collective-permute-start.21 = (f32[128,2048]{1,0:T(8,128)S(1)}, f32[128,2048]{1,0:T(8,128)S(1)}, u32[]{:S(2)}, u32[]{:S(2)}) collective-permute-start(f32[128,2048]{1,0:T(8,128)S(1)} %pad_maximum_fusion), channel_id=1, source_target_pairs={{0,2},{2,4},{4,6},{6,8},{8,10},{10,12},{12,14},{14,0},{1,3},{3,5},... | collective-permute-start | bytes 3145736 | tf_op jit(solution)/shard_map/ppermute | solution.py:204
  107.5 0.9 collective-permute-start.22
  108.3 0.9 add.408
  109.2 2.6 %collective-permute-done.18 = f32[128,1536]{1,0:T(8,128)} collective-permute-done((f32[128,1536]{1,0:T(8,128)}, f32[128,1536]{1,0:T(8,128)}, u32[]{:S(2)}, u32[]{:S(2)}) %collective-permute-start.18) | collective-permute-done | bytes 786464 | tf_op jit(solution)/shard_map/ppermute | solution.py:204
  111.9 1.6 %fusion.2 = f32[128,1536]{1,0:T(8,128)S(1)} fusion(f32[128,1536]{1,0:T(8,128)} %collective-permute-done.19, f32[128,1536]{1,0:T(8,128)} %collective-permute-done.18, bf16[1,1,1024,4096]{3,2,1,0:T(8,128)(2,1)} %param.6, s32[]{:T(128)S(6)} %select_n.152), kind=kLoop, calls=%fused_computation.11 | loop fusion | flops 589824 | bytes 2752516 | tf_op jit(solution)/shard_map/add | solution.py:361
  113.6 3.3 %collective-permute-start.20 = (f32[64,1792]{1,0:T(8,128)S(1)}, f32[64,1792]{1,0:T(8,128)S(1)}, u32[]{:S(2)}, u32[]{:S(2)}) collective-permute-start(f32[64,1792]{1,0:T(8,128)S(1)} %pad_maximum_fusion.3), channel_id=1, source_target_pairs={{0,1},{1,0},{2,3},{3,2},{4,5},{5,4},{6,7},{7,6},{8,9},{9,8},{10,11... | collective-permute-start | bytes 1376264 | tf_op jit(solution)/shard_map/ppermute | solution.py:200
  116.9 1.0 fusion.17
  118.0 8.1 %collective-permute-done.20 = f32[64,1792]{1,0:T(8,128)S(1)} collective-permute-done((f32[64,1792]{1,0:T(8,128)S(1)}, f32[64,1792]{1,0:T(8,128)S(1)}, u32[]{:S(2)}, u32[]{:S(2)}) %collective-permute-start.20) | collective-permute-done | bytes 458784 | tf_op jit(solution)/shard_map/ppermute | solution.py:200
  126.1 4.7 %collective-permute-start.24 = (f32[4,32,128]{2,1,0:T(8,128)S(1)}, f32[4,32,128]{2,1,0:T(8,128)S(1)}, u32[]{:S(2)}, u32[]{:S(2)}) collective-permute-start(f32[4,32,128]{2,1,0:T(8,128)S(1)} %add.413), channel_id=1, source_target_pairs={{0,8},{2,10},{4,12},{6,14},{8,0},{10,2},{12,4},{14,6},{1,9},{3,11}... | collective-permute-start | bytes 196616 | tf_op jit(solution)/shard_map/ppermute | solution.py:200
  130.8 1.6 finish.2.refs_0_
  132.3 1.0 collective-permute-done.21
  133.5 2.9 %collective-permute-start.25 = (f32[128,512]{1,0:T(8,128)S(1)}, f32[128,512]{1,0:T(8,128)S(1)}, u32[]{:S(2)}, u32[]{:S(2)}) collective-permute-start(f32[128,512]{1,0:T(8,128)S(1)} %maximum_add_fusion.2), channel_id=1, source_target_pairs={{0,2},{2,4},{4,6},{6,8},{8,10},{10,12},{12,14},{14,0},{1,3},{3,5},... | collective-permute-start | bytes 786440 | tf_op jit(solution)/shard_map/ppermute | solution.py:204
  136.4 1.9 %collective-permute-start.26 = (f32[128,512]{1,0:T(8,128)S(1)}, f32[128,512]{1,0:T(8,128)S(1)}, u32[]{:S(2)}, u32[]{:S(2)}) collective-permute-start(f32[128,512]{1,0:T(8,128)S(1)} %maximum_add_fusion.3), channel_id=1, source_target_pairs={{0,14},{2,0},{4,2},{6,4},{8,6},{10,8},{12,10},{14,12},{1,15},{3,1}... | collective-permute-start | bytes 786440 | tf_op jit(solution)/shard_map/ppermute | solution.py:208
  138.3 1.1 fusion.1
  139.5 3.3 %collective-permute-start.23 = (f32[64,1536]{1,0:T(8,128)S(1)}, f32[64,1536]{1,0:T(8,128)S(1)}, u32[]{:S(2)}, u32[]{:S(2)}) collective-permute-start(f32[64,1536]{1,0:T(8,128)S(1)} %get-tuple-element.124), channel_id=1, source_target_pairs={{0,1},{1,0},{2,3},{3,2},{4,5},{5,4},{6,7},{7,6},{8,9},{9,8},{10,11... | collective-permute-start | bytes 1179656 | tf_op jit(solution)/shard_map/ppermute | solution.py:200
  142.8 0.9 collective-permute-start.27
  144.1 0.7 collective-permute-done.26
  144.8 1.3 collective-permute-start.29
  146.1 2.9 %collective-permute-start.30 = (f32[128,512]{1,0:T(8,128)S(1)}, f32[128,512]{1,0:T(8,128)S(1)}, u32[]{:S(2)}, u32[]{:S(2)}) collective-permute-start(f32[128,512]{1,0:T(8,128)S(1)} %maximum_add_fusion.5), channel_id=1, source_target_pairs={{0,14},{2,0},{4,2},{6,4},{8,6},{10,8},{12,10},{14,12},{1,15},{3,1}... | collective-permute-start | bytes 786440 | tf_op jit(solution)/shard_map/ppermute | solution.py:208
  149.4 1.8 %average.1 = (f32[8,128]{1,0:T(8,128)S(1)}, f32[64,4096]{1,0:T(8,128)S(1)}) custom-call(s32[2]{0:T(128)S(1)} %pad_add_fusion.where_ref, f32[4,32,128]{2,1,0:T(8,128)S(1)} %add.427.coeffs_ref, f32[4,32,128]{2,1,0:T(8,128)S(1)} %collective-permute-done.27.more_ref, f32[32,32]{1,0:T(8,128)S(1)} %convolution_multiply_fusion.gram_ref, ...), custom_call_target="tpu_custom_call" | custom-call | tf_op jit(solution)/shard_map/average/pallas_call | solution.py:189
  151.1 1.0 collective-permute-start.28
  152.2 1.6 finish.3.front_ref
  153.8 2.0 %collective-permute-done.28.more_ref = f32[8,128]{1,0:T(8,128)S(1)} collective-permute-done((f32[8,128]{1,0:T(8,128)S(1)}, f32[8,128]{1,0:T(8,128)S(1)}, u32[]{:S(2)}, u32[]{:S(2)}) %collective-permute-start.28) | collective-permute-done | bytes 4128 | tf_op jit(solution)/shard_map/ppermute | solution.py:200
  155.7 1.7 %last.1 = (f32[64,4096]{1,0:T(8,128)}, f32[64,4096]{1,0:T(8,128)}) custom-call(f32[64,4096]{1,0:T(8,128)} %finish.3.front_ref, f32[8,128]{1,0:T(8,128)S(1)} %get-tuple-element.91.squares_ref, f32[8,128]{1,0:T(8,128)S(1)} %collective-permute-done.28.more_ref, f32[64,4096]{1,0:T(8,128)S(1)} %get-tuple-element.93.average_ref, ...), custom_call_target="tpu_custom_call", output_to_operand_aliasing={{0}: (0, {})} | custom-call | tf_op jit(solution)/shard_map/last/pallas_call | solution.py:155
  (85 shorter events, 2.8 us)
Async XLA Ops:
  0.6 15.1 %copy-start.10 = (s32[32]{0:T(128)S(1)}, s32[32]{0:T(128)}, u32[]{:S(2)}) copy-start(s32[32]{0:T(128)} %param.8) | copy-start | bytes 388
  2.0 29.3 %copy-start.1 = (f32[1,64,4096]{2,1,0:T(8,128)S(1)}, f32[1,64,4096]{2,1,0:T(8,128)}, u32[]{:S(2)}) copy-start(f32[1,64,4096]{2,1,0:T(8,128)} %param.7) | copy-start | bytes 3145732
  2.0 14.2 %collective-permute-start.3 = (f32[128,768]{1,0:T(8,128)S(1)}, f32[128,768]{1,0:T(8,128)}, u32[]{:S(2)}, u32[]{:S(2)}) collective-permute-start(f32[128,768]{1,0:T(8,128)S(1)} %get-tuple-element.131), channel_id=1, source_target_pairs={{0,2},{2,4},{4,6},{6,8},{8,10},{10,12},{12,14},{14,0},{1,3},{3,5},... | collective-permute-start | bytes 1179656 | tf_op jit(solution)/shard_map/ppermute | solution.py:204
  2.3 14.0 %collective-permute-start.4 = (f32[128,768]{1,0:T(8,128)S(1)}, f32[128,768]{1,0:T(8,128)}, u32[]{:S(2)}, u32[]{:S(2)}) collective-permute-start(f32[128,768]{1,0:T(8,128)S(1)} %get-tuple-element.130), channel_id=1, source_target_pairs={{0,14},{2,0},{4,2},{6,4},{8,6},{10,8},{12,10},{14,12},{1,15},{3,1}... | collective-permute-start | bytes 1179656 | tf_op jit(solution)/shard_map/ppermute | solution.py:208
  6.4 18.2 %collective-permute-start.1 = (f32[128,768]{1,0:T(8,128)S(1)}, f32[128,768]{1,0:T(8,128)S(1)}, u32[]{:S(2)}, u32[]{:S(2)}) collective-permute-start(f32[128,768]{1,0:T(8,128)S(1)} %get-tuple-element.129), channel_id=1, source_target_pairs={{0,2},{2,4},{4,6},{6,8},{8,10},{10,12},{12,14},{14,0},{1,3},{3,5},... | collective-permute-start | bytes 1179656 | tf_op jit(solution)/shard_map/ppermute | solution.py:204
  6.5 18.1 %collective-permute-start.2 = (f32[128,768]{1,0:T(8,128)S(1)}, f32[128,768]{1,0:T(8,128)S(1)}, u32[]{:S(2)}, u32[]{:S(2)}) collective-permute-start(f32[128,768]{1,0:T(8,128)S(1)} %get-tuple-element.128), channel_id=1, source_target_pairs={{0,14},{2,0},{4,2},{6,4},{8,6},{10,8},{12,10},{14,12},{1,15},{3,1}... | collective-permute-start | bytes 1179656 | tf_op jit(solution)/shard_map/ppermute | solution.py:208
  12.5 48.3 %collective-permute-start = (f32[8,64,1024]{2,1,0:T(8,128)}, f32[8,64,1024]{2,1,0:T(8,128)}, u32[]{:S(2)}, u32[]{:S(2)}) collective-permute-start(f32[8,64,1024]{2,1,0:T(8,128)} %dynamic-slice_convert_fusion), channel_id=1, source_target_pairs={{0,1},{1,0},{2,3},{3,2},{4,5},{5,4},{6,7},{7,6},{8,9},{9,8},{10,11... | collective-permute-start | bytes 6291464 | tf_op jit(solution)/shard_map/ppermute | solution.py:200
  15.9 82.7 %copy-start.9 = (f32[32]{0:T(128)}, f32[32]{0:T(128)S(1)}, u32[]{:S(2)}) copy-start(f32[32]{0:T(128)S(1)} %convert_element_type.177) | copy-start | bytes 388
  19.0 26.5 %collective-permute-start.5 = (f32[128,1536]{1,0:T(8,128)}, f32[128,1536]{1,0:T(8,128)}, u32[]{:S(2)}, u32[]{:S(2)}) collective-permute-start(f32[128,1536]{1,0:T(8,128)} %get-tuple-element.121), channel_id=1, source_target_pairs={{0,2},{2,4},{4,6},{6,8},{8,10},{10,12},{12,14},{14,0},{1,3},{3,5},... | collective-permute-start | bytes 2359304 | tf_op jit(solution)/shard_map/ppermute | solution.py:204
  19.0 26.5 %collective-permute-start.6 = (f32[128,1536]{1,0:T(8,128)}, f32[128,1536]{1,0:T(8,128)}, u32[]{:S(2)}, u32[]{:S(2)}) collective-permute-start(f32[128,1536]{1,0:T(8,128)} %get-tuple-element.120), channel_id=1, source_target_pairs={{0,14},{2,0},{4,2},{6,4},{8,6},{10,8},{12,10},{14,12},{1,15},{3,1}... | collective-permute-start | bytes 2359304 | tf_op jit(solution)/shard_map/ppermute | solution.py:208
  22.3 23.2 %copy-start.7 = (f32[32]{0:T(128)}, f32[32]{0:T(128)S(1)}, u32[]{:S(2)}) copy-start(f32[32]{0:T(128)S(1)} %fusion.11) | copy-start | bytes 388
  27.1 31.2 %collective-permute-start.7 = (f32[128,1536]{1,0:T(8,128)}, f32[128,1536]{1,0:T(8,128)S(1)}, u32[]{:S(2)}, u32[]{:S(2)}) collective-permute-start(f32[128,1536]{1,0:T(8,128)} %get-tuple-element.119), channel_id=1, source_target_pairs={{0,2},{2,4},{4,6},{6,8},{8,10},{10,12},{12,14},{14,0},{1,3},{3,5},... | collective-permute-start | bytes 2359304 | tf_op jit(solution)/shard_map/ppermute | solution.py:204
  27.1 31.2 %collective-permute-start.8 = (f32[128,1536]{1,0:T(8,128)}, f32[128,1536]{1,0:T(8,128)}, u32[]{:S(2)}, u32[]{:S(2)}) collective-permute-start(f32[128,1536]{1,0:T(8,128)} %get-tuple-element.118), channel_id=1, source_target_pairs={{0,14},{2,0},{4,2},{6,4},{8,6},{10,8},{12,10},{14,12},{1,15},{3,1}... | collective-permute-start | bytes 2359304 | tf_op jit(solution)/shard_map/ppermute | solution.py:208
  31.3 3.4 %copy-start = (bf16[1,1,1024,4096]{3,2,1,0:T(8,128)(2,1)S(1)}, bf16[1,1,1024,4096]{3,2,1,0:T(8,128)(2,1)}, u32[]{:S(2)}) copy-start(bf16[1,1,1024,4096]{3,2,1,0:T(8,128)(2,1)} %param.6) | copy-start | bytes 25165828
  34.6 1.6 %copy-start.2 = (bf16[2,4096,128]{2,1,0:T(8,128)(2,1)S(1)}, bf16[2,4096,128]{2,1,0:T(8,128)(2,1)}, u32[]{:S(2)}) copy-start(bf16[2,4096,128]{2,1,0:T(8,128)(2,1)} %constant.186.clone.ones_ref) | copy-start | bytes 6291460
  48.3 27.0 %collective-permute-start.11 = (f32[128,1536]{1,0:T(8,128)}, f32[128,1536]{1,0:T(8,128)}, u32[]{:S(2)}, u32[]{:S(2)}) collective-permute-start(f32[128,1536]{1,0:T(8,128)} %get-tuple-element.117), channel_id=1, source_target_pairs={{0,2},{2,4},{4,6},{6,8},{8,10},{10,12},{12,14},{14,0},{1,3},{3,5},... | collective-permute-start | bytes 2359304 | tf_op jit(solution)/shard_map/ppermute | solution.py:204
  48.3 27.0 %collective-permute-start.12 = (f32[128,1536]{1,0:T(8,128)}, f32[128,1536]{1,0:T(8,128)}, u32[]{:S(2)}, u32[]{:S(2)}) collective-permute-start(f32[128,1536]{1,0:T(8,128)} %get-tuple-element.116), channel_id=1, source_target_pairs={{0,14},{2,0},{4,2},{6,4},{8,6},{10,8},{12,10},{14,12},{1,15},{3,1}... | collective-permute-start | bytes 2359304 | tf_op jit(solution)/shard_map/ppermute | solution.py:208
  60.9 4.9 %collective-permute-start.9 = (f32[8,32,128]{2,1,0:T(8,128)S(1)}, f32[8,32,128]{2,1,0:T(8,128)S(1)}, u32[]{:S(2)}, u32[]{:S(2)}) collective-permute-start(f32[8,32,128]{2,1,0:T(8,128)S(1)} %partial_coeffs.1), channel_id=1, source_target_pairs={{0,16},{16,0},{1,17},{17,1},{2,18},{18,2},{3,19},{19,3},{4,20},{20... | collective-permute-start | bytes 393224 | tf_op jit(solution)/shard_map/ppermute | solution.py:200
  65.8 6.0 %collective-permute-start.10 = (f32[8,32,128]{2,1,0:T(8,128)S(1)}, f32[8,32,128]{2,1,0:T(8,128)S(1)}, u32[]{:S(2)}, u32[]{:S(2)}) collective-permute-start(f32[8,32,128]{2,1,0:T(8,128)S(1)} %add.377), channel_id=1, source_target_pairs={{0,64},{64,0},{128,192},{192,128},{1,65},{65,1},{129,193},{193,129... | collective-permute-start | bytes 393224 | tf_op jit(solution)/shard_map/ppermute | solution.py:200
  68.4 27.4 %collective-permute-start.15 = (f32[128,1792]{1,0:T(8,128)}, f32[128,1792]{1,0:T(8,128)}, u32[]{:S(2)}, u32[]{:S(2)}) collective-permute-start(f32[128,1792]{1,0:T(8,128)} %pad_maximum_fusion.2), channel_id=1, source_target_pairs={{0,2},{2,4},{4,6},{6,8},{8,10},{10,12},{12,14},{14,0},{1,3},{3,5},... | collective-permute-start | bytes 2752520 | tf_op jit(solution)/shard_map/ppermute | solution.py:204
  68.4 27.3 %collective-permute-start.16 = (f32[128,1792]{1,0:T(8,128)}, f32[128,1792]{1,0:T(8,128)}, u32[]{:S(2)}, u32[]{:S(2)}) collective-permute-start(f32[128,1792]{1,0:T(8,128)} %fusion), channel_id=1, source_target_pairs={{0,14},{2,0},{4,2},{6,4},{8,6},{10,8},{12,10},{14,12},{1,15},{3,1}... | collective-permute-start | bytes 2752520 | tf_op jit(solution)/shard_map/ppermute | solution.py:208
  75.3 6.5 %collective-permute-start.13 = (f32[8,32,128]{2,1,0:T(8,128)S(1)}, f32[8,32,128]{2,1,0:T(8,128)S(1)}, u32[]{:S(2)}, u32[]{:S(2)}) collective-permute-start(f32[8,32,128]{2,1,0:T(8,128)S(1)} %add.378), channel_id=1, source_target_pairs={{0,128},{64,192},{128,0},{192,64},{1,129},{65,193},{129,1},{193,65... | collective-permute-start | bytes 393224 | tf_op jit(solution)/shard_map/ppermute | solution.py:200
  81.8 14.0 %collective-permute-start.14 = (f32[4,32,128]{2,1,0:T(8,128)S(1)}, f32[4,32,128]{2,1,0:T(8,128)S(1)}, u32[]{:S(2)}, u32[]{:S(2)}) collective-permute-start(f32[4,32,128]{2,1,0:T(8,128)S(1)} %bitcast.120), channel_id=1, source_target_pairs={{0,4},{2,6},{4,0},{6,2},{8,12},{10,14},{12,8},{14,10},{1,5},{3,7},... | collective-permute-start | bytes 196616 | tf_op jit(solution)/shard_map/ppermute | solution.py:200
  87.9 23.9 %collective-permute-start.18 = (f32[128,1536]{1,0:T(8,128)}, f32[128,1536]{1,0:T(8,128)}, u32[]{:S(2)}, u32[]{:S(2)}) collective-permute-start(f32[128,1536]{1,0:T(8,128)} %get-tuple-element.113), channel_id=1, source_target_pairs={{0,2},{2,4},{4,6},{6,8},{8,10},{10,12},{12,14},{14,0},{1,3},{3,5},... | collective-permute-start | bytes 2359304 | tf_op jit(solution)/shard_map/ppermute | solution.py:204
  90.6 21.2 %collective-permute-start.19 = (f32[128,1536]{1,0:T(8,128)}, f32[128,1536]{1,0:T(8,128)}, u32[]{:S(2)}, u32[]{:S(2)}) collective-permute-start(f32[128,1536]{1,0:T(8,128)} %get-tuple-element.112), channel_id=1, source_target_pairs={{0,14},{2,0},{4,2},{6,4},{8,6},{10,8},{12,10},{14,12},{1,15},{3,1}... | collective-permute-start | bytes 2359304 | tf_op jit(solution)/shard_map/ppermute | solution.py:208
  98.5 32.2 %copy-start.4 = (bf16[128,128]{1,0:T(8,128)(2,1)S(1)}, bf16[128,128]{1,0:T(8,128)(2,1)}, u32[]{:S(2)}) copy-start(bf16[128,128]{1,0:T(8,128)(2,1)} %constant.187.clone.refs_4_.refs_5_) | copy-start | bytes 98308
  100.6 7.7 %collective-permute-start.17 = (f32[4,32,128]{2,1,0:T(8,128)S(1)}, f32[4,32,128]{2,1,0:T(8,128)}, u32[]{:S(2)}, u32[]{:S(2)}) collective-permute-start(f32[4,32,128]{2,1,0:T(8,128)S(1)} %add.407), channel_id=1, source_target_pairs={{0,32},{32,0},{1,33},{33,1},{2,34},{34,2},{3,35},{35,3},{4,36},{36... | collective-permute-start | bytes 196616 | tf_op jit(solution)/shard_map/ppermute | solution.py:200
  103.9 29.4 %collective-permute-start.21 = (f32[128,2048]{1,0:T(8,128)S(1)}, f32[128,2048]{1,0:T(8,128)S(1)}, u32[]{:S(2)}, u32[]{:S(2)}) collective-permute-start(f32[128,2048]{1,0:T(8,128)S(1)} %pad_maximum_fusion), channel_id=1, source_target_pairs={{0,2},{2,4},{4,6},{6,8},{8,10},{10,12},{12,14},{14,0},{1,3},{3,5},... | collective-permute-start | bytes 3145736 | tf_op jit(solution)/shard_map/ppermute | solution.py:204
  107.5 26.0 %collective-permute-start.22 = (f32[128,2048]{1,0:T(8,128)}, f32[128,2048]{1,0:T(8,128)S(1)}, u32[]{:S(2)}, u32[]{:S(2)}) collective-permute-start(f32[128,2048]{1,0:T(8,128)} %pad_maximum_fusion.1), channel_id=1, source_target_pairs={{0,14},{2,0},{4,2},{6,4},{8,6},{10,8},{12,10},{14,12},{1,15},{3,1}... | collective-permute-start | bytes 3145736 | tf_op jit(solution)/shard_map/ppermute | solution.py:208
  113.5 35.5 %copy-start.8 = (f32[32]{0:T(128)S(1)}, f32[32]{0:T(128)}, u32[]{:S(2)}) copy-start(f32[32]{0:T(128)} %copy-done.7) | copy-start | bytes 388
  113.5 35.5 %copy-start.11 = (f32[32,32]{1,0:T(8,128)S(1)}, f32[32,32]{1,0:T(8,128)}, u32[]{:S(2)}) copy-start(f32[32,32]{1,0:T(8,128)} %fusion.4) | copy-start | bytes 12292
  113.5 35.9 %copy-start.3 = (bf16[64,4096]{1,0:T(8,128)(2,1)S(1)}, bf16[64,4096]{1,0:T(8,128)(2,1)}, u32[]{:S(2)}) copy-start(bf16[64,4096]{1,0:T(8,128)(2,1)} %constant.185.clone.spread_ref) | copy-start | bytes 1572868
  113.6 38.6 %copy-start.5 = (f32[64,512]{1,0:T(8,128)S(1)}, f32[64,512]{1,0:T(8,128)}, u32[]{:S(2)}) copy-start(f32[64,512]{1,0:T(8,128)} %get-tuple-element.134) | copy-start | bytes 393220
  113.6 38.6 %copy-start.6 = (f32[64,512]{1,0:T(8,128)S(1)}, f32[64,512]{1,0:T(8,128)}, u32[]{:S(2)}) copy-start(f32[64,512]{1,0:T(8,128)} %get-tuple-element.135) | copy-start | bytes 393220
  113.6 12.4 %collective-permute-start.20 = (f32[64,1792]{1,0:T(8,128)S(1)}, f32[64,1792]{1,0:T(8,128)S(1)}, u32[]{:S(2)}, u32[]{:S(2)}) collective-permute-start(f32[64,1792]{1,0:T(8,128)S(1)} %pad_maximum_fusion.3), channel_id=1, source_target_pairs={{0,1},{1,0},{2,3},{3,2},{4,5},{5,4},{6,7},{7,6},{8,9},{9,8},{10,11... | collective-permute-start | bytes 1376264 | tf_op jit(solution)/shard_map/ppermute | solution.py:200
  126.1 16.8 %collective-permute-start.24 = (f32[4,32,128]{2,1,0:T(8,128)S(1)}, f32[4,32,128]{2,1,0:T(8,128)S(1)}, u32[]{:S(2)}, u32[]{:S(2)}) collective-permute-start(f32[4,32,128]{2,1,0:T(8,128)S(1)} %add.413), channel_id=1, source_target_pairs={{0,8},{2,10},{4,12},{6,14},{8,0},{10,2},{12,4},{14,6},{1,9},{3,11}... | collective-permute-start | bytes 196616 | tf_op jit(solution)/shard_map/ppermute | solution.py:200
  133.5 10.6 %collective-permute-start.25 = (f32[128,512]{1,0:T(8,128)S(1)}, f32[128,512]{1,0:T(8,128)S(1)}, u32[]{:S(2)}, u32[]{:S(2)}) collective-permute-start(f32[128,512]{1,0:T(8,128)S(1)} %maximum_add_fusion.2), channel_id=1, source_target_pairs={{0,2},{2,4},{4,6},{6,8},{8,10},{10,12},{12,14},{14,0},{1,3},{3,5},... | collective-permute-start | bytes 786440 | tf_op jit(solution)/shard_map/ppermute | solution.py:204
  136.4 8.3 %collective-permute-start.26 = (f32[128,512]{1,0:T(8,128)S(1)}, f32[128,512]{1,0:T(8,128)S(1)}, u32[]{:S(2)}, u32[]{:S(2)}) collective-permute-start(f32[128,512]{1,0:T(8,128)S(1)} %maximum_add_fusion.3), channel_id=1, source_target_pairs={{0,14},{2,0},{4,2},{6,4},{8,6},{10,8},{12,10},{14,12},{1,15},{3,1}... | collective-permute-start | bytes 786440 | tf_op jit(solution)/shard_map/ppermute | solution.py:208
  139.5 12.7 %collective-permute-start.23 = (f32[64,1536]{1,0:T(8,128)S(1)}, f32[64,1536]{1,0:T(8,128)S(1)}, u32[]{:S(2)}, u32[]{:S(2)}) collective-permute-start(f32[64,1536]{1,0:T(8,128)S(1)} %get-tuple-element.124), channel_id=1, source_target_pairs={{0,1},{1,0},{2,3},{3,2},{4,5},{5,4},{6,7},{7,6},{8,9},{9,8},{10,11... | collective-permute-start | bytes 1179656 | tf_op jit(solution)/shard_map/ppermute | solution.py:200
  142.8 6.5 %collective-permute-start.27 = (f32[4,32,128]{2,1,0:T(8,128)S(1)}, f32[4,32,128]{2,1,0:T(8,128)S(1)}, u32[]{:S(2)}, u32[]{:S(2)}) collective-permute-start(f32[4,32,128]{2,1,0:T(8,128)S(1)} %add.427.coeffs_ref), channel_id=1, source_target_pairs={{0,2},{2,0},{4,6},{6,4},{8,10},{10,8},{12,14},{14,12},{1,3},{3,1},... | collective-permute-start | bytes 196616 | tf_op jit(solution)/shard_map/ppermute | solution.py:200
  144.8 10.9 %collective-permute-start.29 = (f32[128,512]{1,0:T(8,128)S(1)}, f32[128,512]{1,0:T(8,128)S(1)}, u32[]{:S(2)}, u32[]{:S(2)}) collective-permute-start(f32[128,512]{1,0:T(8,128)S(1)} %maximum_add_fusion.4), channel_id=1, source_target_pairs={{0,2},{2,4},{4,6},{6,8},{8,10},{10,12},{12,14},{14,0},{1,3},{3,5},... | collective-permute-start | bytes 786440 | tf_op jit(solution)/shard_map/ppermute | solution.py:204
  146.1 9.6 %collective-permute-start.30 = (f32[128,512]{1,0:T(8,128)S(1)}, f32[128,512]{1,0:T(8,128)S(1)}, u32[]{:S(2)}, u32[]{:S(2)}) collective-permute-start(f32[128,512]{1,0:T(8,128)S(1)} %maximum_add_fusion.5), channel_id=1, source_target_pairs={{0,14},{2,0},{4,2},{6,4},{8,6},{10,8},{12,10},{14,12},{1,15},{3,1}... | collective-permute-start | bytes 786440 | tf_op jit(solution)/shard_map/ppermute | solution.py:208
  151.1 4.6 %collective-permute-start.28 = (f32[8,128]{1,0:T(8,128)S(1)}, f32[8,128]{1,0:T(8,128)S(1)}, u32[]{:S(2)}, u32[]{:S(2)}) collective-permute-start(f32[8,128]{1,0:T(8,128)S(1)} %get-tuple-element.91.squares_ref), channel_id=1, source_target_pairs={{0,4},{2,6},{4,0},{6,2},{8,12},{10,14},{12,8},{14,10},{1,5},{3,7},... | collective-permute-start | bytes 12296 | tf_op jit(solution)/shard_map/ppermute | solution.py:200

commit v4 on v3

--- a/solution.py
+++ b/solution.py
@@ -299,13 +299,21 @@
 
         return block
 
+    def y_rows(rows, k, half):
+        return lax.dynamic_slice(rows, ((owner(k) * 2 + half) * SPAN, Y_AT), (SPAN, Y_COLS)).astype(jnp.float32)
+
+    def y_give(rows, places):
+        return jnp.concatenate([y_rows(rows, k, 1 - yh) for k in places], axis=0)
+
     def y_block(got):
         def block(k):
-            rows = lax.dynamic_slice(grad, ((owner(k) * 2 + yh) * SPAN, Y_AT), (SPAN, Y_COLS))
-            term = lax.dynamic_index_in_dim(got, owner(k), 0, keepdims=False) + rows.astype(jnp.float32)
+            term = got[k] + y_rows(grad, k, yh)
             return jnp.concatenate([term[:, : Y_COLS // 2], term[:, Y_COLS // 2 :]], axis=0)
 
         return block
+
+    def by_place(places, rows):
+        return {k: rows[i * SPAN : (i + 1) * SPAN] for i, k in enumerate(places)}
 
     def cross_y(total):
         give = lax.dynamic_slice(total, ((1 - yh) * SPAN, 0), (SPAN, CHUNK))
@@ -316,9 +324,9 @@
     a = Flight(ring_a)
     ring_b.first = meet(ring_b.first, *a.sent)[0]
     b = Flight(ring_b)
-    rows = after(grad, *b.sent).reshape(NZ, 2 * SPAN, COLS)
-    give = lax.dynamic_slice(rows, (0, (1 - yh) * SPAN, Y_AT), (NZ, SPAN, Y_COLS)).astype(jnp.float32)
-    got = flip(give, "yh", 2, 1)
+    far, near = (4, 3, -3, 2, -2), (1, -1, 0)
+    give = y_give(after(grad, *b.sent), far)
+    got_far = flip(give, "yh", 2, 1)
 
     a.land(meet(*a.got, give)[:2])
     a = Flight(ring_a)
@@ -329,32 +337,36 @@
     pair = second[:, :128]
     gram = jnp.dot(first, first.T, precision=HIGHEST) * jnp.dot(second_table, second_table.T, precision=HIGHEST)
 
-    coeffs, pair, *rest = meet(coeffs, pair, *a.got)
+    got_far, coeffs, pair, *rest = meet(got_far, coeffs, pair, *a.got)
     a.land(rest)
-    a = Flight(ring_a)
-
-    got, coeffs, *rest = meet(got, coeffs, *b.got, *a.sent)
+    got = by_place(far, got_far)
+    ring_y = Ring(y_block(got), Y_COLS // 2)
+    a = Flight(ring_a, ring_y)
+    got_near = flip(y_give(after(grad, *a.sent), near), "yh", 2, 1)
+
+    coeffs, *rest = meet(coeffs, *b.got, *a.sent)
     b.land(rest[:2])
-    ring_y = Ring(y_block(got), Y_COLS // 2)
-    b = Flight(ring_b, ring_y)
+    b = Flight(ring_b)
+    coeffs, got_near = meet(coeffs, got_near, *b.sent)[:2]
+    got.update(by_place(near, got_near))
     for axis, size, bit in (("c", 2, 1), ("x", 4, 1)):
         coeffs = coeffs + flip(coeffs, axis, size, bit)
 
     coeffs, *rest = meet(coeffs, *a.got, *b.sent)
-    a.land(rest[:2])
-    a = Flight(ring_a)
-    coeffs = coeffs + flip(coeffs, "x", 4, 2)
     side = (z // 2) % 2
     pairs = coeffs.reshape(2, 2, 2, BAND, 128)
     keep = lax.dynamic_index_in_dim(pairs, side, 1, keepdims=False).reshape(4, BAND, 128)
     other = lax.dynamic_index_in_dim(pairs, 1 - side, 1, keepdims=False).reshape(4, BAND, 128)
     more = flip(other, "z", NZ, 2)
+    a.land(meet(*rest[:2], other)[:2])
+    a = Flight(ring_a, ring_y)
 
     keep, more, *rest = meet(keep, more, *b.got, *a.sent)
     b.land(rest[:2])
-    b = Flight(ring_b, ring_y)
+    b = Flight(ring_b)
     coeffs = after(keep, *b.sent) + more
-    coeffs = coeffs + flip(coeffs, "yl", 2, 1)
+    for axis, size, bit in (("x", 4, 2), ("yl", 2, 1)):
+        coeffs = coeffs + flip(coeffs, axis, size, bit)
 
     coeffs, *rest = meet(coeffs, *a.got)
     a.land(rest)
@@ -363,6 +375,7 @@
     give_a = lax.dynamic_slice(total, ((1 - yh) * SPAN, 0), (SPAN, CHUNK))
     flat = coeffs.reshape(2, SPAN, 128)
     got_a = flip(jnp.concatenate([give_a, flat[0], flat[1]], axis=1), "yh", 2, 1)
+    y = Flight(ring_y)
     got_a, more = got_a[:, :CHUNK], got_a[:, CHUNK:]
     coeffs = coeffs + jnp.stack([more[:, :128], more[:, 128:]]).reshape(4, BAND, 128)
     more = flip(coeffs, "z", NZ, 4)
@@ -370,8 +383,7 @@
 
     coeffs, front, *rest = meet(coeffs, front, *b.got)
     b.land(rest)
-    y = Flight(ring_y)
-    keep_b, give_b, got_b = cross_y(after(sum(ring_b.parts()), *y.sent))
+    keep_b, give_b, got_b = cross_y(sum(ring_b.parts()))
     coeffs = after(coeffs, give_b) + more
     more = flip(coeffs, "z", NZ, 1)
 

time: 160 us -> 163 us (1.019)
  waiting for transfers between devices: 37.9 us -> 58.7 us
  starting transfers between devices: 63.1 us -> 49.7 us
  other arithmetic: 28 us -> 22.7 us
  local copies, waits for them, and re-layouts: 9.4 us -> 12.2 us
    ppermute x11 -> x12, waiting for transfers between devices: 20.1 us -> 34.6 us  [flip(): return lax.ppermute(x, axis, [(i, i ^ bit) for i in range(size)])]
    ppermute x10, waiting for transfers between devices: 0.94 us -> 10.9 us  [down(): return lax.ppermute(x, 'z', [(i, (i - 1) % NZ) for i in range(NZ)])]
    ppermute x11 -> x12, starting transfers between devices: 25.8 us -> 17.4 us  [flip(): return lax.ppermute(x, axis, [(i, i ^ bit) for i in range(size)])]
    ppermute x10, starting transfers between devices: 10.8 us -> 5.45 us  [up(): return lax.ppermute(x, 'z', [(i, (i + 1) % NZ) for i in range(NZ)])]
    unnamed x24 -> x18, local copies, waits for them, and re-layouts: 5.02 us -> 9.53 us
    ppermute x10, waiting for transfers between devices: 16.8 us -> 13.2 us  [up(): return lax.ppermute(x, 'z', [(i, (i + 1) % NZ) for i in range(NZ)])]
    convert_element_type x1 -> x0, other arithmetic: 2.83 us -> none  [per_device(): lax.dynamic_slice(rows, (0, (1 - yh) * SPAN, Y_AT), (NZ, SPAN, Y_COLS))]
    add x12, other arithmetic: 14.2 us -> 11.4 us  [next(): terms = (self.block(self.step) + upward, self.block(-self.step) + downward)]
  transfers between devices with their start and end apart: 31 -> 32, of which waited for: 16 -> 14; matrix products, arithmetic and copies ran while one was open for 21% -> 18% of each run, Pallas kernels for 9% -> 9%
where the time goes in v4:
time: 163 us; the launch traced here: 161 us
  waiting for transfers between devices  58.7 us (36%)
  starting transfers between devices  49.7 us (30%)
  other arithmetic  22.7 us (14%)
  Pallas kernels  15.9 us (10%)
  local copies, waits for them, and re-layouts  12.2 us (7%)
    ppermute x12, waiting for transfers between devices, flip(): return lax.ppermute(x, axis, [(i, i ^ bit) for i in range(size)])  34.6 us
    ppermute x10, starting transfers between devices, down(): return lax.ppermute(x, 'z', [(i, (i - 1) % NZ) for i in range(NZ)])  26.8 us
    ppermute x12, starting transfers between devices, flip(): return lax.ppermute(x, axis, [(i, i ^ bit) for i in range(size)])  17.4 us
    ppermute x10, waiting for transfers between devices, up(): return lax.ppermute(x, 'z', [(i, (i + 1) % NZ) for i in range(NZ)])  13.2 us
    add x12, other arithmetic, next(): terms = (self.block(self.step) + upward, self.block(-self.step) + downward)  11.4 us
    ppermute x10, waiting for transfers between devices, down(): return lax.ppermute(x, 'z', [(i, (i - 1) % NZ) for i in range(NZ)])  10.9 us
    unnamed x18, local copies, waits for them, and re-layouts  9.53 us
    pallas_call x1, Pallas kernels, partial_coeffs(): pl.pallas_call(partial_coeffs_kernel, out_shape=jax.ShapeDtypeStruct((NZ,...  9.24 us
  transfers between devices with their start and end apart: 32, of which 14 were waited for; matrix products, arithmetic and copies ran while one was open for 18% of the time, Pallas kernels for 9%

profile of v4, /device:TPU:0, one launch (start us, length us, event | category | flops | bytes accessed | tf_op | source)
XLA Modules:
  0.0 161.2 jit_solution(1946296088145029842)
XLA Ops:
  0.7 1.3 bitcast_convert_fusion.1
  2.3 4.0 %collective-permute-start.4 = (f32[128,768]{1,0:T(8,128)S(1)}, f32[128,768]{1,0:T(8,128)S(1)}, u32[]{:S(2)}, u32[]{:S(2)}) collective-permute-start(f32[128,768]{1,0:T(8,128)S(1)} %get-tuple-element.141), channel_id=1, source_target_pairs={{0,14},{2,0},{4,2},{6,4},{8,6},{10,8},{12,10},{14,12},{1,15},{3,1}... | collective-permute-start | bytes 1179656 | tf_op jit(solution)/shard_map/ppermute | solution.py:208
  6.3 0.9 fusion.12
  7.3 3.2 %collective-permute-start.2 = (f32[128,768]{1,0:T(8,128)}, f32[128,768]{1,0:T(8,128)}, u32[]{:S(2)}, u32[]{:S(2)}) collective-permute-start(f32[128,768]{1,0:T(8,128)} %get-tuple-element.139), channel_id=1, source_target_pairs={{0,14},{2,0},{4,2},{6,4},{8,6},{10,8},{12,10},{14,12},{1,15},{3,1}... | collective-permute-start | bytes 1179656 | tf_op jit(solution)/shard_map/ppermute | solution.py:208
  10.5 0.9 dynamic-slice_dynamic-update-slice_fusion.4
  11.4 0.9 dynamic-slice_dynamic-update-slice_fusion.3
  12.3 0.9 dynamic-slice_dynamic-update-slice_fusion.2
  13.3 0.9 dynamic-slice_dynamic-update-slice_fusion.1
  14.2 0.9 dynamic-slice_dynamic-update-slice_fusion
  15.1 1.2 concatenate.70
  16.4 3.2 %collective-permute-start = (f32[320,1024]{1,0:T(8,128)}, f32[320,1024]{1,0:T(8,128)}, u32[]{:S(2)}, u32[]{:S(2)}) collective-permute-start(f32[320,1024]{1,0:T(8,128)} %concatenate.70), channel_id=1, source_target_pairs={{0,1},{1,0},{2,3},{3,2},{4,5},{5,4},{6,7},{7,6},{8,9},{9,8},{10,11... | collective-permute-start | bytes 3932168 | tf_op jit(solution)/shard_map/ppermute | solution.py:200
  19.6 2.4 %convert_add_fusion.11 = (f32[128,1536]{1,0:T(8,128)}, f32[128,1536]{1,0:T(8,128)}) fusion(f32[128,768]{1,0:T(8,128)S(1)} %collective-permute-done.4, bf16[1,1,1024,4096]{3,2,1,0:T(8,128)(2,1)} %param.6, s32[]{:T(128)S(6)} %select_n.135, f32[128,768]{1,0:T(8,128)S(1)} %collective-permute-done.3, s32[]{:T(128)S(6)} %select_n.134), kind=kLoop, calls=%fused_computation.20 | loop fusion | flops 786432 | bytes 3145736 | tf_op jit(solution)/shard_map/add | solution.py:248
  22.1 3.2 %collective-permute-start.6 = (f32[128,1536]{1,0:T(8,128)}, f32[128,1536]{1,0:T(8,128)}, u32[]{:S(2)}, u32[]{:S(2)}) collective-permute-start(f32[128,1536]{1,0:T(8,128)} %get-tuple-element.131), channel_id=1, source_target_pairs={{0,14},{2,0},{4,2},{6,4},{8,6},{10,8},{12,10},{14,12},{1,15},{3,1}... | collective-permute-start | bytes 2359304 | tf_op jit(solution)/shard_map/ppermute | solution.py:208
  25.7 0.4 tile.10.second_ref
  26.2 2.7 %convert_add_fusion.10 = (f32[128,1536]{1,0:T(8,128)}, f32[128,1536]{1,0:T(8,128)}) fusion(f32[128,768]{1,0:T(8,128)} %collective-permute-done.2, bf16[1,1,1024,4096]{3,2,1,0:T(8,128)(2,1)} %param.6, s32[]{:T(128)S(6)} %select_n.135, f32[128,768]{1,0:T(8,128)} %collective-permute-done.1, s32[]{:T(128)S(6)} %select_n.134), kind=kLoop, calls=%fused_computation.19 | loop fusion | flops 786432 | bytes 3145736 | tf_op jit(solution)/shard_map/add | solution.py:248
  28.9 3.2 %collective-permute-start.8 = (f32[128,1536]{1,0:T(8,128)}, f32[128,1536]{1,0:T(8,128)}, u32[]{:S(2)}, u32[]{:S(2)}) collective-permute-start(f32[128,1536]{1,0:T(8,128)} %get-tuple-element.129), channel_id=1, source_target_pairs={{0,14},{2,0},{4,2},{6,4},{8,6},{10,8},{12,10},{14,12},{1,15},{3,1}... | collective-permute-start | bytes 2359304 | tf_op jit(solution)/shard_map/ppermute | solution.py:208
  32.2 3.4 %copy-done = bf16[1,1,1024,4096]{3,2,1,0:T(8,128)(2,1)S(1)} copy-done((bf16[1,1,1024,4096]{3,2,1,0:T(8,128)(2,1)S(1)}, bf16[1,1,1024,4096]{3,2,1,0:T(8,128)(2,1)}, u32[]{:S(2)}) %copy-start) | copy-done | bytes 8388632
  35.5 1.6 copy-done.2
  37.1 9.2 %partial_coeffs.1 = f32[8,32,128]{2,1,0:T(8,128)S(1)} custom-call(s32[2]{0:T(128)S(1)} %pad_add_fusion.where_ref, bf16[1024,4096]{1,0:T(8,128)(2,1)S(1)} %bitcast.96, f32[64,4096]{1,0:T(8,128)S(1)} %bitcast.98, f32[32,64]{1,0:T(8,128)S(1)} %get-tuple-element.166.first_ref.refs_2_.refs_3_, f32[32,4096]{1,0:T(8,128)S(1)} %tile.10.second_ref, ...), custom_call_target="tpu_custom_call" | custom-call | tf_op jit(solution)/shard_map/partial_coeffs/pallas_call | solution.py:75
  46.4 0.9 copy-done.5
  47.3 0.6 collective-permute-done
  47.9 1.4 convert_add_fusion.17
  49.3 1.6 convert_add_fusion.8
  50.9 1.0 fusion
  51.9 1.0 pad_maximum_fusion.2
  52.9 1.0 maximum_convert_fusion
  53.9 3.2 %collective-permute-start.9 = (f32[192,1024]{1,0:T(8,128)}, f32[192,1024]{1,0:T(8,128)}, u32[]{:S(2)}, u32[]{:S(2)}) collective-permute-start(f32[192,1024]{1,0:T(8,128)} %maximum_convert_fusion), channel_id=1, source_target_pairs={{0,1},{1,0},{2,3},{3,2},{4,5},{5,4},{6,7},{7,6},{8,9},{9,8},{10,11... | collective-permute-start | bytes 2359304 | tf_op jit(solution)/shard_map/ppermute | solution.py:200
  57.8 0.7 collective-permute-start.13
  58.5 1.6 collective-permute-start.12
  60.1 1.8 %convert_add_fusion.6 = (f32[128,1536]{1,0:T(8,128)S(1)}, f32[128,1536]{1,0:T(8,128)S(1)}) fusion(f32[128,1536]{1,0:T(8,128)} %collective-permute-done.8, bf16[1,1,1024,4096]{3,2,1,0:T(8,128)(2,1)} %param.6, s32[]{:T(128)S(6)} %select_n.142, f32[128,1536]{1,0:T(8,128)} %collective-permute-done.7, s32[]{:T(128)S(6)} %select_n.140), kind=kLoop, calls=%fused_computation.15 | loop fusion | flops 786432 | bytes 3932168 | tf_op jit(solution)/shard_map/add | solution.py:248
  62.0 3.2 %collective-permute-start.16 = (f32[128,1536]{1,0:T(8,128)S(1)}, f32[128,1536]{1,0:T(8,128)S(1)}, u32[]{:S(2)}, u32[]{:S(2)}) collective-permute-start(f32[128,1536]{1,0:T(8,128)S(1)} %get-tuple-element.122), channel_id=1, source_target_pairs={{0,14},{2,0},{4,2},{6,4},{8,6},{10,8},{12,10},{14,12},{1,15},{3,1}... | collective-permute-start | bytes 2359304 | tf_op jit(solution)/shard_map/ppermute | solution.py:208
  65.2 8.1 %collective-permute-done.9 = f32[192,1024]{1,0:T(8,128)} collective-permute-done((f32[192,1024]{1,0:T(8,128)}, f32[192,1024]{1,0:T(8,128)}, u32[]{:S(2)}, u32[]{:S(2)}) %collective-permute-start.9) | collective-permute-done | bytes 786464 | tf_op jit(solution)/shard_map/ppermute | solution.py:200
  73.3 1.3 collective-permute-done.10
  74.6 1.6 collective-permute-start.11
  76.3 4.0 %collective-permute-done.11 = f32[8,32,128]{2,1,0:T(8,128)S(1)} collective-permute-done((f32[8,32,128]{2,1,0:T(8,128)S(1)}, f32[8,32,128]{2,1,0:T(8,128)S(1)}, u32[]{:S(2)}, u32[]{:S(2)}) %collective-permute-start.11) | collective-permute-done | bytes 131104 | tf_op jit(solution)/shard_map/ppermute | solution.py:200
  80.3 1.2 collective-permute-done.13
  81.5 1.7 %collective-permute-done.12 = f32[128,1792]{1,0:T(8,128)S(1)} collective-permute-done((f32[128,1792]{1,0:T(8,128)}, f32[128,1792]{1,0:T(8,128)S(1)}, u32[]{:S(2)}, u32[]{:S(2)}) %collective-permute-start.12) | collective-permute-done | bytes 917536 | tf_op jit(solution)/shard_map/ppermute | solution.py:204
  83.3 1.3 convert_add_fusion.4
  84.8 3.7 %collective-permute-start.20 = (f32[128,2048]{1,0:T(8,128)S(1)}, f32[128,2048]{1,0:T(8,128)S(1)}, u32[]{:S(2)}, u32[]{:S(2)}) collective-permute-start(f32[128,2048]{1,0:T(8,128)S(1)} %pad_maximum_fusion.1), channel_id=1, source_target_pairs={{0,14},{2,0},{4,2},{6,4},{8,6},{10,8},{12,10},{14,12},{1,15},{3,1}... | collective-permute-start | bytes 3145736 | tf_op jit(solution)/shard_map/ppermute | solution.py:208
  88.7 11.3 %collective-permute-done.15 = f32[128,1536]{1,0:T(8,128)S(1)} collective-permute-done((f32[128,1536]{1,0:T(8,128)S(1)}, f32[128,1536]{1,0:T(8,128)S(1)}, u32[]{:S(2)}, u32[]{:S(2)}) %collective-permute-start.15) | collective-permute-done | bytes 786464 | tf_op jit(solution)/shard_map/ppermute | solution.py:204
  100.1 1.3 convert_add_fusion.2
  101.4 3.1 %collective-permute-start.17 = (f32[4,32,128]{2,1,0:T(8,128)S(1)}, f32[4,32,128]{2,1,0:T(8,128)S(1)}, u32[]{:S(2)}, u32[]{:S(2)}) collective-permute-start(f32[4,32,128]{2,1,0:T(8,128)S(1)} %add.441), channel_id=1, source_target_pairs={{0,128},{64,192},{128,0},{192,64},{1,129},{65,193},{129,1},{193,65... | collective-permute-start | bytes 196616 | tf_op jit(solution)/shard_map/ppermute | solution.py:200
  104.5 1.3 convert_add_fusion.14
  105.9 1.4 collective-permute-done.17
  107.3 0.8 collective-permute-start.18
  108.1 0.4 collective-permute-start.22
  108.5 4.1 %collective-permute-start.23 = (f32[128,1536]{1,0:T(8,128)S(1)}, f32[128,1536]{1,0:T(8,128)S(1)}, u32[]{:S(2)}, u32[]{:S(2)}) collective-permute-start(f32[128,1536]{1,0:T(8,128)S(1)} %get-tuple-element.118), channel_id=1, source_target_pairs={{0,14},{2,0},{4,2},{6,4},{8,6},{10,8},{12,10},{14,12},{1,15},{3,1}... | collective-permute-start | bytes 2359304 | tf_op jit(solution)/shard_map/ppermute | solution.py:208
  112.7 9.6 %collective-permute-done.20 = f32[128,2048]{1,0:T(8,128)S(1)} collective-permute-done((f32[128,2048]{1,0:T(8,128)S(1)}, f32[128,2048]{1,0:T(8,128)S(1)}, u32[]{:S(2)}, u32[]{:S(2)}) %collective-permute-start.20) | collective-permute-done | bytes 1048608 | tf_op jit(solution)/shard_map/ppermute | solution.py:208
  122.5 1.2 fusion.2
  123.9 0.4 collective-permute-start.21
  124.3 1.3 collective-permute-start.27
  125.6 0.9 collective-permute-start.26
  126.5 7.4 %collective-permute-done.21 = f32[64,1792]{1,0:T(8,128)S(1)} collective-permute-done((f32[64,1792]{1,0:T(8,128)S(1)}, f32[64,1792]{1,0:T(8,128)S(1)}, u32[]{:S(2)}, u32[]{:S(2)}) %collective-permute-start.21) | collective-permute-done | bytes 458784 | tf_op jit(solution)/shard_map/ppermute | solution.py:200
  134.0 4.5 %collective-permute-start.25 = (f32[4,32,128]{2,1,0:T(8,128)S(1)}, f32[4,32,128]{2,1,0:T(8,128)S(1)}, u32[]{:S(2)}, u32[]{:S(2)}) collective-permute-start(f32[4,32,128]{2,1,0:T(8,128)S(1)} %add.448), channel_id=1, source_target_pairs={{0,8},{2,10},{4,12},{6,14},{8,0},{10,2},{12,4},{14,6},{1,9},{3,11}... | collective-permute-start | bytes 196616 | tf_op jit(solution)/shard_map/ppermute | solution.py:200
  138.5 1.6 finish.2.refs_0_
  140.0 1.1 fusion.1
  141.3 0.4 collective-permute-start.24
  141.7 7.0 %collective-permute-done.25 = f32[4,32,128]{2,1,0:T(8,128)S(1)} collective-permute-done((f32[4,32,128]{2,1,0:T(8,128)S(1)}, f32[4,32,128]{2,1,0:T(8,128)S(1)}, u32[]{:S(2)}, u32[]{:S(2)}) %collective-permute-start.25) | collective-permute-done | bytes 65568 | tf_op jit(solution)/shard_map/ppermute | solution.py:200
  149.0 2.1 %collective-permute-start.30 = (f32[128,512]{1,0:T(8,128)S(1)}, f32[128,512]{1,0:T(8,128)S(1)}, u32[]{:S(2)}, u32[]{:S(2)}) collective-permute-start(f32[128,512]{1,0:T(8,128)S(1)} %maximum_add_fusion.4), channel_id=1, source_target_pairs={{0,2},{2,4},{4,6},{6,8},{8,10},{10,12},{12,14},{14,0},{1,3},{3,5},... | collective-permute-start | bytes 786440 | tf_op jit(solution)/shard_map/ppermute | solution.py:204
  151.1 1.9 %collective-permute-done.28.more_ref = f32[4,32,128]{2,1,0:T(8,128)S(1)} collective-permute-done((f32[4,32,128]{2,1,0:T(8,128)S(1)}, f32[4,32,128]{2,1,0:T(8,128)S(1)}, u32[]{:S(2)}, u32[]{:S(2)}) %collective-permute-start.28) | collective-permute-done | bytes 65568 | tf_op jit(solution)/shard_map/ppermute | solution.py:200
  153.0 1.8 %average.1 = (f32[8,128]{1,0:T(8,128)S(1)}, f32[64,4096]{1,0:T(8,128)S(1)}) custom-call(s32[2]{0:T(128)S(1)} %pad_add_fusion.where_ref, f32[4,32,128]{2,1,0:T(8,128)S(1)} %add.452.coeffs_ref, f32[4,32,128]{2,1,0:T(8,128)S(1)} %collective-permute-done.28.more_ref, f32[32,32]{1,0:T(8,128)S(1)} %convolution_multiply_fusion.gram_ref, ...), custom_call_target="tpu_custom_call" | custom-call | tf_op jit(solution)/shard_map/average/pallas_call | solution.py:189
  155.0 1.6 finish.3.front_ref
  156.5 2.9 %collective-permute-done.29.more_ref = f32[8,128]{1,0:T(8,128)S(1)} collective-permute-done((f32[8,128]{1,0:T(8,128)S(1)}, f32[8,128]{1,0:T(8,128)S(1)}, u32[]{:S(2)}, u32[]{:S(2)}) %collective-permute-start.29) | collective-permute-done | bytes 4128 | tf_op jit(solution)/shard_map/ppermute | solution.py:200
  159.4 1.8 %last.1 = (f32[64,4096]{1,0:T(8,128)}, f32[64,4096]{1,0:T(8,128)}) custom-call(f32[64,4096]{1,0:T(8,128)} %finish.3.front_ref, f32[8,128]{1,0:T(8,128)S(1)} %get-tuple-element.99.squares_ref, f32[8,128]{1,0:T(8,128)S(1)} %collective-permute-done.29.more_ref, f32[64,4096]{1,0:T(8,128)S(1)} %get-tuple-element.101.average_ref, ...), custom_call_target="tpu_custom_call", output_to_operand_aliasing={{0}: (0, {})} | custom-call | tf_op jit(solution)/shard_map/last/pallas_call | solution.py:155
  (86 shorter events, 3.1 us)
Async XLA Ops:
  0.6 18.9 %copy-start.6 = (s32[32]{0:T(128)S(1)}, s32[32]{0:T(128)}, u32[]{:S(2)}) copy-start(s32[32]{0:T(128)} %param.8) | copy-start | bytes 388
  2.0 30.2 %copy-start.1 = (f32[1,64,4096]{2,1,0:T(8,128)S(1)}, f32[1,64,4096]{2,1,0:T(8,128)}, u32[]{:S(2)}) copy-start(f32[1,64,4096]{2,1,0:T(8,128)} %param.7) | copy-start | bytes 3145732
  2.0 17.6 %collective-permute-start.3 = (f32[128,768]{1,0:T(8,128)S(1)}, f32[128,768]{1,0:T(8,128)S(1)}, u32[]{:S(2)}, u32[]{:S(2)}) collective-permute-start(f32[128,768]{1,0:T(8,128)S(1)} %get-tuple-element.142), channel_id=1, source_target_pairs={{0,2},{2,4},{4,6},{6,8},{8,10},{10,12},{12,14},{14,0},{1,3},{3,5},... | collective-permute-start | bytes 1179656 | tf_op jit(solution)/shard_map/ppermute | solution.py:204
  2.3 17.3 %collective-permute-start.4 = (f32[128,768]{1,0:T(8,128)S(1)}, f32[128,768]{1,0:T(8,128)S(1)}, u32[]{:S(2)}, u32[]{:S(2)}) collective-permute-start(f32[128,768]{1,0:T(8,128)S(1)} %get-tuple-element.141), channel_id=1, source_target_pairs={{0,14},{2,0},{4,2},{6,4},{8,6},{10,8},{12,10},{14,12},{1,15},{3,1}... | collective-permute-start | bytes 1179656 | tf_op jit(solution)/shard_map/ppermute | solution.py:208
  7.3 18.9 %collective-permute-start.1 = (f32[128,768]{1,0:T(8,128)}, f32[128,768]{1,0:T(8,128)}, u32[]{:S(2)}, u32[]{:S(2)}) collective-permute-start(f32[128,768]{1,0:T(8,128)} %get-tuple-element.140), channel_id=1, source_target_pairs={{0,2},{2,4},{4,6},{6,8},{8,10},{10,12},{12,14},{14,0},{1,3},{3,5},... | collective-permute-start | bytes 1179656 | tf_op jit(solution)/shard_map/ppermute | solution.py:204
  7.3 18.9 %collective-permute-start.2 = (f32[128,768]{1,0:T(8,128)}, f32[128,768]{1,0:T(8,128)}, u32[]{:S(2)}, u32[]{:S(2)}) collective-permute-start(f32[128,768]{1,0:T(8,128)} %get-tuple-element.139), channel_id=1, source_target_pairs={{0,14},{2,0},{4,2},{6,4},{8,6},{10,8},{12,10},{14,12},{1,15},{3,1}... | collective-permute-start | bytes 1179656 | tf_op jit(solution)/shard_map/ppermute | solution.py:208
  16.4 31.5 %collective-permute-start = (f32[320,1024]{1,0:T(8,128)}, f32[320,1024]{1,0:T(8,128)}, u32[]{:S(2)}, u32[]{:S(2)}) collective-permute-start(f32[320,1024]{1,0:T(8,128)} %concatenate.70), channel_id=1, source_target_pairs={{0,1},{1,0},{2,3},{3,2},{4,5},{5,4},{6,7},{7,6},{8,9},{9,8},{10,11... | collective-permute-start | bytes 3932168 | tf_op jit(solution)/shard_map/ppermute | solution.py:200
  22.1 24.3 %collective-permute-start.5 = (f32[128,1536]{1,0:T(8,128)}, f32[128,1536]{1,0:T(8,128)S(1)}, u32[]{:S(2)}, u32[]{:S(2)}) collective-permute-start(f32[128,1536]{1,0:T(8,128)} %get-tuple-element.132), channel_id=1, source_target_pairs={{0,2},{2,4},{4,6},{6,8},{8,10},{10,12},{12,14},{14,0},{1,3},{3,5},... | collective-permute-start | bytes 2359304 | tf_op jit(solution)/shard_map/ppermute | solution.py:204
  22.1 24.3 %collective-permute-start.6 = (f32[128,1536]{1,0:T(8,128)}, f32[128,1536]{1,0:T(8,128)}, u32[]{:S(2)}, u32[]{:S(2)}) collective-permute-start(f32[128,1536]{1,0:T(8,128)} %get-tuple-element.131), channel_id=1, source_target_pairs={{0,14},{2,0},{4,2},{6,4},{8,6},{10,8},{12,10},{14,12},{1,15},{3,1}... | collective-permute-start | bytes 2359304 | tf_op jit(solution)/shard_map/ppermute | solution.py:208
  28.9 31.1 %collective-permute-start.7 = (f32[128,1536]{1,0:T(8,128)}, f32[128,1536]{1,0:T(8,128)}, u32[]{:S(2)}, u32[]{:S(2)}) collective-permute-start(f32[128,1536]{1,0:T(8,128)} %get-tuple-element.130), channel_id=1, source_target_pairs={{0,2},{2,4},{4,6},{6,8},{8,10},{10,12},{12,14},{14,0},{1,3},{3,5},... | collective-permute-start | bytes 2359304 | tf_op jit(solution)/shard_map/ppermute | solution.py:204
  28.9 31.1 %collective-permute-start.8 = (f32[128,1536]{1,0:T(8,128)}, f32[128,1536]{1,0:T(8,128)}, u32[]{:S(2)}, u32[]{:S(2)}) collective-permute-start(f32[128,1536]{1,0:T(8,128)} %get-tuple-element.129), channel_id=1, source_target_pairs={{0,14},{2,0},{4,2},{6,4},{8,6},{10,8},{12,10},{14,12},{1,15},{3,1}... | collective-permute-start | bytes 2359304 | tf_op jit(solution)/shard_map/ppermute | solution.py:208
  32.2 3.4 %copy-start = (bf16[1,1,1024,4096]{3,2,1,0:T(8,128)(2,1)S(1)}, bf16[1,1,1024,4096]{3,2,1,0:T(8,128)(2,1)}, u32[]{:S(2)}) copy-start(bf16[1,1,1024,4096]{3,2,1,0:T(8,128)(2,1)} %param.6) | copy-start | bytes 25165828
  35.5 1.6 copy-start.2
  46.4 0.9 copy-start.5
  53.9 19.3 %collective-permute-start.9 = (f32[192,1024]{1,0:T(8,128)}, f32[192,1024]{1,0:T(8,128)}, u32[]{:S(2)}, u32[]{:S(2)}) collective-permute-start(f32[192,1024]{1,0:T(8,128)} %maximum_convert_fusion), channel_id=1, source_target_pairs={{0,1},{1,0},{2,3},{3,2},{4,5},{5,4},{6,7},{7,6},{8,9},{9,8},{10,11... | collective-permute-start | bytes 2359304 | tf_op jit(solution)/shard_map/ppermute | solution.py:200
  57.8 23.8 %collective-permute-start.13 = (f32[128,1792]{1,0:T(8,128)}, f32[128,1792]{1,0:T(8,128)S(1)}, u32[]{:S(2)}, u32[]{:S(2)}) collective-permute-start(f32[128,1792]{1,0:T(8,128)} %fusion), channel_id=1, source_target_pairs={{0,14},{2,0},{4,2},{6,4},{8,6},{10,8},{12,10},{14,12},{1,15},{3,1}... | collective-permute-start | bytes 2752520 | tf_op jit(solution)/shard_map/ppermute | solution.py:208
  58.5 24.7 %collective-permute-start.12 = (f32[128,1792]{1,0:T(8,128)}, f32[128,1792]{1,0:T(8,128)S(1)}, u32[]{:S(2)}, u32[]{:S(2)}) collective-permute-start(f32[128,1792]{1,0:T(8,128)} %pad_maximum_fusion.2), channel_id=1, source_target_pairs={{0,2},{2,4},{4,6},{6,8},{8,10},{10,12},{12,14},{14,0},{1,3},{3,5},... | collective-permute-start | bytes 2752520 | tf_op jit(solution)/shard_map/ppermute | solution.py:204
  61.9 38.2 %collective-permute-start.15 = (f32[128,1536]{1,0:T(8,128)S(1)}, f32[128,1536]{1,0:T(8,128)S(1)}, u32[]{:S(2)}, u32[]{:S(2)}) collective-permute-start(f32[128,1536]{1,0:T(8,128)S(1)} %get-tuple-element.123), channel_id=1, source_target_pairs={{0,2},{2,4},{4,6},{6,8},{8,10},{10,12},{12,14},{14,0},{1,3},{3,5},... | collective-permute-start | bytes 2359304 | tf_op jit(solution)/shard_map/ppermute | solution.py:204
  62.0 38.1 %collective-permute-start.16 = (f32[128,1536]{1,0:T(8,128)S(1)}, f32[128,1536]{1,0:T(8,128)S(1)}, u32[]{:S(2)}, u32[]{:S(2)}) collective-permute-start(f32[128,1536]{1,0:T(8,128)S(1)} %get-tuple-element.122), channel_id=1, source_target_pairs={{0,14},{2,0},{4,2},{6,4},{8,6},{10,8},{12,10},{14,12},{1,15},{3,1}... | collective-permute-start | bytes 2359304 | tf_op jit(solution)/shard_map/ppermute | solution.py:208
  73.3 1.3 collective-permute-start.10
  74.6 5.6 %collective-permute-start.11 = (f32[8,32,128]{2,1,0:T(8,128)S(1)}, f32[8,32,128]{2,1,0:T(8,128)S(1)}, u32[]{:S(2)}, u32[]{:S(2)}) collective-permute-start(f32[8,32,128]{2,1,0:T(8,128)S(1)} %add.422), channel_id=1, source_target_pairs={{0,64},{64,0},{128,192},{192,128},{1,65},{65,1},{129,193},{193,129... | collective-permute-start | bytes 393224 | tf_op jit(solution)/shard_map/ppermute | solution.py:200
  83.2 16.8 %collective-permute-start.14 = (f32[4,32,128]{2,1,0:T(8,128)S(1)}, f32[4,32,128]{2,1,0:T(8,128)S(1)}, u32[]{:S(2)}, u32[]{:S(2)}) collective-permute-start(f32[4,32,128]{2,1,0:T(8,128)S(1)} %bitcast.108), channel_id=1, source_target_pairs={{0,4},{2,6},{4,0},{6,2},{8,12},{10,14},{12,8},{14,10},{1,5},{3,7},... | collective-permute-start | bytes 196616 | tf_op jit(solution)/shard_map/ppermute | solution.py:200
  84.8 37.5 %collective-permute-start.20 = (f32[128,2048]{1,0:T(8,128)S(1)}, f32[128,2048]{1,0:T(8,128)S(1)}, u32[]{:S(2)}, u32[]{:S(2)}) collective-permute-start(f32[128,2048]{1,0:T(8,128)S(1)} %pad_maximum_fusion.1), channel_id=1, source_target_pairs={{0,14},{2,0},{4,2},{6,4},{8,6},{10,8},{12,10},{14,12},{1,15},{3,1}... | collective-permute-start | bytes 3145736 | tf_op jit(solution)/shard_map/ppermute | solution.py:208
  88.6 49.8 %copy-start.4 = (bf16[128,128]{1,0:T(8,128)(2,1)S(1)}, bf16[128,128]{1,0:T(8,128)(2,1)}, u32[]{:S(2)}) copy-start(bf16[128,128]{1,0:T(8,128)(2,1)} %constant.169.clone.refs_4_.refs_5_) | copy-start | bytes 98308
  88.7 33.9 %collective-permute-start.19 = (f32[128,2048]{1,0:T(8,128)S(1)}, f32[128,2048]{1,0:T(8,128)S(1)}, u32[]{:S(2)}, u32[]{:S(2)}) collective-permute-start(f32[128,2048]{1,0:T(8,128)S(1)} %pad_maximum_fusion), channel_id=1, source_target_pairs={{0,2},{2,4},{4,6},{6,8},{8,10},{10,12},{12,14},{14,0},{1,3},{3,5},... | collective-permute-start | bytes 3145736 | tf_op jit(solution)/shard_map/ppermute | solution.py:204
  101.4 5.9 %collective-permute-start.17 = (f32[4,32,128]{2,1,0:T(8,128)S(1)}, f32[4,32,128]{2,1,0:T(8,128)S(1)}, u32[]{:S(2)}, u32[]{:S(2)}) collective-permute-start(f32[4,32,128]{2,1,0:T(8,128)S(1)} %add.441), channel_id=1, source_target_pairs={{0,128},{64,192},{128,0},{192,64},{1,129},{65,193},{129,1},{193,65... | collective-permute-start | bytes 196616 | tf_op jit(solution)/shard_map/ppermute | solution.py:200
  107.3 5.4 %collective-permute-start.18 = (f32[4,32,128]{2,1,0:T(8,128)S(1)}, f32[4,32,128]{2,1,0:T(8,128)S(1)}, u32[]{:S(2)}, u32[]{:S(2)}) collective-permute-start(f32[4,32,128]{2,1,0:T(8,128)S(1)} %add.442), channel_id=1, source_target_pairs={{0,32},{32,0},{1,33},{33,1},{2,34},{34,2},{3,35},{35,3},{4,36},{36... | collective-permute-start | bytes 196616 | tf_op jit(solution)/shard_map/ppermute | solution.py:200
  108.1 31.9 %collective-permute-start.22 = (f32[128,1536]{1,0:T(8,128)S(1)}, f32[128,1536]{1,0:T(8,128)S(1)}, u32[]{:S(2)}, u32[]{:S(2)}) collective-permute-start(f32[128,1536]{1,0:T(8,128)S(1)} %get-tuple-element.119), channel_id=1, source_target_pairs={{0,2},{2,4},{4,6},{6,8},{8,10},{10,12},{12,14},{14,0},{1,3},{3,5},... | collective-permute-start | bytes 2359304 | tf_op jit(solution)/shard_map/ppermute | solution.py:204
  108.5 31.5 %collective-permute-start.23 = (f32[128,1536]{1,0:T(8,128)S(1)}, f32[128,1536]{1,0:T(8,128)S(1)}, u32[]{:S(2)}, u32[]{:S(2)}) collective-permute-start(f32[128,1536]{1,0:T(8,128)S(1)} %get-tuple-element.118), channel_id=1, source_target_pairs={{0,14},{2,0},{4,2},{6,4},{8,6},{10,8},{12,10},{14,12},{1,15},{3,1}... | collective-permute-start | bytes 2359304 | tf_op jit(solution)/shard_map/ppermute | solution.py:208
  122.5 30.5 %copy-start.3 = (bf16[64,4096]{1,0:T(8,128)(2,1)S(1)}, bf16[64,4096]{1,0:T(8,128)(2,1)}, u32[]{:S(2)}) copy-start(bf16[64,4096]{1,0:T(8,128)(2,1)} %constant.167.clone.spread_ref) | copy-start | bytes 1572868
  123.9 10.1 %collective-permute-start.21 = (f32[64,1792]{1,0:T(8,128)S(1)}, f32[64,1792]{1,0:T(8,128)S(1)}, u32[]{:S(2)}, u32[]{:S(2)}) collective-permute-start(f32[64,1792]{1,0:T(8,128)S(1)} %pad_maximum_fusion.3), channel_id=1, source_target_pairs={{0,1},{1,0},{2,3},{3,2},{4,5},{5,4},{6,7},{7,6},{8,9},{9,8},{10,11... | collective-permute-start | bytes 1376264 | tf_op jit(solution)/shard_map/ppermute | solution.py:200
  124.3 24.5 %collective-permute-start.27 = (f32[128,512]{1,0:T(8,128)S(1)}, f32[128,512]{1,0:T(8,128)S(1)}, u32[]{:S(2)}, u32[]{:S(2)}) collective-permute-start(f32[128,512]{1,0:T(8,128)S(1)} %maximum_add_fusion.3), channel_id=1, source_target_pairs={{0,14},{2,0},{4,2},{6,4},{8,6},{10,8},{12,10},{14,12},{1,15},{3,1}... | collective-permute-start | bytes 786440 | tf_op jit(solution)/shard_map/ppermute | solution.py:208
  125.6 23.2 %collective-permute-start.26 = (f32[128,512]{1,0:T(8,128)S(1)}, f32[128,512]{1,0:T(8,128)S(1)}, u32[]{:S(2)}, u32[]{:S(2)}) collective-permute-start(f32[128,512]{1,0:T(8,128)S(1)} %maximum_add_fusion.2), channel_id=1, source_target_pairs={{0,2},{2,4},{4,6},{6,8},{8,10},{10,12},{12,14},{14,0},{1,3},{3,5},... | collective-permute-start | bytes 786440 | tf_op jit(solution)/shard_map/ppermute | solution.py:204
  134.0 14.7 %collective-permute-start.25 = (f32[4,32,128]{2,1,0:T(8,128)S(1)}, f32[4,32,128]{2,1,0:T(8,128)S(1)}, u32[]{:S(2)}, u32[]{:S(2)}) collective-permute-start(f32[4,32,128]{2,1,0:T(8,128)S(1)} %add.448), channel_id=1, source_target_pairs={{0,8},{2,10},{4,12},{6,14},{8,0},{10,2},{12,4},{14,6},{1,9},{3,11}... | collective-permute-start | bytes 196616 | tf_op jit(solution)/shard_map/ppermute | solution.py:200
  141.3 13.7 %collective-permute-start.24 = (f32[64,1536]{1,0:T(8,128)S(1)}, f32[64,1536]{1,0:T(8,128)S(1)}, u32[]{:S(2)}, u32[]{:S(2)}) collective-permute-start(f32[64,1536]{1,0:T(8,128)S(1)} %get-tuple-element.135), channel_id=1, source_target_pairs={{0,1},{1,0},{2,3},{3,2},{4,5},{5,4},{6,7},{7,6},{8,9},{9,8},{10,11... | collective-permute-start | bytes 1179656 | tf_op jit(solution)/shard_map/ppermute | solution.py:200
  148.7 4.4 %collective-permute-start.28 = (f32[4,32,128]{2,1,0:T(8,128)S(1)}, f32[4,32,128]{2,1,0:T(8,128)S(1)}, u32[]{:S(2)}, u32[]{:S(2)}) collective-permute-start(f32[4,32,128]{2,1,0:T(8,128)S(1)} %add.452.coeffs_ref), channel_id=1, source_target_pairs={{0,2},{2,0},{4,6},{6,4},{8,10},{10,8},{12,14},{14,12},{1,3},{3,1},... | collective-permute-start | bytes 196616 | tf_op jit(solution)/shard_map/ppermute | solution.py:200
  148.9 10.6 %collective-permute-start.31 = (f32[128,512]{1,0:T(8,128)S(1)}, f32[128,512]{1,0:T(8,128)S(1)}, u32[]{:S(2)}, u32[]{:S(2)}) collective-permute-start(f32[128,512]{1,0:T(8,128)S(1)} %maximum_add_fusion.5), channel_id=1, source_target_pairs={{0,14},{2,0},{4,2},{6,4},{8,6},{10,8},{12,10},{14,12},{1,15},{3,1}... | collective-permute-start | bytes 786440 | tf_op jit(solution)/shard_map/ppermute | solution.py:208
  149.0 10.4 %collective-permute-start.30 = (f32[128,512]{1,0:T(8,128)S(1)}, f32[128,512]{1,0:T(8,128)S(1)}, u32[]{:S(2)}, u32[]{:S(2)}) collective-permute-start(f32[128,512]{1,0:T(8,128)S(1)} %maximum_add_fusion.4), channel_id=1, source_target_pairs={{0,2},{2,4},{4,6},{6,8},{8,10},{10,12},{12,14},{14,0},{1,3},{3,5},... | collective-permute-start | bytes 786440 | tf_op jit(solution)/shard_map/ppermute | solution.py:204
  154.8 4.6 %collective-permute-start.29 = (f32[8,128]{1,0:T(8,128)S(1)}, f32[8,128]{1,0:T(8,128)S(1)}, u32[]{:S(2)}, u32[]{:S(2)}) collective-permute-start(f32[8,128]{1,0:T(8,128)S(1)} %get-tuple-element.99.squares_ref), channel_id=1, source_target_pairs={{0,4},{2,6},{4,0},{6,2},{8,12},{10,14},{12,8},{14,10},{1,5},{3,7},... | collective-permute-start | bytes 12296 | tf_op jit(solution)/shard_map/ppermute | solution.py:200
